TPU v7x, 32 devices: a whole 2x2x4 slice. The times are simulated.
32 devices in a mesh: cells: 8 (over z, y), samp: 4 (over x, core).
Axes of the slice: x: 2, y: 2, z: 4, core: 2. Of those that a mesh axis runs over, the one named last changes fastest.
Arguments:
- snapshots: bfloat16 [16384, 4096], P('cells', 'samp'), may hold values from -6 to 6
- left_slow: bfloat16 [120, 256], P(None, 'cells'), may hold values from -0.375 to 0.375
- left_fast: bfloat16 [120, 64], replicated, may hold values from -0.75 to 0.75
- right_slow: bfloat16 [150, 128], P(None, 'samp'), may hold values from -0.5 to 0.5
- right_fast: bfloat16 [150, 32], replicated, may hold values from -1 to 1
Outputs:
- range_sketch: float32 [16384, 150], P(('cells', 'samp'))
- core: float32 [150, 4096], P(None, ('samp', 'cells'))
All inputs are finite; a program needn't handle non-finite values.
Results may differ from a plain program's by a relative error of at most 0.012.
The roundings to bfloat16 on the way count: a program that leaves them out, or rounds other values in their place, can miss the bound.
Values sent between devices are 32-bit elements; how exact they have to be, the bound alone decides.
No kernel may reach another device: no remote copies, remote signals or barrier semaphores. Data moves between devices by JAX's collectives and lax.ppermute only.
A program may use at most 64 MiB of HBM per device.

v0:
```python
import jax
import jax.numpy as jnp
from jax import lax
from jax.sharding import PartitionSpec as P


def expand(slow, fast):
    rows = slow.shape[0]
    return (
        (slow.astype(jnp.float32)[:, :, None] * fast.astype(jnp.float32)[:, None, :])
        .reshape(rows, -1)
        .astype(jnp.bfloat16)
    )


def on_device(snapshots, left_slow, left_fast, right_slow, right_fast):
    psi = expand(left_slow, left_fast)
    omega = expand(right_slow, right_fast)
    left_term = jnp.dot(psi, snapshots, preferred_element_type=jnp.float32)
    range_term = lax.dot_general(
        snapshots, omega, (((1,), (1,)), ((), ())), preferred_element_type=jnp.float32
    )
    range_part = lax.psum_scatter(range_term, "samp", scatter_dimension=0, tiled=True)
    left_part = lax.psum_scatter(left_term, "cells", scatter_dimension=1, tiled=True)
    height = range_part.shape[0]
    psi_rows = lax.dynamic_slice_in_dim(psi, lax.axis_index("samp") * height, height, 1).astype(
        jnp.float32
    )
    partial_value = jnp.dot(psi_rows, range_part, precision=lax.Precision.HIGHEST)
    core_input = lax.psum(partial_value, ("cells", "samp"))
    rank_left = core_input.shape[0]
    gram = jnp.dot(core_input, core_input.T, precision=lax.Precision.HIGHEST) + 0.5 * jnp.eye(
        rank_left, dtype=jnp.float32
    )
    factor = jnp.linalg.cholesky(gram)
    solved = jax.scipy.linalg.cho_solve((factor, True), left_part)
    core = jnp.dot(core_input.T, solved, precision=lax.Precision.HIGHEST)
    return (range_part, core)


def solution(mesh):
    placed = (P("cells", "samp"), P(None, "cells"), P(), P(None, "samp"), P())
    return jax.shard_map(
        on_device,
        mesh=mesh,
        in_specs=placed,
        out_specs=(P(("cells", "samp"), None), P(None, ("samp", "cells"))),
        check_vma=False,
    )
```

profile of v0, /device:TPU:0, one launch (start us, length us, event | category | flops | bytes accessed | tf_op | source)
XLA Modules:
  0.0 203.3 jit_solution(1140995992063141425)
XLA Ops:
  8.0 0.0 copy-start
  8.0 0.0 copy-start.1
  8.0 0.0 reduce-scatter.3.cloned.1.call-start
  8.1 0.7 convert_element_type.27
  8.8 0.7 convert_element_type.26
  9.5 0.1 multiply_convert_fusion.1
  9.6 4.8 %convolution_bitcast_fusion = f32[2048,150]{0,1:T(8,128)} fusion(bf16[150,1024]{0,1:T(8,128)(2,1)S(1)} %bitcast.30, bf16[2048,1024]{1,0:T(8,128)(2,1)} %param.5), kind=kOutput, calls=%fused_computation | convolution fusion | flops 629145600 | bytes 5730304 | tf_op jit(solution)/shard_map/dot_general | solution.py:20
  14.4 0.0 reduce-scatter.3.cloned.1.call-update
  14.5 0.0 all-reduce.2.cloned.1.call-start
  14.5 0.0 copy-done
  14.5 0.0 copy-done.1
  14.6 0.1 multiply_convert_fusion
  14.7 28.7 %reduce-scatter.3.cloned.1.call-done = f32[512,150]{0,1:T(8,128)} async-done(((f32[2048,150]{0,1:T(8,128)}), f32[512,150]{0,1:T(8,128)}) %reduce-scatter.3.cloned.1.call-update) | async-done | bytes 307216 | tf_op jit(solution)/shard_map/reduce_scatter | solution.py:23
  43.4 1.9 fusion
  45.3 0.0 all-reduce.2.cloned.1.call-update
  45.3 0.0 reduce-scatter.5.cloned.1.call-start
  45.4 3.7 %fusion.11 = f32[120,1024]{1,0:T(8,128)} fusion(bf16[120,2048]{0,1:T(8,128)(2,1)S(1)} %bitcast.29, bf16[2048,1024]{1,0:T(8,128)(2,1)} %param.5), kind=kOutput, calls=%fused_computation.21 | convolution fusion | flops 503316480 | bytes 5177344 | tf_op jit(solution)/shard_map/dot_general | solution.py:19
  49.1 0.0 reduce-scatter.5.cloned.1.call-update
  49.1 120.5 %all-reduce.2.cloned.1.call-done = f32[120,150]{0,1:T(8,128)} async-done(((f32[120,150]{0,1:T(8,128)}), f32[120,150]{0,1:T(8,128)}) %all-reduce.2.cloned.1.call-update) | async-done | bytes 72016 | tf_op jit(solution)/shard_map/psum | solution.py:30
  169.6 1.4 fusion.10
  171.0 0.1 copy.12
  171.1 11.0 %cholesky.16 = f32[120,120]{1,0:T(8,128)S(1)} custom-call(f32[120,120]{1,0:T(8,128)S(1)} %fusion.8), custom_call_target="Cholesky" | custom-call | tf_op jit(solution)/shard_map/jit(cholesky)/cholesky | solution.py:35
  182.1 0.6 compare_reduce_fusion
  182.8 0.7 fusion.2
  183.4 9.2 %custom-call.10 = f32[1,120,120]{1,2,0:T(8,128)S(1)} custom-call(f32[1,120,120]{2,1,0:T(8,128)S(1)} %fusion.2), custom_call_target="InvertDiagBlocksLowerTriangular" | custom-call | tf_op jit(solution)/shard_map/jit(_cho_solve)/triangular_solve | solution.py:36
  192.6 0.0 reduce-scatter.5.cloned.1.call-done
  192.7 1.1 fusion.5
  193.8 0.3 fusion.3
  194.1 1.8 fusion.12
  (4 shorter events, 0.1 us)
Async XLA Ops:
  8.0 6.5 %copy-start = (bf16[120,64]{0,1:T(8,128)(2,1)S(1)}, bf16[120,64]{0,1:T(8,128)(2,1)}, u32[]{:S(2)}) copy-start(bf16[120,64]{0,1:T(8,128)(2,1)} %param.7) | copy-start | bytes 46084
  8.0 6.5 %copy-start.1 = (bf16[120,32]{0,1:T(8,128)(2,1)S(1)}, bf16[120,32]{0,1:T(8,128)(2,1)}, u32[]{:S(2)}) copy-start(bf16[120,32]{0,1:T(8,128)(2,1)} %param.6) | copy-start | bytes 23044
  8.0 35.4 %reduce-scatter.3.cloned.1.call-start = ((), (), s32[]{:S(2)}) async-start(), calls=%async_computation.2 | async-start | bytes 1556480 | tf_op jit(solution)/shard_map/reduce_scatter | solution.py:23
  14.5 155.1 %all-reduce.2.cloned.1.call-start = ((), (), s32[]{:S(2)}) async-start(), calls=%async_computation.3 | async-start | bytes 155648 | tf_op jit(solution)/shard_map/psum | solution.py:30
  45.3 147.4 %reduce-scatter.5.cloned.1.call-start = ((), (), s32[]{:S(2)}) async-start(), calls=%async_computation.4 | async-start | bytes 552960 | tf_op jit(solution)/shard_map/reduce_scatter | solution.py:24
Sparse Core Ops, SparseCore 0:
  14.6 28.7 reduce-scatter.2
  50.5 119.0 all-reduce.1
Sparse Core Ops, SparseCore 1:
  49.4 59.2 reduce-scatter.4
where the time goes:
time: 205 us; the launch traced here: 203 us
  waiting for transfers between devices  149 us (73%)
  other arithmetic  23.2 us (11%)
  between operations  15.6 us (8%)
  matrix products  14.9 us (7%)
    psum x1, waiting for transfers between devices, on_device(): core_input = lax.psum(partial_value, ('cells', 'samp'))  121 us
    reduce_scatter x1, waiting for transfers between devices, on_device(): lax.psum_scatter(range_term, 'samp', scatter_dimension=0, tiled=True)  28.7 us
    another operation x3, other arithmetic, on_device(): factor = jnp.linalg.cholesky(gram)  11.6 us
    another operation x2, other arithmetic, on_device(): solved = jax.scipy.linalg.cho_solve((factor, True), left_part)  9.85 us
    dot_general x1, matrix products, on_device(): lax.dot_general(snapshots, omega, (((1,), (1,)), ((), ())), preferred_ele...  4.8 us
  transfers between devices with their start and end apart: 3, of which 2 were waited for; matrix products, arithmetic and copies ran while one was open for 13% of the time, Pallas kernels for 0%

commit v1 on v0

v1 whole, which is shorter than its diff:
```python
import jax
import jax.numpy as jnp
from jax import lax
from jax.sharding import PartitionSpec as P

F32 = jnp.float32
HIGHEST = lax.Precision.HIGHEST


def expand(slow, fast):
    rows = slow.shape[0]
    return (
        (slow.astype(F32)[:, :, None] * fast.astype(F32)[:, None, :])
        .reshape(rows, -1)
        .astype(jnp.bfloat16)
    )


def swap(value, axis, size, bit):
    return lax.ppermute(value, axis, [(i, i ^ bit) for i in range(size)])


def bits(size):
    return [1 << b for b in range(size.bit_length() - 1)]


def halve(blocks, axis, size, order):
    count = size.bit_length() - 1
    tail = blocks.shape[1:]
    held = blocks.reshape((2,) * count + tail)
    me = lax.axis_index(axis)
    left = list(bits(size))[::-1]
    for bit in order:
        dim = left.index(bit)
        left.pop(dim)
        mine = (me // bit) % 2
        kept = lax.dynamic_index_in_dim(held, mine, dim, False)
        sent = lax.dynamic_index_in_dim(held, 1 - mine, dim, False)
        held = kept + swap(sent, axis, size, bit)
    return held


def build(sizes):
    cells, samp = sizes["cells"], sizes["samp"]

    def on_device(snapshots, left_slow, left_fast, right_slow, right_fast):
        psi = expand(left_slow, left_fast)
        omega = expand(right_slow, right_fast)
        rank_left, rank_right = psi.shape[0], omega.shape[0]
        left_term = jnp.dot(psi, snapshots, preferred_element_type=F32)
        core_input = lax.dot_general(
            omega.astype(F32), left_term, (((1,), (1,)), ((), ())), precision=HIGHEST
        )
        for axis, size in (("samp", samp), ("cells", cells)):
            for bit in bits(size):
                core_input = core_input + swap(core_input, axis, size, bit)
        range_term = lax.dot_general(
            omega, snapshots, (((1,), (1,)), ((), ())), preferred_element_type=F32
        )
        range_blocks = range_term.reshape(rank_right, samp, -1).transpose(1, 0, 2)
        range_part = halve(range_blocks, "samp", samp, bits(samp)).T
        left_blocks = left_term.reshape(rank_left, cells, -1).transpose(1, 0, 2)
        left_part = halve(left_blocks, "cells", cells, bits(cells))
        gram = lax.dot_general(
            core_input, core_input, (((0,), (0,)), ((), ())), precision=HIGHEST
        ) + 0.5 * jnp.eye(rank_left, dtype=F32)
        factor = jnp.linalg.cholesky(gram)
        solved = jax.scipy.linalg.cho_solve((factor, True), left_part)
        core = jnp.dot(core_input, solved, precision=HIGHEST)
        return (range_part, core)

    return on_device


def solution(mesh):
    placed = (P("cells", "samp"), P(None, "cells"), P(), P(None, "samp"), P())
    return jax.shard_map(
        build(mesh.shape),
        mesh=mesh,
        in_specs=placed,
        out_specs=(P(("cells", "samp"), None), P(None, ("samp", "cells"))),
        check_vma=False,
    )
```

time: 205 us -> 66.2 us (0.32)
  waiting for transfers between devices: 149 us -> 11.2 us
  starting transfers between devices: 0.12 us -> 16.1 us
  between operations: 15.6 us -> 0.98 us
  matrix products: 14.9 us -> 9.15 us
  other arithmetic: 23.2 us -> 26.3 us
    psum x1 -> x0, waiting for transfers between devices: 121 us -> none  [on_device(): core_input = lax.psum(partial_value, ('cells', 'samp'))]
    reduce_scatter x2 -> x0, waiting for transfers between devices: 28.7 us -> none  [the longest x1 28.7 us: on_device(): lax.psum_scatter(range_term, 'samp', scatter_dimension=0, tiled=True)]
    ppermute x0 -> x10, starting transfers between devices: none -> 16.1 us  [swap(): return lax.ppermute(value, axis, [(i, i ^ bit) for i in range(size)])]
    ppermute x0 -> x10, waiting for transfers between devices: none -> 11.2 us  [swap(): return lax.ppermute(value, axis, [(i, i ^ bit) for i in range(size)])]
    dot_general x5, matrix products: 13.6 us -> 8.6 us  [the longest x1 3.72 us: on_device(): lax.dot_general(omega, snapshots, (((1,), (1,)), ((), ())), preferred_ele...]
  transfers between devices with their start and end apart: 3 -> 10, of which waited for: 2 -> 6; matrix products, arithmetic and copies ran while one was open for 13% -> 44% of each run, Pallas kernels for 0% -> 0%
where the time goes in v1:
time: 66.2 us; the launch traced here: 65.7 us
  other arithmetic  26.3 us (40%)
  starting transfers between devices  16.1 us (24%)
  waiting for transfers between devices  11.2 us (17%)
  matrix products  9.15 us (14%)
  local copies, waits for them, and re-layouts  2.06 us (3%)
  between operations  0.98 us (1%)
    ppermute x10, starting transfers between devices, swap(): return lax.ppermute(value, axis, [(i, i ^ bit) for i in range(size)])  16.1 us
    another operation x3, other arithmetic, on_device(): factor = jnp.linalg.cholesky(gram)  11.6 us
    ppermute x10, waiting for transfers between devices, swap(): return lax.ppermute(value, axis, [(i, i ^ bit) for i in range(size)])  11.2 us
    another operation x2, other arithmetic, on_device(): solved = jax.scipy.linalg.cho_solve((factor, True), left_part)  9.85 us
    dot_general x1, matrix products, on_device(): lax.dot_general(omega, snapshots, (((1,), (1,)), ((), ())), preferred_ele...  3.72 us
    dot_general x1, matrix products, on_device(): left_term = jnp.dot(psi, snapshots, preferred_element_type=F32)  2.92 us
    convert_element_type x2, other arithmetic, expand(): fast.astype(F32)[:, None, :]  1.44 us
    convert_element_type x2, other arithmetic, expand(): slow.astype(F32)[:, :, None] * fast.astype(F32)[:, None, :]  1.42 us
  transfers between devices with their start and end apart: 10, of which 6 were waited for; matrix products, arithmetic and copies ran while one was open for 44% of the time, Pallas kernels for 0%

profile of v1, /device:TPU:0, one launch (start us, length us, event | category | flops | bytes accessed | tf_op | source)
XLA Modules:
  0.0 65.7 jit_solution(6539632936131705868)
XLA Ops:
  0.6 0.7 %convert_element_type.37 = f32[120,32]{0,1:T(8,128)S(1)} convert(bf16[120,32]{0,1:T(8,128)(2,1)} %param.6) | non-fusion elementwise | flops 3840 | bytes 23040 | tf_op jit(solution)/shard_map/convert_element_type | solution.py:13
  1.3 0.7 %convert_element_type.38 = f32[120,64]{0,1:T(8,128)S(1)} convert(bf16[120,64]{0,1:T(8,128)(2,1)} %param.7) | non-fusion elementwise | flops 7680 | bytes 46080 | tf_op jit(solution)/shard_map/convert_element_type | solution.py:13
  2.1 0.7 %convert_element_type.33 = f32[150,32]{0,1:T(8,128)S(1)} convert(bf16[150,32]{0,1:T(8,128)(2,1)} %param.8) | non-fusion elementwise | flops 4800 | bytes 28800 | tf_op jit(solution)/shard_map/convert_element_type | solution.py:13
  2.8 0.7 %convert_element_type.34 = f32[150,32]{0,1:T(8,128)S(1)} convert(bf16[150,32]{0,1:T(8,128)(2,1)} %param.9) | non-fusion elementwise | flops 4800 | bytes 28800 | tf_op jit(solution)/shard_map/convert_element_type | solution.py:13
  3.5 0.1 multiply_convert_fusion.1
  3.6 0.1 multiply_convert_fusion
  3.8 2.9 %fusion.10 = f32[120,1024]{1,0:T(8,128)S(1)} fusion(bf16[120,2048]{0,1:T(8,128)(2,1)S(1)} %bitcast.63, bf16[2048,1024]{1,0:T(8,128)(2,1)} %param.5), kind=kOutput, calls=%fused_computation.33 | convolution fusion | flops 503316480 | bytes 5177344 | tf_op jit(solution)/shard_map/dot_general | solution.py:50
  6.7 0.6 fusion.11
  7.3 0.5 collective-permute-start.2
  7.8 0.1 copy.22
  7.9 0.8 %collective-permute-done.2 = f32[150,120]{1,0:T(8,128)S(1)} collective-permute-done((f32[150,120]{1,0:T(8,128)S(1)}, f32[150,120]{1,0:T(8,128)S(1)}, u32[]{:S(2)}, u32[]{:S(2)}) %collective-permute-start.2) | collective-permute-done | bytes 72032 | tf_op jit(solution)/shard_map/ppermute | solution.py:20
  8.8 2.9 %collective-permute-start.3 = (f32[150,120]{1,0:T(8,128)S(1)}, f32[150,120]{1,0:T(8,128)S(1)}, u32[]{:S(2)}, u32[]{:S(2)}) collective-permute-start(f32[150,120]{1,0:T(8,128)S(1)} %add.120), channel_id=1, source_target_pairs={{0,2},{1,3},{2,0},{3,1},{4,6},{5,7},{6,4},{7,5},{8,10},{9,11},{10,... | collective-permute-start | bytes 216008 | tf_op jit(solution)/shard_map/ppermute | solution.py:20
  11.7 0.4 constant_dynamic-slice_fusion.4
  12.1 1.6 %collective-permute-start.7 = (f32[2,2,120,128]{3,1,0,2:T(2,128)S(1)}, f32[2,2,120,128]{3,1,0,2:T(2,128)S(1)}, u32[]{:S(2)}, u32[]{:S(2)}) collective-permute-start(f32[2,2,120,128]{3,1,0,2:T(2,128)S(1)} %bitcast.69), channel_id=1, source_target_pairs={{0,4},{4,0},{8,12},{12,8},{16,20},{20,16},{24,28},{28,24},{1,5},{5... | collective-permute-start | bytes 737288 | tf_op jit(solution)/shard_map/ppermute | solution.py:20
  13.7 0.7 %collective-permute-done.3 = f32[150,120]{1,0:T(8,128)S(1)} collective-permute-done((f32[150,120]{1,0:T(8,128)S(1)}, f32[150,120]{1,0:T(8,128)S(1)}, u32[]{:S(2)}, u32[]{:S(2)}) %collective-permute-start.3) | collective-permute-done | bytes 72032 | tf_op jit(solution)/shard_map/ppermute | solution.py:20
  14.4 1.8 %collective-permute-start.4 = (f32[150,120]{1,0:T(8,128)S(1)}, f32[150,120]{1,0:T(8,128)S(1)}, u32[]{:S(2)}, u32[]{:S(2)}) collective-permute-start(f32[150,120]{1,0:T(8,128)S(1)} %add.121), channel_id=1, source_target_pairs={{0,4},{4,0},{8,12},{12,8},{16,20},{20,16},{24,28},{28,24},{1,5},{5... | collective-permute-start | bytes 216008 | tf_op jit(solution)/shard_map/ppermute | solution.py:20
  16.2 3.7 %fusion.9 = f32[150,4,512]{2,0,1:T(8,128)S(1)} fusion(bf16[150,1024,1]{0,1,2:T(8,128)(2,1)S(1)} %bitcast.61, bf16[4,512,1024]{2,1,0:T(8,128)(2,1)} %bitcast.58), kind=kOutput, calls=%fused_computation.32 | convolution fusion | flops 629145600 | bytes 5730304 | tf_op jit(solution)/shard_map/dot_general | solution.py:57
  19.9 1.6 %collective-permute-done.4 = f32[150,120]{1,0:T(8,128)S(1)} collective-permute-done((f32[150,120]{1,0:T(8,128)S(1)}, f32[150,120]{1,0:T(8,128)S(1)}, u32[]{:S(2)}, u32[]{:S(2)}) %collective-permute-start.4) | collective-permute-done | bytes 72032 | tf_op jit(solution)/shard_map/ppermute | solution.py:20
  21.6 1.6 %collective-permute-start.5 = (f32[150,120]{1,0:T(8,128)S(1)}, f32[150,120]{1,0:T(8,128)S(1)}, u32[]{:S(2)}, u32[]{:S(2)}) collective-permute-start(f32[150,120]{1,0:T(8,128)S(1)} %add.122), channel_id=1, source_target_pairs={{0,8},{4,12},{8,0},{12,4},{16,24},{20,28},{24,16},{28,20},{1,9},{5... | collective-permute-start | bytes 216008 | tf_op jit(solution)/shard_map/ppermute | solution.py:20
  23.2 0.1 constant_dynamic-slice_fusion.9
  23.3 0.5 copy.27
  23.8 0.1 collective-permute-start
  24.0 0.0 collective-permute-done.7
  24.0 0.1 add.131
  24.2 1.9 %collective-permute-done.5 = f32[150,120]{1,0:T(8,128)S(1)} collective-permute-done((f32[150,120]{1,0:T(8,128)S(1)}, f32[150,120]{1,0:T(8,128)S(1)}, u32[]{:S(2)}, u32[]{:S(2)}) %collective-permute-start.5) | collective-permute-done | bytes 72032 | tf_op jit(solution)/shard_map/ppermute | solution.py:20
  26.1 2.7 %collective-permute-start.6 = (f32[150,120]{1,0:T(8,128)S(1)}, f32[150,120]{1,0:T(8,128)S(1)}, u32[]{:S(2)}, u32[]{:S(2)}) collective-permute-start(f32[150,120]{1,0:T(8,128)S(1)} %add.123), channel_id=1, source_target_pairs={{0,16},{4,20},{8,24},{12,28},{16,0},{20,4},{24,8},{28,12},{1,17},{... | collective-permute-start | bytes 216008 | tf_op jit(solution)/shard_map/ppermute | solution.py:20
  28.7 0.2 constant_dynamic-slice_fusion.2
  28.9 1.6 %collective-permute-start.8 = (f32[2,120,128]{2,0,1:T(2,128)S(1)}, f32[2,120,128]{2,0,1:T(2,128)S(1)}, u32[]{:S(2)}, u32[]{:S(2)}) collective-permute-start(f32[2,120,128]{2,0,1:T(2,128)S(1)} %bitcast.71), channel_id=1, source_target_pairs={{0,8},{4,12},{8,0},{12,4},{16,24},{20,28},{24,16},{28,20},{1,9},{5... | collective-permute-start | bytes 368648 | tf_op jit(solution)/shard_map/ppermute | solution.py:20
  30.6 1.0 %collective-permute-done.6 = f32[150,120]{1,0:T(8,128)S(1)} collective-permute-done((f32[150,120]{1,0:T(8,128)S(1)}, f32[150,120]{1,0:T(8,128)S(1)}, u32[]{:S(2)}, u32[]{:S(2)}) %collective-permute-start.6) | collective-permute-done | bytes 72032 | tf_op jit(solution)/shard_map/ppermute | solution.py:20
  31.5 0.4 fusion.12
  32.0 0.1 copy.17
  32.1 11.0 %cholesky.16 = f32[120,120]{1,0:T(8,128)S(1)} custom-call(f32[120,120]{1,0:T(8,128)S(1)} %fusion.7), custom_call_target="Cholesky" | custom-call | tf_op jit(solution)/shard_map/jit(cholesky)/cholesky | solution.py:67
  43.1 0.6 compare_reduce_fusion
  43.8 0.0 collective-permute-done.8
  43.8 0.1 add.135
  43.8 0.1 constant_dynamic-slice_fusion
  43.9 2.6 %collective-permute-start.9 = (f32[120,128]{1,0:T(8,128)S(1)}, f32[120,128]{1,0:T(8,128)S(1)}, u32[]{:S(2)}, u32[]{:S(2)}) collective-permute-start(f32[120,128]{1,0:T(8,128)S(1)} %bitcast.72), channel_id=1, source_target_pairs={{0,16},{4,20},{8,24},{12,28},{16,0},{20,4},{24,8},{28,12},{1,17},{... | collective-permute-start | bytes 184328 | tf_op jit(solution)/shard_map/ppermute | solution.py:20
  46.6 0.7 %fusion.1 = f32[1,120,120]{2,1,0:T(8,128)S(1)} fusion(f32[120,120]{1,0:T(8,128)S(1)} %cholesky.16, pred[]{:T(512)} %compare_reduce_fusion), kind=kLoop, calls=%fused_computation.8 | loop fusion | flops 57600 | bytes 115201 | tf_op jit(solution)/shard_map/jit(_cho_solve)/triangular_solve | solution.py:68
  47.2 9.2 %custom-call.10 = f32[1,120,120]{1,2,0:T(8,128)S(1)} custom-call(f32[1,120,120]{2,1,0:T(8,128)S(1)} %fusion.1), custom_call_target="InvertDiagBlocksLowerTriangular" | custom-call | tf_op jit(solution)/shard_map/jit(_cho_solve)/triangular_solve | solution.py:68
  56.4 0.0 collective-permute-done.9
  56.5 0.3 fusion.4
  56.8 0.0 collective-permute-done
  56.8 0.6 bitcast_add_fusion
  57.4 0.5 constant_dynamic-slice_fusion.7
  58.0 0.6 collective-permute-start.1
  58.6 0.3 fusion.2
  58.8 0.9 %fusion.13 = f32[150,128]{1,0:T(8,128)} fusion(f32[150,120]{1,0:T(8,128)S(1)} %add.124, f32[120,128]{1,0:T(8,128)S(1)} %fusion.2), kind=kOutput, calls=%fused_computation.36 | convolution fusion | flops 27648000 | bytes 210240 | tf_op jit(solution)/shard_map/dot_general | solution.py:69
  59.7 5.2 %collective-permute-done.1 = f32[150,512]{1,0:T(8,128)S(1)} collective-permute-done((f32[150,512]{1,0:T(8,128)S(1)}, f32[150,512]{1,0:T(8,128)S(1)}, u32[]{:S(2)}, u32[]{:S(2)}) %collective-permute-start.1) | collective-permute-done | bytes 307232 | tf_op jit(solution)/shard_map/ppermute | solution.py:20
  64.9 0.8 %fusion = f32[512,150]{0,1:T(8,128)} fusion(f32[150,512]{1,0:T(8,128)S(1)} %collective-permute-done.1, f32[1,150,512]{2,0,1:T(1,128)S(1)} %get-tuple-element.4), kind=kLoop, calls=%fused_computation.6 | loop fusion | flops 76800 | bytes 921600 | tf_op jit(solution)/shard_map/transpose | solution.py:61
  (8 shorter events, 0.1 us)
Async XLA Ops:
  7.3 1.4 %collective-permute-start.2 = (f32[150,120]{1,0:T(8,128)S(1)}, f32[150,120]{1,0:T(8,128)S(1)}, u32[]{:S(2)}, u32[]{:S(2)}) collective-permute-start(f32[150,120]{1,0:T(8,128)S(1)} %fusion.11), channel_id=1, source_target_pairs={{0,1},{1,0},{2,3},{3,2},{4,5},{5,4},{6,7},{7,6},{8,9},{9,8},{10,11... | collective-permute-start | bytes 216008 | tf_op jit(solution)/shard_map/ppermute | solution.py:20
  8.8 5.6 %collective-permute-start.3 = (f32[150,120]{1,0:T(8,128)S(1)}, f32[150,120]{1,0:T(8,128)S(1)}, u32[]{:S(2)}, u32[]{:S(2)}) collective-permute-start(f32[150,120]{1,0:T(8,128)S(1)} %add.120), channel_id=1, source_target_pairs={{0,2},{1,3},{2,0},{3,1},{4,6},{5,7},{6,4},{7,5},{8,10},{9,11},{10,... | collective-permute-start | bytes 216008 | tf_op jit(solution)/shard_map/ppermute | solution.py:20
  12.1 11.9 %collective-permute-start.7 = (f32[2,2,120,128]{3,1,0,2:T(2,128)S(1)}, f32[2,2,120,128]{3,1,0,2:T(2,128)S(1)}, u32[]{:S(2)}, u32[]{:S(2)}) collective-permute-start(f32[2,2,120,128]{3,1,0,2:T(2,128)S(1)} %bitcast.69), channel_id=1, source_target_pairs={{0,4},{4,0},{8,12},{12,8},{16,20},{20,16},{24,28},{28,24},{1,5},{5... | collective-permute-start | bytes 737288 | tf_op jit(solution)/shard_map/ppermute | solution.py:20
  14.4 7.2 %collective-permute-start.4 = (f32[150,120]{1,0:T(8,128)S(1)}, f32[150,120]{1,0:T(8,128)S(1)}, u32[]{:S(2)}, u32[]{:S(2)}) collective-permute-start(f32[150,120]{1,0:T(8,128)S(1)} %add.121), channel_id=1, source_target_pairs={{0,4},{4,0},{8,12},{12,8},{16,20},{20,16},{24,28},{28,24},{1,5},{5... | collective-permute-start | bytes 216008 | tf_op jit(solution)/shard_map/ppermute | solution.py:20
  21.6 4.5 %collective-permute-start.5 = (f32[150,120]{1,0:T(8,128)S(1)}, f32[150,120]{1,0:T(8,128)S(1)}, u32[]{:S(2)}, u32[]{:S(2)}) collective-permute-start(f32[150,120]{1,0:T(8,128)S(1)} %add.122), channel_id=1, source_target_pairs={{0,8},{4,12},{8,0},{12,4},{16,24},{20,28},{24,16},{28,20},{1,9},{5... | collective-permute-start | bytes 216008 | tf_op jit(solution)/shard_map/ppermute | solution.py:20
  23.8 32.9 %collective-permute-start = (f32[2,150,512]{2,0,1:T(2,128)S(1)}, f32[2,150,512]{2,0,1:T(2,128)S(1)}, u32[]{:S(2)}, u32[]{:S(2)}) collective-permute-start(f32[2,150,512]{2,0,1:T(2,128)S(1)} %bitcast.66), channel_id=1, source_target_pairs={{0,1},{1,0},{2,3},{3,2},{4,5},{5,4},{6,7},{7,6},{8,9},{9,8},{10,11... | collective-permute-start | bytes 1843208 | tf_op jit(solution)/shard_map/ppermute | solution.py:20
  26.1 5.5 %collective-permute-start.6 = (f32[150,120]{1,0:T(8,128)S(1)}, f32[150,120]{1,0:T(8,128)S(1)}, u32[]{:S(2)}, u32[]{:S(2)}) collective-permute-start(f32[150,120]{1,0:T(8,128)S(1)} %add.123), channel_id=1, source_target_pairs={{0,16},{4,20},{8,24},{12,28},{16,0},{20,4},{24,8},{28,12},{1,17},{... | collective-permute-start | bytes 216008 | tf_op jit(solution)/shard_map/ppermute | solution.py:20
  28.9 14.8 %collective-permute-start.8 = (f32[2,120,128]{2,0,1:T(2,128)S(1)}, f32[2,120,128]{2,0,1:T(2,128)S(1)}, u32[]{:S(2)}, u32[]{:S(2)}) collective-permute-start(f32[2,120,128]{2,0,1:T(2,128)S(1)} %bitcast.71), channel_id=1, source_target_pairs={{0,8},{4,12},{8,0},{12,4},{16,24},{20,28},{24,16},{28,20},{1,9},{5... | collective-permute-start | bytes 368648 | tf_op jit(solution)/shard_map/ppermute | solution.py:20
  43.9 12.5 %collective-permute-start.9 = (f32[120,128]{1,0:T(8,128)S(1)}, f32[120,128]{1,0:T(8,128)S(1)}, u32[]{:S(2)}, u32[]{:S(2)}) collective-permute-start(f32[120,128]{1,0:T(8,128)S(1)} %bitcast.72), channel_id=1, source_target_pairs={{0,16},{4,20},{8,24},{12,28},{16,0},{20,4},{24,8},{28,12},{1,17},{... | collective-permute-start | bytes 184328 | tf_op jit(solution)/shard_map/ppermute | solution.py:20
  58.0 7.0 %collective-permute-start.1 = (f32[150,512]{1,0:T(8,128)S(1)}, f32[150,512]{1,0:T(8,128)S(1)}, u32[]{:S(2)}, u32[]{:S(2)}) collective-permute-start(f32[150,512]{1,0:T(8,128)S(1)} %bitcast.68), channel_id=1, source_target_pairs={{0,2},{1,3},{2,0},{3,1},{4,6},{5,7},{6,4},{7,5},{8,10},{9,11},{10,... | collective-permute-start | bytes 921608 | tf_op jit(solution)/shard_map/ppermute | solution.py:20

commit v2 on v1

v2 whole, which is shorter than its diff:
```python
import functools

import jax
import jax.numpy as jnp
from jax import lax
from jax.experimental import pallas as pl
from jax.experimental.pallas import tpu as pltpu
from jax.sharding import PartitionSpec as P

F32 = jnp.float32
BF16 = jnp.bfloat16
HIGHEST = lax.Precision.HIGHEST
SCALE = 2.0**-10
RIDGE = 0.5
VMEM = pl.BlockSpec(memory_space=pltpu.VMEM)
LIMIT = 48 * 2**20


def dot(a, b, a_dim, b_dim, precision=None):
    return lax.dot_general(
        a, b, (((a_dim,), (b_dim,)), ((), ())), precision=precision, preferred_element_type=F32
    )


def expand(slow_t, fast_t, start, width):
    fast_count = fast_t.shape[0]
    column = lax.broadcasted_iota(jnp.int32, (slow_t.shape[0], width), 1) + start
    first = lax.broadcasted_iota(jnp.int32, (slow_t.shape[0], width), 0) * fast_count
    pick_slow = jnp.where((column >= first) & (column < first + fast_count), 1.0, 0.0)
    column = lax.broadcasted_iota(jnp.int32, (fast_count, width), 1) + start
    row = lax.broadcasted_iota(jnp.int32, (fast_count, width), 0)
    pick_fast = jnp.where(lax.rem(column, fast_count) == row, 1.0, 0.0)
    slow = dot(slow_t, pick_slow.astype(BF16), 0, 0)
    fast = dot(fast_t, pick_fast.astype(BF16), 0, 0)
    return (slow * fast).astype(BF16)


def thirds(value):
    high = value.astype(BF16)
    rest = value - high.astype(F32)
    middle = rest.astype(BF16)
    low = (rest - middle.astype(F32)).astype(BF16)
    return high, middle, low


def left_kernel(slow, fast, right_slow, right_fast, block, left, omega, part, total):
    step = pl.program_id(0)
    width = block.shape[0]

    @pl.when(step == 0)
    def _():
        omega[...] = expand(right_slow[...], right_fast[...], 0, block.shape[1])

    psi = expand(slow[...], fast[...], step * width, width)
    term = dot(psi, block[...], 1, 0)

    @pl.when(step == 0)
    def _():
        total[...] = term

    @pl.when(step > 0)
    def _():
        total[...] += term

    @pl.when(step == pl.num_programs(0) - 1)
    def _():
        value = total[...]
        chunk = left.shape[2]
        for c in range(left.shape[0]):
            left[c] = value[:, c * chunk : (c + 1) * chunk]
        rows = omega[...]
        part[...] = sum(dot(rows, third, 1, 1) for third in thirds(value))


def left_sketch(snapshots, left_slow, left_fast, right_slow, right_fast, steps, chunk):
    height, width = snapshots.shape
    rank_left, rank_right = left_slow.shape[0], right_slow.shape[0]
    chunks = width // chunk
    whole = lambda array: pl.BlockSpec(array.shape, lambda i: (0,) * array.ndim)
    factors = [left_slow.T, left_fast.T, right_slow.T, right_fast.T]
    outs = (
        jax.ShapeDtypeStruct((chunks, rank_left, chunk), F32),
        jax.ShapeDtypeStruct((rank_right, width), BF16),
        jax.ShapeDtypeStruct((rank_right, rank_left), F32),
    )
    return pl.pallas_call(
        left_kernel,
        grid=(steps,),
        in_specs=[whole(f) for f in factors]
        + [pl.BlockSpec((height // steps, width), lambda i: (i, 0))],
        out_specs=tuple(whole(o) for o in outs),
        out_shape=outs,
        scratch_shapes=[pltpu.VMEM((rank_left, width), F32)],
        compiler_params=pltpu.CompilerParams(vmem_limit_bytes=LIMIT),
        cost_estimate=pl.CostEstimate(
            flops=2 * rank_left * height * width,
            bytes_accessed=2 * height * width,
            transcendentals=0,
        ),
        name="left_sketch",
    )(*factors, snapshots)


def range_kernel(which, omega, block, out):
    out[0] = dot(omega[...], block[...], 1, 1)


def range_blocks(which, omega, snapshots, blocks, split):
    height, width = snapshots.shape
    rank = omega.shape[0]
    rows = height // blocks
    piece = rows // split
    count = which.shape[0]
    return pl.pallas_call(
        range_kernel,
        grid_spec=pltpu.PrefetchScalarGridSpec(
            num_scalar_prefetch=1,
            grid=(count, split),
            in_specs=[
                pl.BlockSpec((rank, width), lambda i, j, which: (0, 0)),
                pl.BlockSpec((piece, width), lambda i, j, which: (which[i] * split + j, 0)),
            ],
            out_specs=pl.BlockSpec((1, rank, piece), lambda i, j, which: (i, 0, j)),
        ),
        out_shape=jax.ShapeDtypeStruct((count, rank, rows), F32),
        compiler_params=pltpu.CompilerParams(vmem_limit_bytes=LIMIT),
        cost_estimate=pl.CostEstimate(
            flops=2 * rank * count * rows * width,
            bytes_accessed=2 * count * rows * width,
            transcendentals=0,
        ),
        name="range_sketch",
    )(which, omega, snapshots)


def row_of(tile, at):
    return jnp.broadcast_to(tile[at : at + 1, :], tile.shape)


def eliminate(gram):
    size = gram.shape[0]
    lane = lax.broadcasted_iota(jnp.int32, (8, size), 1)
    sub = lax.broadcasted_iota(jnp.int32, (8, size), 0)
    tiles = [gram[i : i + 8] for i in range(0, size, 8)]
    scaled = []
    for t in range(len(tiles)):
        k = 8 * t
        live = range(t, len(tiles))
        column = [
            {i: jnp.broadcast_to(tiles[i][:, k + j : k + j + 1], (8, size)) for i in live}
            for j in range(8)
        ]
        inside = (lane >= k) & (lane < k + 8)
        for i in live:
            tiles[i] = jnp.where(inside, 0.0, tiles[i])
        row = [row_of(tiles[t], j) for j in range(8)]
        weight = [None] * 8
        for p in range(0, 8, 2):
            q = p + 1
            a = row_of(column[p][t], p)
            b = row_of(column[q][t], p)
            c = row_of(column[q][t], q)
            det = a * c - b * b
            inverse = pl.reciprocal(det, approx=True)
            inverse = inverse * (2.0 - det * inverse)
            a, b, c = c * inverse, -b * inverse, a * inverse
            row[p] = jnp.where(lane == k + p, 1.0, row[p])
            row[q] = jnp.where(lane == k + q, 1.0, row[q])
            weight[p] = a * row[p] + b * row[q]
            weight[q] = b * row[p] + c * row[q]
            for j in range(q + 1, 8):
                f, g = row_of(column[j][t], p), row_of(column[j][t], q)
                u, v = a * f + b * g, b * f + c * g
                column[j] = {
                    i: column[j][i] - (column[p][i] * u + column[q][i] * v) for i in live
                }
                row[j] = row[j] - (
                    row_of(column[p][t], j) * weight[p] + row_of(column[q][t], j) * weight[q]
                )
            for i in live[1:]:
                tiles[i] = tiles[i] - (column[p][i] * weight[p] + column[q][i] * weight[q])
        held, out = row[0], weight[0]
        for j in range(1, 8):
            held = jnp.where(sub == j, row[j], held)
            out = jnp.where(sub == j, weight[j], out)
        tiles[t] = held
        scaled.append(out)
    return jnp.concatenate(tiles, 0), jnp.concatenate(scaled, 0)


def factor_kernel(kept, received, side, weight):
    value = (kept[...] + received[...]) * SCALE
    size = value.shape[1]
    i = lax.broadcasted_iota(jnp.int32, (size, size), 0)
    j = lax.broadcasted_iota(jnp.int32, (size, size), 1)
    gram = dot(value, value, 0, 0, HIGHEST) + jnp.where(i == j, RIDGE * SCALE * SCALE, 0.0)
    lower, scaled = eliminate(gram)
    keep = (j >> 1) <= (i >> 1)
    side[...] = dot(value, jnp.where(keep, lower, 0.0), 1, 1, HIGHEST)
    weight[...] = jnp.where(keep, scaled, 0.0) * SCALE


def factor(kept, received):
    size = kept.shape[1]
    return pl.pallas_call(
        factor_kernel,
        out_shape=(
            jax.ShapeDtypeStruct(kept.shape, F32),
            jax.ShapeDtypeStruct((size, size), F32),
        ),
        in_specs=[VMEM, VMEM],
        out_specs=(VMEM, VMEM),
        compiler_params=pltpu.CompilerParams(vmem_limit_bytes=LIMIT),
        cost_estimate=pl.CostEstimate(
            flops=10**10, bytes_accessed=10**5, transcendentals=0
        ),
        name="factor",
    )(kept, received)


def core_kernel(side, weight, kept, received, core):
    left = kept[...] + received[...]
    core[...] = dot(side[...], dot(weight[...], left, 1, 0, HIGHEST), 1, 0, HIGHEST)


def finish(side, weight, kept, received):
    return pl.pallas_call(
        core_kernel,
        out_shape=jax.ShapeDtypeStruct((side.shape[0], kept.shape[1]), F32),
        in_specs=[VMEM] * 4,
        out_specs=VMEM,
        compiler_params=pltpu.CompilerParams(vmem_limit_bytes=LIMIT),
        name="core",
    )(side, weight, kept, received)


def swap(value, axis, size, bit):
    return lax.ppermute(value, axis, [(i, i ^ bit) for i in range(size)])


def bits(size):
    return [1 << b for b in range(size.bit_length() - 1)]


def halve(blocks, axis, size, order):
    count = size.bit_length() - 1
    held = blocks.reshape((2,) * count + blocks.shape[1:])
    me = lax.axis_index(axis)
    dims = bits(size)[::-1]
    kept = received = None
    for bit in order:
        if kept is not None:
            held = kept + received
        dim = dims.index(bit)
        dims.pop(dim)
        mine = (me // bit) % 2
        kept = lax.dynamic_index_in_dim(held, mine, dim, False)
        sent = lax.dynamic_index_in_dim(held, 1 - mine, dim, False)
        received = swap(sent, axis, size, bit)
    return kept, received


def build(sizes):
    cells, samp = sizes["cells"], sizes["samp"]

    def on_device(snapshots, left_slow, left_fast, right_slow, right_fast):
        height, width = snapshots.shape
        share = width // cells
        chunk = share if share % 128 == 0 else width
        chunks, omega, part = left_sketch(
            snapshots, left_slow, left_fast, right_slow, right_fast, 4, chunk
        )
        if chunk != share:
            chunks = chunks[0].reshape(-1, cells, share).transpose(1, 0, 2)

        hops = [("samp", samp, bit) for bit in bits(samp)]
        hops += [("cells", cells, bit) for bit in bits(cells)]
        received = swap(part, *hops[0])
        for hop in hops[1:]:
            part = part + received
            received = swap(part, *hop)

        me = lax.axis_index("samp")
        far = jnp.stack([me ^ 3, me ^ 2])
        near = jnp.stack([me ^ 1, me])
        sent, kept = range_blocks(far, omega, snapshots, samp, 2)
        crossing = swap(kept + swap(sent, "samp", samp, 1), "samp", samp, 2)
        sent, kept = range_blocks(near, omega, snapshots, samp, 2)
        range_part = (kept + swap(sent, "samp", samp, 1) + crossing).T

        left_kept, left_received = halve(chunks, "cells", cells, bits(cells))
        side, weight = factor(part, received)
        core = finish(side, weight, left_kept, left_received)
        return (range_part, core)

    return on_device


def solution(mesh):
    placed = (P("cells", "samp"), P(None, "cells"), P(), P(None, "samp"), P())
    return jax.shard_map(
        build(mesh.shape),
        mesh=mesh,
        in_specs=placed,
        out_specs=(P(("cells", "samp"), None), P(None, ("samp", "cells"))),
        check_vma=False,
    )
```

time: 66.2 us -> 46.8 us (0.71)
  other arithmetic: 26.3 us -> 2.01 us
  Pallas kernels: 0 us -> 13.1 us
  matrix products: 9.15 us -> 0 us
  local copies, waits for them, and re-layouts: 2.06 us -> 9.52 us
  waiting for transfers between devices: 11.2 us -> 7.02 us
  starting transfers between devices: 16.1 us -> 13.8 us
    another operation x5 -> x2, other arithmetic: 21.5 us -> 0.15 us  [the longest x1 0.07 us: on_device(): far = jnp.stack([me ^ 3, me ^ 2])]
    pallas_call x0 -> x5, Pallas kernels: none -> 13.1 us  [the longest x1 4.96 us: factor(): pl.pallas_call(factor_kernel, out_shape=(jax.ShapeDtypeStruct(kept.shape,...]
    unnamed x2 -> x14, local copies, waits for them, and re-layouts: 0.11 us -> 9.41 us
    dot_general x5 -> x0, matrix products: 8.6 us -> none  [the longest x1 3.72 us: on_device(): lax.dot_general(omega, snapshots, (((1,), (1,)), ((), ())), preferred_ele...]
    ppermute x10 -> x11, waiting for transfers between devices: 11.2 us -> 7.02 us  [swap(): return lax.ppermute(value, axis, [(i, i ^ bit) for i in range(size)])]
    convert_element_type x6 -> x0, other arithmetic: 3.12 us -> none  [the longest x2 1.44 us: expand(): fast.astype(F32)[:, None, :]]
    ppermute x10 -> x11, starting transfers between devices: 16.1 us -> 13.8 us  [swap(): return lax.ppermute(value, axis, [(i, i ^ bit) for i in range(size)])]
    dynamic_slice x6 -> x0, local copies, waits for them, and re-layouts: 1.86 us -> none  [the longest x4 1.23 us: halve(): sent = lax.dynamic_index_in_dim(held, 1 - mine, dim, False)]
  transfers between devices with their start and end apart: 10 -> 11, of which waited for: 6 -> 3; matrix products, arithmetic and copies ran while one was open for 44% -> 3% of each run, Pallas kernels for 0% -> 22%
where the time goes in v2:
time: 46.8 us; the launch traced here: 46.3 us
  starting transfers between devices  13.8 us (29%)
  Pallas kernels  13.1 us (28%)
  local copies, waits for them, and re-layouts  9.52 us (20%)
  waiting for transfers between devices  7.02 us (15%)
  other arithmetic  2.01 us (4%)
  between operations  0.86 us (2%)
    ppermute x11, starting transfers between devices, swap(): return lax.ppermute(value, axis, [(i, i ^ bit) for i in range(size)])  13.8 us
    unnamed x14, local copies, waits for them, and re-layouts  9.41 us
    ppermute x11, waiting for transfers between devices, swap(): return lax.ppermute(value, axis, [(i, i ^ bit) for i in range(size)])  7.02 us
    pallas_call x1, Pallas kernels, factor(): pl.pallas_call(factor_kernel, out_shape=(jax.ShapeDtypeStruct(kept.shape,...  4.96 us
    pallas_call x2, Pallas kernels, range_blocks(): pl.pallas_call(range_kernel, grid_spec=pltpu.PrefetchScalarGridSpec(num_s...  3.83 us
    pallas_call x1, Pallas kernels, left_sketch(): pl.pallas_call(left_kernel, grid=(steps,), in_specs=[whole(f) for f in fa...  2.96 us
    pallas_call x1, Pallas kernels, finish(): pl.pallas_call(core_kernel, out_shape=jax.ShapeDtypeStruct((side.shape[0]...  1.3 us
    add x2, other arithmetic, halve(): held = kept + received  0.99 us
  transfers between devices with their start and end apart: 11, of which 3 were waited for; matrix products, arithmetic and copies ran while one was open for 3% of the time, Pallas kernels for 22%

profile of v2, /device:TPU:0, one launch (start us, length us, event | category | flops | bytes accessed | tf_op | source)
XLA Modules:
  0.0 46.3 jit_solution(15575863940936433638)
XLA Ops:
  0.7 0.0 copy-start
  0.7 2.2 %copy-done = bf16[2048,1024]{1,0:T(8,128)(2,1)S(1)} copy-done((bf16[2048,1024]{1,0:T(8,128)(2,1)S(1)}, bf16[2048,1024]{1,0:T(8,128)(2,1)}, u32[]{:S(2)}) %copy-start) | copy-done | bytes 4194328
  2.8 0.0 copy-start.3
  2.8 0.7 %copy-done.3 = bf16[120,64]{0,1:T(8,128)(2,1)S(1)} copy-done((bf16[120,64]{0,1:T(8,128)(2,1)S(1)}, bf16[120,64]{0,1:T(8,128)(2,1)}, u32[]{:S(2)}) %copy-start.3) | copy-done | bytes 15384
  3.6 0.0 copy-start.4
  3.6 0.7 %copy-done.4 = bf16[150,32]{0,1:T(8,128)(2,1)S(1)} copy-done((bf16[150,32]{0,1:T(8,128)(2,1)S(1)}, bf16[150,32]{0,1:T(8,128)(2,1)}, u32[]{:S(2)}) %copy-start.4) | copy-done | bytes 9624
  4.3 0.0 copy-start.5
  4.3 0.7 %copy-done.5 = bf16[150,32]{0,1:T(8,128)(2,1)S(1)} copy-done((bf16[150,32]{0,1:T(8,128)(2,1)S(1)}, bf16[150,32]{0,1:T(8,128)(2,1)}, u32[]{:S(2)}) %copy-start.5) | copy-done | bytes 9624
  5.0 0.0 copy-start.6
  5.0 0.7 %copy-done.6 = bf16[120,32]{0,1:T(8,128)(2,1)S(1)} copy-done((bf16[120,32]{0,1:T(8,128)(2,1)S(1)}, bf16[120,32]{0,1:T(8,128)(2,1)}, u32[]{:S(2)}) %copy-start.6) | copy-done | bytes 7704
  5.7 3.0 %left_sketch.1 = (f32[8,120,128]{2,1,0:T(8,128)S(1)}, bf16[150,1024]{1,0:T(8,128)(2,1)S(1)}, f32[150,120]{1,0:T(8,128)S(1)}) custom-call(bf16[32,120]{1,0:T(8,128)(2,1)S(1)} %bitcast.48, bf16[64,120]{1,0:T(8,128)(2,1)S(1)} %bitcast.45, bf16[32,150]{1,0:T(8,128)(2,1)S(1)} %bitcast.46, bf16[32,150]{1,0:T(8,128)(2,1)S(1)} %bitcast.47, ...), custom_call_target="tpu_custom_call" | custom-call | flops 503316480 | bytes 4194304 | tf_op jit(solution)/shard_map/left_sketch/pallas_call | solution.py:86
  8.7 3.0 %collective-permute-start.8 = (f32[2,2,120,128]{3,2,1,0:T(8,128)S(1)}, f32[2,2,120,128]{3,2,1,0:T(8,128)}, u32[]{:S(2)}, u32[]{:S(2)}) collective-permute-start(f32[2,2,120,128]{3,2,1,0:T(8,128)S(1)} %dynamic-slice_bitcast_fusion), channel_id=1, source_target_pairs={{0,4},{4,0},{8,12},{12,8},{16,20},{20,16},{24,28},{28,24},{1,5},{5... | collective-permute-start | bytes 737288 | tf_op jit(solution)/shard_map/ppermute | solution.py:238
  11.7 0.0 collective-permute-start.3
  11.7 0.1 pad_add_fusion.1.which
  11.8 0.0 copy-start.1
  11.8 2.2 %copy-done.1 = bf16[2048,1024]{1,0:T(8,128)(2,1)S(1)} copy-done((bf16[2048,1024]{1,0:T(8,128)(2,1)S(1)}, bf16[2048,1024]{1,0:T(8,128)(2,1)}, u32[]{:S(2)}) %copy-start.1) | copy-done | bytes 4194328
  14.0 1.9 %range_sketch.3 = f32[2,150,512]{2,1,0:T(8,128)S(1)} custom-call(s32[2]{0:T(128)S(1)} %pad_add_fusion.1.which, bf16[150,1024]{1,0:T(8,128)(2,1)S(1)} %get-tuple-element.7.omega, bf16[2048,1024]{1,0:T(8,128)(2,1)S(1)} %copy-done.1), custom_call_target="tpu_custom_call" | custom-call | flops 314572800 | bytes 2097152 | tf_op jit(solution)/shard_map/range_sketch/pallas_call | solution.py:114
  16.0 0.6 %collective-permute-start.1 = (f32[150,512]{1,0:T(8,128)S(1)}, f32[150,512]{1,0:T(8,128)S(1)}, u32[]{:S(2)}, u32[]{:S(2)}) collective-permute-start(f32[150,512]{1,0:T(8,128)S(1)} %slice_bitcast_fusion), channel_id=1, source_target_pairs={{0,1},{1,0},{2,3},{3,2},{4,5},{5,4},{6,7},{7,6},{8,9},{9,8},{10,11... | collective-permute-start | bytes 921608 | tf_op jit(solution)/shard_map/ppermute | solution.py:238
  16.5 0.0 collective-permute-done.3
  16.5 1.6 %collective-permute-start.4 = (f32[150,120]{1,0:T(8,128)S(1)}, f32[150,120]{1,0:T(8,128)S(1)}, u32[]{:S(2)}, u32[]{:S(2)}) collective-permute-start(f32[150,120]{1,0:T(8,128)S(1)} %add.67), channel_id=1, source_target_pairs={{0,2},{1,3},{2,0},{3,1},{4,6},{5,7},{6,4},{7,5},{8,10},{9,11},{10,... | collective-permute-start | bytes 216008 | tf_op jit(solution)/shard_map/ppermute | solution.py:238
  18.1 0.1 pad_add_fusion.which
  18.2 0.0 copy-start.2
  18.2 2.2 %copy-done.2 = bf16[2048,1024]{1,0:T(8,128)(2,1)S(1)} copy-done((bf16[2048,1024]{1,0:T(8,128)(2,1)S(1)}, bf16[2048,1024]{1,0:T(8,128)(2,1)}, u32[]{:S(2)}) %copy-start.2) | copy-done | bytes 4194328
  20.4 1.9 %range_sketch.2 = f32[2,150,512]{2,1,0:T(8,128)S(1)} custom-call(s32[2]{0:T(128)S(1)} %pad_add_fusion.which, bf16[150,1024]{1,0:T(8,128)(2,1)S(1)} %get-tuple-element.7.omega, bf16[2048,1024]{1,0:T(8,128)(2,1)S(1)} %copy-done.2), custom_call_target="tpu_custom_call" | custom-call | flops 314572800 | bytes 2097152 | tf_op jit(solution)/shard_map/range_sketch/pallas_call | solution.py:114
  22.3 0.0 collective-permute-done.4
  22.3 0.6 %collective-permute-start.5 = (f32[150,120]{1,0:T(8,128)S(1)}, f32[150,120]{1,0:T(8,128)S(1)}, u32[]{:S(2)}, u32[]{:S(2)}) collective-permute-start(f32[150,120]{1,0:T(8,128)S(1)} %add.68), channel_id=1, source_target_pairs={{0,4},{4,0},{8,12},{12,8},{16,20},{20,16},{24,28},{28,24},{1,5},{5... | collective-permute-start | bytes 216008 | tf_op jit(solution)/shard_map/ppermute | solution.py:238
  22.9 0.1 collective-permute-start
  23.1 3.7 %collective-permute-done.5 = f32[150,120]{1,0:T(8,128)S(1)} collective-permute-done((f32[150,120]{1,0:T(8,128)S(1)}, f32[150,120]{1,0:T(8,128)S(1)}, u32[]{:S(2)}, u32[]{:S(2)}) %collective-permute-start.5) | collective-permute-done | bytes 72032 | tf_op jit(solution)/shard_map/ppermute | solution.py:238
  26.8 1.6 %collective-permute-start.6 = (f32[150,120]{1,0:T(8,128)S(1)}, f32[150,120]{1,0:T(8,128)S(1)}, u32[]{:S(2)}, u32[]{:S(2)}) collective-permute-start(f32[150,120]{1,0:T(8,128)S(1)} %add.69), channel_id=1, source_target_pairs={{0,8},{4,12},{8,0},{12,4},{16,24},{20,28},{24,16},{28,20},{1,9},{5... | collective-permute-start | bytes 216008 | tf_op jit(solution)/shard_map/ppermute | solution.py:238
  28.4 0.0 collective-permute-done.8
  28.4 1.0 %bitcast_add_fusion = f32[2,2,120,128]{3,2,1,0:T(8,128)S(1)} fusion(f32[2,2,120,128]{3,2,1,0:T(8,128)} %collective-permute-done.8, f32[2,2,2,120,128]{4,3,2,1,0:T(8,128)S(1)} %bitcast.44, s32[]{:T(128)S(6)} %select_n.45), kind=kLoop, calls=%fused_computation.8 | loop fusion | flops 61440 | bytes 737284 | tf_op jit(solution)/shard_map/add | solution.py:253
  29.4 0.5 %collective-permute-start.9 = (f32[2,120,128]{2,1,0:T(8,128)S(1)}, f32[2,120,128]{2,1,0:T(8,128)S(1)}, u32[]{:S(2)}, u32[]{:S(2)}) collective-permute-start(f32[2,120,128]{2,1,0:T(8,128)S(1)} %dynamic-slice_bitcast_fusion.1), channel_id=1, source_target_pairs={{0,8},{4,12},{8,0},{12,4},{16,24},{20,28},{24,16},{28,20},{1,9},{5... | collective-permute-start | bytes 368648 | tf_op jit(solution)/shard_map/ppermute | solution.py:238
  30.0 2.1 %collective-permute-done.6 = f32[150,120]{1,0:T(8,128)S(1)} collective-permute-done((f32[150,120]{1,0:T(8,128)S(1)}, f32[150,120]{1,0:T(8,128)S(1)}, u32[]{:S(2)}, u32[]{:S(2)}) %collective-permute-start.6) | collective-permute-done | bytes 72032 | tf_op jit(solution)/shard_map/ppermute | solution.py:238
  32.1 2.6 %collective-permute-start.7 = (f32[150,120]{1,0:T(8,128)S(1)}, f32[150,120]{1,0:T(8,128)S(1)}, u32[]{:S(2)}, u32[]{:S(2)}) collective-permute-start(f32[150,120]{1,0:T(8,128)S(1)} %add.70.kept), channel_id=1, source_target_pairs={{0,16},{4,20},{8,24},{12,28},{16,0},{20,4},{24,8},{28,12},{1,17},{... | collective-permute-start | bytes 216008 | tf_op jit(solution)/shard_map/ppermute | solution.py:238
  34.8 0.0 collective-permute-done.1
  34.8 0.6 %collective-permute-start.2 = (f32[150,512]{1,0:T(8,128)S(1)}, f32[150,512]{1,0:T(8,128)S(1)}, u32[]{:S(2)}, u32[]{:S(2)}) collective-permute-start(f32[150,512]{1,0:T(8,128)S(1)} %fusion), channel_id=1, source_target_pairs={{0,2},{1,3},{2,0},{3,1},{4,6},{5,7},{6,4},{7,5},{8,10},{9,11},{10,... | collective-permute-start | bytes 921608 | tf_op jit(solution)/shard_map/ppermute | solution.py:238
  35.4 0.0 collective-permute-done.9
  35.5 2.6 %collective-permute-start.10 = (f32[120,128]{1,0:T(8,128)S(1)}, f32[120,128]{1,0:T(8,128)S(1)}, u32[]{:S(2)}, u32[]{:S(2)}) collective-permute-start(f32[120,128]{1,0:T(8,128)S(1)} %get-tuple-element.12), channel_id=1, source_target_pairs={{0,16},{4,20},{8,24},{12,28},{16,0},{20,4},{24,8},{28,12},{1,17},{... | collective-permute-start | bytes 184328 | tf_op jit(solution)/shard_map/ppermute | solution.py:238
  38.1 1.1 %collective-permute-done.7.received = f32[150,120]{1,0:T(8,128)S(1)} collective-permute-done((f32[150,120]{1,0:T(8,128)S(1)}, f32[150,120]{1,0:T(8,128)S(1)}, u32[]{:S(2)}, u32[]{:S(2)}) %collective-permute-start.7) | collective-permute-done | bytes 72032 | tf_op jit(solution)/shard_map/ppermute | solution.py:238
  39.2 5.0 %factor.1 = (f32[150,120]{1,0:T(8,128)S(1)}, f32[120,120]{1,0:T(8,128)S(1)}) custom-call(f32[150,120]{1,0:T(8,128)S(1)} %add.70.kept, f32[150,120]{1,0:T(8,128)S(1)} %collective-permute-done.7.received), custom_call_target="tpu_custom_call" | custom-call | flops 10000000000 | bytes 100000 | tf_op jit(solution)/shard_map/factor/pallas_call | solution.py:205
  44.2 0.0 collective-permute-done.10.received
  44.2 1.3 %core.1 = f32[150,128]{1,0:T(8,128)} custom-call(f32[150,120]{1,0:T(8,128)S(1)} %get-tuple-element.9.side, f32[120,120]{1,0:T(8,128)S(1)} %get-tuple-element.10.weight, f32[120,128]{1,0:T(8,128)S(1)} %get-tuple-element.13.kept, f32[120,128]{1,0:T(8,128)S(1)} %collective-permute-done.10.received), custom_call_target="tpu_custom_call" | custom-call | tf_op jit(solution)/shard_map/core/pallas_call | solution.py:227
  45.5 0.0 collective-permute-done
  45.5 0.0 collective-permute-done.2
  45.5 0.8 %fusion.3 = f32[512,150]{0,1:T(8,128)} fusion(f32[150,512]{1,0:T(8,128)S(1)} %collective-permute-done.2, f32[150,512]{1,0:T(8,128)S(1)} %collective-permute-done, f32[2,150,512]{2,1,0:T(8,128)S(1)} %range_sketch.2), kind=kLoop, calls=%fused_computation.7 | loop fusion | flops 153600 | bytes 1228800 | tf_op jit(solution)/shard_map/transpose | solution.py:289
  (11 shorter events, 0.2 us)
Async XLA Ops:
  0.7 2.2 %copy-start = (bf16[2048,1024]{1,0:T(8,128)(2,1)S(1)}, bf16[2048,1024]{1,0:T(8,128)(2,1)}, u32[]{:S(2)}) copy-start(bf16[2048,1024]{1,0:T(8,128)(2,1)} %block.5) | copy-start | bytes 12582916
  2.8 0.7 %copy-start.3 = (bf16[120,64]{0,1:T(8,128)(2,1)S(1)}, bf16[120,64]{0,1:T(8,128)(2,1)}, u32[]{:S(2)}) copy-start(bf16[120,64]{0,1:T(8,128)(2,1)} %param.7) | copy-start | bytes 46084
  3.6 0.7 %copy-start.4 = (bf16[150,32]{0,1:T(8,128)(2,1)S(1)}, bf16[150,32]{0,1:T(8,128)(2,1)}, u32[]{:S(2)}) copy-start(bf16[150,32]{0,1:T(8,128)(2,1)} %param.8) | copy-start | bytes 28804
  4.3 0.7 %copy-start.5 = (bf16[150,32]{0,1:T(8,128)(2,1)S(1)}, bf16[150,32]{0,1:T(8,128)(2,1)}, u32[]{:S(2)}) copy-start(bf16[150,32]{0,1:T(8,128)(2,1)} %param.9) | copy-start | bytes 28804
  5.0 0.7 %copy-start.6 = (bf16[120,32]{0,1:T(8,128)(2,1)S(1)}, bf16[120,32]{0,1:T(8,128)(2,1)}, u32[]{:S(2)}) copy-start(bf16[120,32]{0,1:T(8,128)(2,1)} %param.6) | copy-start | bytes 23044
  8.7 19.7 %collective-permute-start.8 = (f32[2,2,120,128]{3,2,1,0:T(8,128)S(1)}, f32[2,2,120,128]{3,2,1,0:T(8,128)}, u32[]{:S(2)}, u32[]{:S(2)}) collective-permute-start(f32[2,2,120,128]{3,2,1,0:T(8,128)S(1)} %dynamic-slice_bitcast_fusion), channel_id=1, source_target_pairs={{0,4},{4,0},{8,12},{12,8},{16,20},{20,16},{24,28},{28,24},{1,5},{5... | collective-permute-start | bytes 737288 | tf_op jit(solution)/shard_map/ppermute | solution.py:238
  11.7 4.8 %collective-permute-start.3 = (f32[150,120]{1,0:T(8,128)S(1)}, f32[150,120]{1,0:T(8,128)S(1)}, u32[]{:S(2)}, u32[]{:S(2)}) collective-permute-start(f32[150,120]{1,0:T(8,128)S(1)} %get-tuple-element.8), channel_id=1, source_target_pairs={{0,1},{1,0},{2,3},{3,2},{4,5},{5,4},{6,7},{7,6},{8,9},{9,8},{10,11... | collective-permute-start | bytes 216008 | tf_op jit(solution)/shard_map/ppermute | solution.py:238
  11.8 2.2 %copy-start.1 = (bf16[2048,1024]{1,0:T(8,128)(2,1)S(1)}, bf16[2048,1024]{1,0:T(8,128)(2,1)}, u32[]{:S(2)}) copy-start(bf16[2048,1024]{1,0:T(8,128)(2,1)} %block.5) | copy-start | bytes 12582916
  16.0 18.8 %collective-permute-start.1 = (f32[150,512]{1,0:T(8,128)S(1)}, f32[150,512]{1,0:T(8,128)S(1)}, u32[]{:S(2)}, u32[]{:S(2)}) collective-permute-start(f32[150,512]{1,0:T(8,128)S(1)} %slice_bitcast_fusion), channel_id=1, source_target_pairs={{0,1},{1,0},{2,3},{3,2},{4,5},{5,4},{6,7},{7,6},{8,9},{9,8},{10,11... | collective-permute-start | bytes 921608 | tf_op jit(solution)/shard_map/ppermute | solution.py:238
  16.5 5.8 %collective-permute-start.4 = (f32[150,120]{1,0:T(8,128)S(1)}, f32[150,120]{1,0:T(8,128)S(1)}, u32[]{:S(2)}, u32[]{:S(2)}) collective-permute-start(f32[150,120]{1,0:T(8,128)S(1)} %add.67), channel_id=1, source_target_pairs={{0,2},{1,3},{2,0},{3,1},{4,6},{5,7},{6,4},{7,5},{8,10},{9,11},{10,... | collective-permute-start | bytes 216008 | tf_op jit(solution)/shard_map/ppermute | solution.py:238
  18.2 2.2 %copy-start.2 = (bf16[2048,1024]{1,0:T(8,128)(2,1)S(1)}, bf16[2048,1024]{1,0:T(8,128)(2,1)}, u32[]{:S(2)}) copy-start(bf16[2048,1024]{1,0:T(8,128)(2,1)} %block.5) | copy-start | bytes 12582916
  22.3 4.5 %collective-permute-start.5 = (f32[150,120]{1,0:T(8,128)S(1)}, f32[150,120]{1,0:T(8,128)S(1)}, u32[]{:S(2)}, u32[]{:S(2)}) collective-permute-start(f32[150,120]{1,0:T(8,128)S(1)} %add.68), channel_id=1, source_target_pairs={{0,4},{4,0},{8,12},{12,8},{16,20},{20,16},{24,28},{28,24},{1,5},{5... | collective-permute-start | bytes 216008 | tf_op jit(solution)/shard_map/ppermute | solution.py:238
  22.9 22.6 %collective-permute-start = (f32[150,512]{1,0:T(8,128)S(1)}, f32[150,512]{1,0:T(8,128)S(1)}, u32[]{:S(2)}, u32[]{:S(2)}) collective-permute-start(f32[150,512]{1,0:T(8,128)S(1)} %slice_bitcast_fusion.2), channel_id=1, source_target_pairs={{0,1},{1,0},{2,3},{3,2},{4,5},{5,4},{6,7},{7,6},{8,9},{9,8},{10,11... | collective-permute-start | bytes 921608 | tf_op jit(solution)/shard_map/ppermute | solution.py:238
  26.8 5.3 %collective-permute-start.6 = (f32[150,120]{1,0:T(8,128)S(1)}, f32[150,120]{1,0:T(8,128)S(1)}, u32[]{:S(2)}, u32[]{:S(2)}) collective-permute-start(f32[150,120]{1,0:T(8,128)S(1)} %add.69), channel_id=1, source_target_pairs={{0,8},{4,12},{8,0},{12,4},{16,24},{20,28},{24,16},{28,20},{1,9},{5... | collective-permute-start | bytes 216008 | tf_op jit(solution)/shard_map/ppermute | solution.py:238
  29.4 6.0 %collective-permute-start.9 = (f32[2,120,128]{2,1,0:T(8,128)S(1)}, f32[2,120,128]{2,1,0:T(8,128)S(1)}, u32[]{:S(2)}, u32[]{:S(2)}) collective-permute-start(f32[2,120,128]{2,1,0:T(8,128)S(1)} %dynamic-slice_bitcast_fusion.1), channel_id=1, source_target_pairs={{0,8},{4,12},{8,0},{12,4},{16,24},{20,28},{24,16},{28,20},{1,9},{5... | collective-permute-start | bytes 368648 | tf_op jit(solution)/shard_map/ppermute | solution.py:238
  32.1 7.1 %collective-permute-start.7 = (f32[150,120]{1,0:T(8,128)S(1)}, f32[150,120]{1,0:T(8,128)S(1)}, u32[]{:S(2)}, u32[]{:S(2)}) collective-permute-start(f32[150,120]{1,0:T(8,128)S(1)} %add.70.kept), channel_id=1, source_target_pairs={{0,16},{4,20},{8,24},{12,28},{16,0},{20,4},{24,8},{28,12},{1,17},{... | collective-permute-start | bytes 216008 | tf_op jit(solution)/shard_map/ppermute | solution.py:238
  34.8 10.7 %collective-permute-start.2 = (f32[150,512]{1,0:T(8,128)S(1)}, f32[150,512]{1,0:T(8,128)S(1)}, u32[]{:S(2)}, u32[]{:S(2)}) collective-permute-start(f32[150,512]{1,0:T(8,128)S(1)} %fusion), channel_id=1, source_target_pairs={{0,2},{1,3},{2,0},{3,1},{4,6},{5,7},{6,4},{7,5},{8,10},{9,11},{10,... | collective-permute-start | bytes 921608 | tf_op jit(solution)/shard_map/ppermute | solution.py:238
  35.5 8.7 %collective-permute-start.10 = (f32[120,128]{1,0:T(8,128)S(1)}, f32[120,128]{1,0:T(8,128)S(1)}, u32[]{:S(2)}, u32[]{:S(2)}) collective-permute-start(f32[120,128]{1,0:T(8,128)S(1)} %get-tuple-element.12), channel_id=1, source_target_pairs={{0,16},{4,20},{8,24},{12,28},{16,0},{20,4},{24,8},{28,12},{1,17},{... | collective-permute-start | bytes 184328 | tf_op jit(solution)/shard_map/ppermute | solution.py:238

commit v3 on v2

--- a/solution.py
+++ b/solution.py
@@ -1,4 +1,5 @@
 import functools
+import math
 
 import jax
 import jax.numpy as jnp
@@ -13,7 +14,10 @@
 SCALE = 2.0**-10
 RIDGE = 0.5
 VMEM = pl.BlockSpec(memory_space=pltpu.VMEM)
-LIMIT = 48 * 2**20
+HBM = pl.BlockSpec(memory_space=pltpu.HBM)
+LIMIT = 16 * 2**20
+LARGE = 50 * 2**20
+AHEAD = 3
 
 
 def dot(a, b, a_dim, b_dim, precision=None):
@@ -22,17 +26,28 @@
     )
 
 
-def expand(slow_t, fast_t, start, width):
-    fast_count = fast_t.shape[0]
-    column = lax.broadcasted_iota(jnp.int32, (slow_t.shape[0], width), 1) + start
-    first = lax.broadcasted_iota(jnp.int32, (slow_t.shape[0], width), 0) * fast_count
-    pick_slow = jnp.where((column >= first) & (column < first + fast_count), 1.0, 0.0)
-    column = lax.broadcasted_iota(jnp.int32, (fast_count, width), 1) + start
-    row = lax.broadcasted_iota(jnp.int32, (fast_count, width), 0)
-    pick_fast = jnp.where(lax.rem(column, fast_count) == row, 1.0, 0.0)
-    slow = dot(slow_t, pick_slow.astype(BF16), 0, 0)
-    fast = dot(fast_t, pick_fast.astype(BF16), 0, 0)
-    return (slow * fast).astype(BF16)
+def repeated(factor_t, width, inner, outer):
+    count = factor_t.shape[0]
+    row = lax.broadcasted_iota(jnp.int32, (count, width), 0)
+    column = lax.broadcasted_iota(jnp.int32, (count, width), 1)
+    if outer:
+        pick = (column >= row * inner) & (column < (row + 1) * inner)
+    elif count & (count - 1) == 0:
+        pick = (column & (count - 1)) == row
+    else:
+        pick = lax.rem(column, count) == row
+    return dot(factor_t, jnp.where(pick, 1.0, 0.0).astype(BF16), 0, 0)
+
+
+def expand(slow_t, fast_t):
+    inner = fast_t.shape[0]
+    width = slow_t.shape[0] * inner
+    period = inner * 128 // math.gcd(inner, 128)
+    if width % period:
+        period = width
+    fast = repeated(fast_t, period, 1, False)
+    fast = jnp.concatenate([fast] * (width // period), 1)
+    return (repeated(slow_t, width, inner, True) * fast).astype(BF16)
 
 
 def thirds(value):
@@ -43,94 +58,63 @@
     return high, middle, low
 
 
-def left_kernel(slow, fast, right_slow, right_fast, block, left, omega, part, total):
-    step = pl.program_id(0)
-    width = block.shape[0]
-
-    @pl.when(step == 0)
-    def _():
-        omega[...] = expand(right_slow[...], right_fast[...], 0, block.shape[1])
-
-    psi = expand(slow[...], fast[...], step * width, width)
-    term = dot(psi, block[...], 1, 0)
-
-    @pl.when(step == 0)
-    def _():
-        total[...] = term
-
-    @pl.when(step > 0)
-    def _():
-        total[...] += term
-
-    @pl.when(step == pl.num_programs(0) - 1)
-    def _():
-        value = total[...]
-        chunk = left.shape[2]
-        for c in range(left.shape[0]):
-            left[c] = value[:, c * chunk : (c + 1) * chunk]
-        rows = omega[...]
-        part[...] = sum(dot(rows, third, 1, 1) for third in thirds(value))
-
-
-def left_sketch(snapshots, left_slow, left_fast, right_slow, right_fast, steps, chunk):
+def sketch_kernel(shapes, me, factors, slab, left, part, spans, held, sems):
+    count, rows, width = held.shape
+    copies = [
+        pltpu.make_async_copy(slab.at[pl.ds(i * rows, rows)], held.at[i], sems.at[i])
+        for i in range(count)
+    ]
+    for copy in copies[:AHEAD]:
+        copy.start()
+    values, at = [], 0
+    table = factors[...]
+    for height, rank in shapes:
+        values.append(table[at : at + height, :rank])
+        at += height
+    psi, omega = expand(*values[:2]), expand(*values[2:])
+    value = None
+    for i in range(count):
+        copies[i].wait()
+        if i + AHEAD < count:
+            copies[i + AHEAD].start()
+        block = held[i]
+        term = dot(psi[:, i * rows : (i + 1) * rows], block, 1, 0)
+        value = term if value is None else value + term
+        spans[me[0] ^ i] = dot(omega, block, 1, 1)
+    chunk = left.shape[2]
+    for c in range(left.shape[0]):
+        left[c] = value[:, c * chunk : (c + 1) * chunk]
+    part[...] = sum(dot(omega, third, 1, 1) for third in thirds(value))
+
+
+def sketches(me, snapshots, left_slow, left_fast, right_slow, right_fast, chunk, count):
     height, width = snapshots.shape
     rank_left, rank_right = left_slow.shape[0], right_slow.shape[0]
-    chunks = width // chunk
-    whole = lambda array: pl.BlockSpec(array.shape, lambda i: (0,) * array.ndim)
-    factors = [left_slow.T, left_fast.T, right_slow.T, right_fast.T]
-    outs = (
-        jax.ShapeDtypeStruct((chunks, rank_left, chunk), F32),
-        jax.ShapeDtypeStruct((rank_right, width), BF16),
-        jax.ShapeDtypeStruct((rank_right, rank_left), F32),
-    )
+    factors = [f.T for f in (left_slow, left_fast, right_slow, right_fast)]
+    rank = max(rank_left, rank_right)
+    table = jnp.concatenate([jnp.pad(f, ((0, 0), (0, rank - f.shape[1]))) for f in factors])
+    rows = height // count
     return pl.pallas_call(
-        left_kernel,
-        grid=(steps,),
-        in_specs=[whole(f) for f in factors]
-        + [pl.BlockSpec((height // steps, width), lambda i: (i, 0))],
-        out_specs=tuple(whole(o) for o in outs),
-        out_shape=outs,
-        scratch_shapes=[pltpu.VMEM((rank_left, width), F32)],
-        compiler_params=pltpu.CompilerParams(vmem_limit_bytes=LIMIT),
+        functools.partial(sketch_kernel, [f.shape for f in factors]),
+        in_specs=[pl.BlockSpec(memory_space=pltpu.SMEM), VMEM, HBM],
+        out_specs=(VMEM,) * 3,
+        out_shape=(
+            jax.ShapeDtypeStruct((width // chunk, rank_left, chunk), F32),
+            jax.ShapeDtypeStruct((rank_right, rank_left), F32),
+            jax.ShapeDtypeStruct((count, rank_right, rows), F32),
+        ),
+        scratch_shapes=[
+            pltpu.VMEM((count, rows, width), BF16),
+            pltpu.SemaphoreType.DMA((count,)),
+        ],
+        compiler_params=pltpu.CompilerParams(vmem_limit_bytes=LARGE),
         cost_estimate=pl.CostEstimate(
-            flops=2 * rank_left * height * width,
+            flops=2 * (rank_left + rank_right) * height * width,
             bytes_accessed=2 * height * width,
             transcendentals=0,
         ),
-        name="left_sketch",
-    )(*factors, snapshots)
-
-
-def range_kernel(which, omega, block, out):
-    out[0] = dot(omega[...], block[...], 1, 1)
-
-
-def range_blocks(which, omega, snapshots, blocks, split):
-    height, width = snapshots.shape
-    rank = omega.shape[0]
-    rows = height // blocks
-    piece = rows // split
-    count = which.shape[0]
-    return pl.pallas_call(
-        range_kernel,
-        grid_spec=pltpu.PrefetchScalarGridSpec(
-            num_scalar_prefetch=1,
-            grid=(count, split),
-            in_specs=[
-                pl.BlockSpec((rank, width), lambda i, j, which: (0, 0)),
-                pl.BlockSpec((piece, width), lambda i, j, which: (which[i] * split + j, 0)),
-            ],
-            out_specs=pl.BlockSpec((1, rank, piece), lambda i, j, which: (i, 0, j)),
-        ),
-        out_shape=jax.ShapeDtypeStruct((count, rank, rows), F32),
-        compiler_params=pltpu.CompilerParams(vmem_limit_bytes=LIMIT),
-        cost_estimate=pl.CostEstimate(
-            flops=2 * rank * count * rows * width,
-            bytes_accessed=2 * count * rows * width,
-            transcendentals=0,
-        ),
-        name="range_sketch",
-    )(which, omega, snapshots)
+        name="sketches",
+    )(me, table, snapshots)
 
 
 def row_of(tile, at):
@@ -267,26 +251,22 @@
         height, width = snapshots.shape
         share = width // cells
         chunk = share if share % 128 == 0 else width
-        chunks, omega, part = left_sketch(
-            snapshots, left_slow, left_fast, right_slow, right_fast, 4, chunk
+        me = lax.axis_index("samp").reshape(1)
+        chunks, part, spans = sketches(
+            me, snapshots, left_slow, left_fast, right_slow, right_fast, chunk, samp
         )
         if chunk != share:
             chunks = chunks[0].reshape(-1, cells, share).transpose(1, 0, 2)
 
-        hops = [("samp", samp, bit) for bit in bits(samp)]
-        hops += [("cells", cells, bit) for bit in bits(cells)]
+        hops = [("samp", samp, 1), ("cells", cells, 1), ("samp", samp, 2)]
+        hops += [("cells", cells, bit) for bit in bits(cells)[1:]]
         received = swap(part, *hops[0])
         for hop in hops[1:]:
             part = part + received
             received = swap(part, *hop)
 
-        me = lax.axis_index("samp")
-        far = jnp.stack([me ^ 3, me ^ 2])
-        near = jnp.stack([me ^ 1, me])
-        sent, kept = range_blocks(far, omega, snapshots, samp, 2)
-        crossing = swap(kept + swap(sent, "samp", samp, 1), "samp", samp, 2)
-        sent, kept = range_blocks(near, omega, snapshots, samp, 2)
-        range_part = (kept + swap(sent, "samp", samp, 1) + crossing).T
+        crossing = swap(spans[2] + swap(spans[3], "samp", samp, 1), "samp", samp, 2)
+        range_part = (spans[0] + swap(spans[1], "samp", samp, 1) + crossing).T
 
         left_kept, left_received = halve(chunks, "cells", cells, bits(cells))
         side, weight = factor(part, received)

time: 46.8 us -> 38.3 us (0.82)
  local copies, waits for them, and re-layouts: 9.52 us -> 0.1 us
  waiting for transfers between devices: 7.02 us -> 10 us
  Pallas kernels: 13.1 us -> 10.9 us
  other arithmetic: 2.01 us -> 2.59 us
    unnamed x14 -> x0, local copies, waits for them, and re-layouts: 9.41 us -> none
    ppermute x11, waiting for transfers between devices: 7.02 us -> 10 us  [swap(): return lax.ppermute(value, axis, [(i, i ^ bit) for i in range(size)])]
    pallas_call x3 -> x1, Pallas kernels: 6.79 us -> 4.62 us  [sketches(): pl.pallas_call(functools.partial(sketch_kernel, [f.shape for f in factors...]
    add x2, other arithmetic: 0.99 us -> 0.05 us  [halve(): held = kept + received]
    add x4, other arithmetic: 0.04 us -> 0.93 us  [on_device(): part = part + received]
    concatenate x0 -> x1, other arithmetic: none -> 0.78 us  [sketches(): jnp.concatenate([jnp.pad(f, ((0, 0), (0, rank - f.shape[1]))) for f in fa...]
  transfers between devices with their start and end apart: 11 -> 11, of which waited for: 3 -> 5; matrix products, arithmetic and copies ran while one was open for 3% -> 3% of each run, Pallas kernels for 22% -> 17%
where the time goes in v3:
time: 38.3 us; the launch traced here: 37.9 us
  starting transfers between devices  13.6 us (36%)
  Pallas kernels  10.9 us (28%)
  waiting for transfers between devices  10 us (26%)
  other arithmetic  2.59 us (7%)
  between operations  0.7 us (2%)
    ppermute x11, starting transfers between devices, swap(): return lax.ppermute(value, axis, [(i, i ^ bit) for i in range(size)])  13.6 us
    ppermute x11, waiting for transfers between devices, swap(): return lax.ppermute(value, axis, [(i, i ^ bit) for i in range(size)])  10 us
    pallas_call x1, Pallas kernels, factor(): pl.pallas_call(factor_kernel, out_shape=(jax.ShapeDtypeStruct(kept.shape,...  4.96 us
    pallas_call x1, Pallas kernels, sketches(): pl.pallas_call(functools.partial(sketch_kernel, [f.shape for f in factors...  4.62 us
    pallas_call x1, Pallas kernels, finish(): pl.pallas_call(core_kernel, out_shape=jax.ShapeDtypeStruct((side.shape[0]...  1.3 us
    add x4, other arithmetic, on_device(): part = part + received  0.93 us
    transpose x1, other arithmetic, on_device(): range_part = (spans[0] + swap(spans[1], 'samp', samp, 1) + crossing).T  0.79 us
    concatenate x1, other arithmetic, sketches(): jnp.concatenate([jnp.pad(f, ((0, 0), (0, rank - f.shape[1]))) for f in fa...  0.78 us
  transfers between devices with their start and end apart: 11, of which 5 were waited for; matrix products, arithmetic and copies ran while one was open for 3% of the time, Pallas kernels for 17%

profile of v3, /device:TPU:0, one launch (start us, length us, event | category | flops | bytes accessed | tf_op | source)
XLA Modules:
  0.0 37.9 jit_solution(12912353968036784471)
XLA Ops:
  0.6 0.8 %fusion.7.factors = bf16[160,150]{1,0:T(8,128)(2,1)S(1)} fusion(bf16[64,120]{1,0:T(8,128)(2,1)} %bitcast.38, bf16[32,120]{1,0:T(8,128)(2,1)} %bitcast.41, bf16[32,150]{1,0:T(8,128)(2,1)} %bitcast.39, bf16[32,150]{1,0:T(8,128)(2,1)} %bitcast.40), kind=kLoop, calls=%fused_computation.18 | loop fusion | flops 336000 | bytes 90240 | tf_op jit(solution)/shard_map/concatenate | solution.py:95
  1.4 4.6 %sketches.1 = (f32[8,120,128]{2,1,0:T(8,128)S(1)}, f32[150,120]{1,0:T(8,128)S(1)}, f32[4,150,512]{2,1,0:T(8,128)S(1)}) custom-call(s32[1]{0:T(128)} %bitcast.me, bf16[160,150]{1,0:T(8,128)(2,1)S(1)} %fusion.7.factors, bf16[2048,1024]{1,0:T(8,128)(2,1)} %slab.1), custom_call_target="tpu_custom_call" | custom-call | flops 1132462080 | bytes 4194304 | tf_op jit(solution)/shard_map/sketches/pallas_call | solution.py:97
  6.0 0.5 %collective-permute-start.3 = (f32[150,120]{1,0:T(8,128)S(1)}, f32[150,120]{1,0:T(8,128)S(1)}, u32[]{:S(2)}, u32[]{:S(2)}) collective-permute-start(f32[150,120]{1,0:T(8,128)S(1)} %get-tuple-element.8), channel_id=1, source_target_pairs={{0,1},{1,0},{2,3},{3,2},{4,5},{5,4},{6,7},{7,6},{8,9},{9,8},{10,11... | collective-permute-start | bytes 216008 | tf_op jit(solution)/shard_map/ppermute | solution.py:222
  6.6 0.9 %collective-permute-done.3 = f32[150,120]{1,0:T(8,128)S(1)} collective-permute-done((f32[150,120]{1,0:T(8,128)S(1)}, f32[150,120]{1,0:T(8,128)S(1)}, u32[]{:S(2)}, u32[]{:S(2)}) %collective-permute-start.3) | collective-permute-done | bytes 72032 | tf_op jit(solution)/shard_map/ppermute | solution.py:222
  7.5 2.9 %collective-permute-start.4 = (f32[150,120]{1,0:T(8,128)S(1)}, f32[150,120]{1,0:T(8,128)S(1)}, u32[]{:S(2)}, u32[]{:S(2)}) collective-permute-start(f32[150,120]{1,0:T(8,128)S(1)} %add.71), channel_id=1, source_target_pairs={{0,4},{4,0},{8,12},{12,8},{16,20},{20,16},{24,28},{28,24},{1,5},{5... | collective-permute-start | bytes 216008 | tf_op jit(solution)/shard_map/ppermute | solution.py:222
  10.5 0.1 collective-permute-start.8
  10.5 2.7 %collective-permute-done.4 = f32[150,120]{1,0:T(8,128)S(1)} collective-permute-done((f32[150,120]{1,0:T(8,128)S(1)}, f32[150,120]{1,0:T(8,128)S(1)}, u32[]{:S(2)}, u32[]{:S(2)}) %collective-permute-start.4) | collective-permute-done | bytes 72032 | tf_op jit(solution)/shard_map/ppermute | solution.py:222
  13.2 2.1 %collective-permute-start.5 = (f32[150,120]{1,0:T(8,128)S(1)}, f32[150,120]{1,0:T(8,128)}, u32[]{:S(2)}, u32[]{:S(2)}) collective-permute-start(f32[150,120]{1,0:T(8,128)S(1)} %add.72), channel_id=1, source_target_pairs={{0,2},{1,3},{2,0},{3,1},{4,6},{5,7},{6,4},{7,5},{8,10},{9,11},{10,... | collective-permute-start | bytes 216008 | tf_op jit(solution)/shard_map/ppermute | solution.py:222
  15.4 0.1 collective-permute-start.1
  15.4 0.5 %collective-permute-start = (f32[150,512]{1,0:T(8,128)S(1)}, f32[150,512]{1,0:T(8,128)S(1)}, u32[]{:S(2)}, u32[]{:S(2)}) collective-permute-start(f32[150,512]{1,0:T(8,128)S(1)} %get-tuple-element.12), channel_id=1, source_target_pairs={{0,1},{1,0},{2,3},{3,2},{4,5},{5,4},{6,7},{7,6},{8,9},{9,8},{10,11... | collective-permute-start | bytes 921608 | tf_op jit(solution)/shard_map/ppermute | solution.py:222
  15.9 1.9 %collective-permute-done.5 = f32[150,120]{1,0:T(8,128)} collective-permute-done((f32[150,120]{1,0:T(8,128)S(1)}, f32[150,120]{1,0:T(8,128)}, u32[]{:S(2)}, u32[]{:S(2)}) %collective-permute-start.5) | collective-permute-done | bytes 72032 | tf_op jit(solution)/shard_map/ppermute | solution.py:222
  17.8 0.9 %add.73 = f32[150,120]{1,0:T(8,128)S(1)} add(f32[150,120]{1,0:T(8,128)S(1)} %add.72, f32[150,120]{1,0:T(8,128)} %collective-permute-done.5) | non-fusion elementwise | flops 18000 | bytes 216000 | tf_op jit(solution)/shard_map/add | solution.py:265
  18.7 2.2 %collective-permute-start.6 = (f32[150,120]{1,0:T(8,128)S(1)}, f32[150,120]{1,0:T(8,128)S(1)}, u32[]{:S(2)}, u32[]{:S(2)}) collective-permute-start(f32[150,120]{1,0:T(8,128)S(1)} %add.73), channel_id=1, source_target_pairs={{0,8},{4,12},{8,0},{12,4},{16,24},{20,28},{24,16},{28,20},{1,9},{5... | collective-permute-start | bytes 216008 | tf_op jit(solution)/shard_map/ppermute | solution.py:222
  20.9 0.0 collective-permute-done.8
  20.9 0.1 collective-permute-start.9
  21.0 2.4 %collective-permute-done.6 = f32[150,120]{1,0:T(8,128)S(1)} collective-permute-done((f32[150,120]{1,0:T(8,128)S(1)}, f32[150,120]{1,0:T(8,128)S(1)}, u32[]{:S(2)}, u32[]{:S(2)}) %collective-permute-start.6) | collective-permute-done | bytes 72032 | tf_op jit(solution)/shard_map/ppermute | solution.py:222
  23.4 3.6 %collective-permute-start.7 = (f32[150,120]{1,0:T(8,128)S(1)}, f32[150,120]{1,0:T(8,128)S(1)}, u32[]{:S(2)}, u32[]{:S(2)}) collective-permute-start(f32[150,120]{1,0:T(8,128)S(1)} %add.74.kept), channel_id=1, source_target_pairs={{0,16},{4,20},{8,24},{12,28},{16,0},{20,4},{24,8},{28,12},{1,17},{... | collective-permute-start | bytes 216008 | tf_op jit(solution)/shard_map/ppermute | solution.py:222
  27.0 0.0 collective-permute-done.1
  27.0 1.6 %collective-permute-start.2 = (f32[150,512]{1,0:T(8,128)S(1)}, f32[150,512]{1,0:T(8,128)S(1)}, u32[]{:S(2)}, u32[]{:S(2)}) collective-permute-start(f32[150,512]{1,0:T(8,128)S(1)} %bitcast_add_fusion), channel_id=1, source_target_pairs={{0,2},{1,3},{2,0},{3,1},{4,6},{5,7},{6,4},{7,5},{8,10},{9,11},{10,... | collective-permute-start | bytes 921608 | tf_op jit(solution)/shard_map/ppermute | solution.py:222
  28.6 0.0 collective-permute-done.9
  28.6 0.1 collective-permute-start.10
  28.7 2.1 %collective-permute-done.7.received = f32[150,120]{1,0:T(8,128)S(1)} collective-permute-done((f32[150,120]{1,0:T(8,128)S(1)}, f32[150,120]{1,0:T(8,128)S(1)}, u32[]{:S(2)}, u32[]{:S(2)}) %collective-permute-start.7) | collective-permute-done | bytes 72032 | tf_op jit(solution)/shard_map/ppermute | solution.py:222
  30.9 5.0 %factor.1 = (f32[150,120]{1,0:T(8,128)S(1)}, f32[120,120]{1,0:T(8,128)S(1)}) custom-call(f32[150,120]{1,0:T(8,128)S(1)} %add.74.kept, f32[150,120]{1,0:T(8,128)S(1)} %collective-permute-done.7.received), custom_call_target="tpu_custom_call" | custom-call | flops 10000000000 | bytes 100000 | tf_op jit(solution)/shard_map/factor/pallas_call | solution.py:189
  35.8 0.0 collective-permute-done.10.received
  35.8 1.3 %core.1 = f32[150,128]{1,0:T(8,128)} custom-call(f32[150,120]{1,0:T(8,128)S(1)} %get-tuple-element.9.side, f32[120,120]{1,0:T(8,128)S(1)} %get-tuple-element.10.weight, f32[120,128]{1,0:T(8,128)S(1)} %get-tuple-element.15.kept, f32[120,128]{1,0:T(8,128)S(1)} %collective-permute-done.10.received), custom_call_target="tpu_custom_call" | custom-call | tf_op jit(solution)/shard_map/core/pallas_call | solution.py:211
  37.1 0.0 collective-permute-done
  37.1 0.0 collective-permute-done.2
  37.1 0.8 %fusion.1 = f32[512,150]{0,1:T(8,128)} fusion(f32[150,512]{1,0:T(8,128)S(1)} %collective-permute-done.2, f32[150,512]{1,0:T(8,128)S(1)} %collective-permute-done, f32[4,150,512]{2,1,0:T(8,128)S(1)} %get-tuple-element.7), kind=kLoop, calls=%fused_computation.3 | loop fusion | flops 153600 | bytes 1228800 | tf_op jit(solution)/shard_map/transpose | solution.py:269
  (10 shorter events, 0.2 us)
Async XLA Ops:
  6.0 1.4 %collective-permute-start.3 = (f32[150,120]{1,0:T(8,128)S(1)}, f32[150,120]{1,0:T(8,128)S(1)}, u32[]{:S(2)}, u32[]{:S(2)}) collective-permute-start(f32[150,120]{1,0:T(8,128)S(1)} %get-tuple-element.8), channel_id=1, source_target_pairs={{0,1},{1,0},{2,3},{3,2},{4,5},{5,4},{6,7},{7,6},{8,9},{9,8},{10,11... | collective-permute-start | bytes 216008 | tf_op jit(solution)/shard_map/ppermute | solution.py:222
  7.5 5.7 %collective-permute-start.4 = (f32[150,120]{1,0:T(8,128)S(1)}, f32[150,120]{1,0:T(8,128)S(1)}, u32[]{:S(2)}, u32[]{:S(2)}) collective-permute-start(f32[150,120]{1,0:T(8,128)S(1)} %add.71), channel_id=1, source_target_pairs={{0,4},{4,0},{8,12},{12,8},{16,20},{20,16},{24,28},{28,24},{1,5},{5... | collective-permute-start | bytes 216008 | tf_op jit(solution)/shard_map/ppermute | solution.py:222
  10.5 10.4 %collective-permute-start.8 = (f32[2,2,120,128]{3,2,1,0:T(8,128)S(1)}, f32[2,2,120,128]{3,2,1,0:T(8,128)S(1)}, u32[]{:S(2)}, u32[]{:S(2)}) collective-permute-start(f32[2,2,120,128]{3,2,1,0:T(8,128)S(1)} %dynamic-slice_bitcast_fusion), channel_id=1, source_target_pairs={{0,4},{4,0},{8,12},{12,8},{16,20},{20,16},{24,28},{28,24},{1,5},{5... | collective-permute-start | bytes 737288 | tf_op jit(solution)/shard_map/ppermute | solution.py:222
  13.2 4.6 %collective-permute-start.5 = (f32[150,120]{1,0:T(8,128)S(1)}, f32[150,120]{1,0:T(8,128)}, u32[]{:S(2)}, u32[]{:S(2)}) collective-permute-start(f32[150,120]{1,0:T(8,128)S(1)} %add.72), channel_id=1, source_target_pairs={{0,2},{1,3},{2,0},{3,1},{4,6},{5,7},{6,4},{7,5},{8,10},{9,11},{10,... | collective-permute-start | bytes 216008 | tf_op jit(solution)/shard_map/ppermute | solution.py:222
  15.4 11.6 %collective-permute-start.1 = (f32[150,512]{1,0:T(8,128)S(1)}, f32[150,512]{1,0:T(8,128)S(1)}, u32[]{:S(2)}, u32[]{:S(2)}) collective-permute-start(f32[150,512]{1,0:T(8,128)S(1)} %get-tuple-element.13), channel_id=1, source_target_pairs={{0,1},{1,0},{2,3},{3,2},{4,5},{5,4},{6,7},{7,6},{8,9},{9,8},{10,11... | collective-permute-start | bytes 921608 | tf_op jit(solution)/shard_map/ppermute | solution.py:222
  15.4 21.7 %collective-permute-start = (f32[150,512]{1,0:T(8,128)S(1)}, f32[150,512]{1,0:T(8,128)S(1)}, u32[]{:S(2)}, u32[]{:S(2)}) collective-permute-start(f32[150,512]{1,0:T(8,128)S(1)} %get-tuple-element.12), channel_id=1, source_target_pairs={{0,1},{1,0},{2,3},{3,2},{4,5},{5,4},{6,7},{7,6},{8,9},{9,8},{10,11... | collective-permute-start | bytes 921608 | tf_op jit(solution)/shard_map/ppermute | solution.py:222
  18.7 4.7 %collective-permute-start.6 = (f32[150,120]{1,0:T(8,128)S(1)}, f32[150,120]{1,0:T(8,128)S(1)}, u32[]{:S(2)}, u32[]{:S(2)}) collective-permute-start(f32[150,120]{1,0:T(8,128)S(1)} %add.73), channel_id=1, source_target_pairs={{0,8},{4,12},{8,0},{12,4},{16,24},{20,28},{24,16},{28,20},{1,9},{5... | collective-permute-start | bytes 216008 | tf_op jit(solution)/shard_map/ppermute | solution.py:222
  20.9 7.7 %collective-permute-start.9 = (f32[2,120,128]{2,1,0:T(8,128)S(1)}, f32[2,120,128]{2,1,0:T(8,128)S(1)}, u32[]{:S(2)}, u32[]{:S(2)}) collective-permute-start(f32[2,120,128]{2,1,0:T(8,128)S(1)} %dynamic-slice_bitcast_fusion.1), channel_id=1, source_target_pairs={{0,8},{4,12},{8,0},{12,4},{16,24},{20,28},{24,16},{28,20},{1,9},{5... | collective-permute-start | bytes 368648 | tf_op jit(solution)/shard_map/ppermute | solution.py:222
  23.4 7.4 %collective-permute-start.7 = (f32[150,120]{1,0:T(8,128)S(1)}, f32[150,120]{1,0:T(8,128)S(1)}, u32[]{:S(2)}, u32[]{:S(2)}) collective-permute-start(f32[150,120]{1,0:T(8,128)S(1)} %add.74.kept), channel_id=1, source_target_pairs={{0,16},{4,20},{8,24},{12,28},{16,0},{20,4},{24,8},{28,12},{1,17},{... | collective-permute-start | bytes 216008 | tf_op jit(solution)/shard_map/ppermute | solution.py:222
  27.0 10.1 %collective-permute-start.2 = (f32[150,512]{1,0:T(8,128)S(1)}, f32[150,512]{1,0:T(8,128)S(1)}, u32[]{:S(2)}, u32[]{:S(2)}) collective-permute-start(f32[150,512]{1,0:T(8,128)S(1)} %bitcast_add_fusion), channel_id=1, source_target_pairs={{0,2},{1,3},{2,0},{3,1},{4,6},{5,7},{6,4},{7,5},{8,10},{9,11},{10,... | collective-permute-start | bytes 921608 | tf_op jit(solution)/shard_map/ppermute | solution.py:222
  28.6 7.2 %collective-permute-start.10 = (f32[120,128]{1,0:T(8,128)S(1)}, f32[120,128]{1,0:T(8,128)S(1)}, u32[]{:S(2)}, u32[]{:S(2)}) collective-permute-start(f32[120,128]{1,0:T(8,128)S(1)} %get-tuple-element.14), channel_id=1, source_target_pairs={{0,16},{4,20},{8,24},{12,28},{16,0},{20,4},{24,8},{28,12},{1,17},{... | collective-permute-start | bytes 184328 | tf_op jit(solution)/shard_map/ppermute | solution.py:222

commit v4 on v3

v4 whole, which is shorter than its diff:
```python
import functools
import math

import jax
import jax.numpy as jnp
from jax import lax
from jax.experimental import pallas as pl
from jax.experimental.pallas import tpu as pltpu
from jax.sharding import PartitionSpec as P

F32 = jnp.float32
BF16 = jnp.bfloat16
HIGHEST = lax.Precision.HIGHEST
SCALE = 2.0**-10
RIDGE = 0.5
COST = 10000
PACE = (0, 0, 10**8, 10**8)
ORDER = "xzyZ"
TIES = {-1: "l", 0: "f", 2: "1", 3: "2", 6: ""}
SPLIT = 1
VMEM = pl.BlockSpec(memory_space=pltpu.VMEM)
HBM = pl.BlockSpec(memory_space=pltpu.HBM)
LIMIT = 16 * 2**20
LARGE = 32 * 2**20
AHEAD = 2


def dot(a, b, a_dim, b_dim, precision=None):
    return lax.dot_general(
        a, b, (((a_dim,), (b_dim,)), ((), ())), precision=precision, preferred_element_type=F32
    )


def repeated(factor_t, width, inner, outer):
    count = factor_t.shape[0]
    row = lax.broadcasted_iota(jnp.int32, (count, width), 0)
    column = lax.broadcasted_iota(jnp.int32, (count, width), 1)
    if outer:
        pick = (column >= row * inner) & (column < (row + 1) * inner)
    elif count & (count - 1) == 0:
        pick = (column & (count - 1)) == row
    else:
        pick = lax.rem(column, count) == row
    return dot(factor_t, jnp.where(pick, 1.0, 0.0).astype(BF16), 0, 0)


def expand(slow_t, fast_t):
    inner = fast_t.shape[0]
    width = slow_t.shape[0] * inner
    period = inner * 128 // math.gcd(inner, 128)
    if width % period:
        period = width
    fast = repeated(fast_t, period, 1, False)
    fast = jnp.concatenate([fast] * (width // period), 1)
    return (repeated(slow_t, width, inner, True) * fast).astype(BF16)


def halves(value):
    high = value.astype(BF16)
    return high, (value - high.astype(F32)).astype(BF16)


def sketch_kernel(place, slow, fast, right_slow, right_fast, slab, left, part, spans, *scratch):
    factors, (held, sems, slab_sems) = scratch[:4], scratch[4:]
    count, rank, rows = spans.shape
    heights = [rows // SPLIT] * (count * SPLIT)
    starts = [i * (rows // SPLIT) for i in range(count * SPLIT)]
    last = len(starts) - 1
    copies = [
        pltpu.make_async_copy(source, target, sems.at[i])
        for i, (source, target) in enumerate(zip((slow, fast, right_slow, right_fast), factors))
    ]
    pieces = [
        pltpu.make_async_copy(slab.at[pl.ds(start, height)], held.at[pl.ds(start, height)], slab_sems.at[i])
        for i, (start, height) in enumerate(zip(starts, heights))
    ]
    for copy in copies:
        copy.start()
    for i, copy in enumerate(pieces[:AHEAD]):
        copy.start(priority=i % 2)
    for copy in copies:
        copy.wait()
    omega = expand(factors[2][...], factors[3][...])
    psi = expand(factors[0][...], factors[1][...])
    value = None
    for i, (start, height) in enumerate(zip(starts, heights)):
        pieces[i].wait()
        if i + AHEAD <= last:
            pieces[i + AHEAD].start(priority=(i + AHEAD) % 2)
        block = held[start : start + height]
        term = dot(psi[:, start : start + height], block, 1, 0)
        value = term if value is None else value + term
        if i == last:
            chunk = left.shape[2]
            for c in range(left.shape[0]):
                left[c] = value[:, c * chunk : (c + 1) * chunk]
            high, low = halves(value)
            whole = dot(omega, high, 1, 1) + dot(omega, low, 1, 1)
            half = part.shape[1]
            bit = place[1]
            part[bit] = whole[:half]
            part[bit ^ 1, : rank - half] = whole[half:]
            part[bit ^ 1, rank - half :] = jnp.zeros((2 * half - rank, whole.shape[1]), F32)
        first = start // rows
        at = start - first * rows
        spans[place[0] ^ first, :, at : at + height] = dot(omega, block, 1, 1)


def half_of(rank):
    return -(-rank // 16) * 8


def sketches(place, snapshots, left_slow, left_fast, right_slow, right_fast, chunk, count):
    height, width = snapshots.shape
    rank_left, rank_right = left_slow.shape[0], right_slow.shape[0]
    factors = [f.T for f in (left_slow, left_fast, right_slow, right_fast)]
    rows = height // count
    inputs = [pltpu.with_memory_space_constraint(x, pltpu.HBM) for x in factors + [snapshots]]
    return pl.pallas_call(
        sketch_kernel,
        in_specs=[pl.BlockSpec(memory_space=pltpu.SMEM)] + [HBM] * 5,
        out_specs=(VMEM,) * 3,
        out_shape=(
            jax.ShapeDtypeStruct((width // chunk, rank_left, chunk), F32),
            jax.ShapeDtypeStruct((2, half_of(rank_right), rank_left), F32),
            jax.ShapeDtypeStruct((count, rank_right, rows), F32),
        ),
        scratch_shapes=[pltpu.VMEM(f.shape, BF16) for f in factors]
        + [
            pltpu.VMEM(snapshots.shape, BF16),
            pltpu.SemaphoreType.DMA((4,)),
            pltpu.SemaphoreType.DMA((count * SPLIT,)),
        ],
        compiler_params=pltpu.CompilerParams(vmem_limit_bytes=LIMIT),
        cost_estimate=pl.CostEstimate(
            flops=2 * (rank_left + rank_right) * height * width,
            bytes_accessed=2 * height * width,
            transcendentals=0,
        ),
        name="sketches",
    )(place, *inputs)


def row_of(tile, at):
    return jnp.broadcast_to(tile[at : at + 1, :], tile.shape)


def eliminate(gram):
    size = gram.shape[0]
    lane = lax.broadcasted_iota(jnp.int32, (8, size), 1)
    sub = lax.broadcasted_iota(jnp.int32, (8, size), 0)
    tiles = [gram[i : i + 8] for i in range(0, size, 8)]
    scaled = []
    for t in range(len(tiles)):
        k = 8 * t
        live = range(t, len(tiles))
        column = [
            {i: jnp.broadcast_to(tiles[i][:, k + j : k + j + 1], (8, size)) for i in live}
            for j in range(8)
        ]
        inside = (lane >= k) & (lane < k + 8)
        for i in live:
            tiles[i] = jnp.where(inside, 0.0, tiles[i])
        row = [row_of(tiles[t], j) for j in range(8)]
        weight = [None] * 8
        for p in range(0, 8, 2):
            q = p + 1
            a = row_of(column[p][t], p)
            b = row_of(column[q][t], p)
            c = row_of(column[q][t], q)
            det = a * c - b * b
            inverse = pl.reciprocal(det, approx=True)
            a, b, c = c * inverse, -b * inverse, a * inverse
            row[p] = jnp.where(lane == k + p, 1.0, row[p])
            row[q] = jnp.where(lane == k + q, 1.0, row[q])
            weight[p] = a * row[p] + b * row[q]
            weight[q] = b * row[p] + c * row[q]
            for j in range(q + 1, 8):
                f, g = row_of(column[j][t], p), row_of(column[j][t], q)
                u, v = a * f + b * g, b * f + c * g
                column[j] = {
                    i: column[j][i] - (column[p][i] * u + column[q][i] * v) for i in live
                }
                row[j] = row[j] - (
                    row_of(column[p][t], j) * weight[p] + row_of(column[q][t], j) * weight[q]
                )
            for i in live[1:]:
                tiles[i] = tiles[i] - (column[p][i] * weight[p] + column[q][i] * weight[q])
        held, out = row[0], weight[0]
        for j in range(1, 8):
            held = jnp.where(sub == j, row[j], held)
            out = jnp.where(sub == j, weight[j], out)
        tiles[t] = held
        scaled.append(out)
    return jnp.concatenate(tiles, 0), jnp.concatenate(scaled, 0)


def factor_kernel(low_first, mine, other, side, weight):
    first = low_first[0] == 0
    mine, other = mine[...], other[...]
    half = mine.shape[0]
    low, high = jnp.where(first, mine, other), jnp.where(first, other, mine)
    value = jnp.concatenate([low, high[: side.shape[0] - half]], 0) * SCALE
    size = value.shape[1]
    i = lax.broadcasted_iota(jnp.int32, (size, size), 0)
    j = lax.broadcasted_iota(jnp.int32, (size, size), 1)
    gram = dot(value, value, 0, 0, HIGHEST) + jnp.where(i == j, RIDGE * SCALE * SCALE, 0.0)
    lower, scaled = eliminate(gram)
    keep = (j >> 1) <= (i >> 1)
    side[...] = dot(value, jnp.where(keep, lower, 0.0), 1, 1, HIGHEST)
    weight[...] = jnp.where(keep, scaled, 0.0) * SCALE


def factor(low_first, mine, other, rank):
    size = mine.shape[1]
    return pl.pallas_call(
        factor_kernel,
        out_shape=(
            jax.ShapeDtypeStruct((rank, size), F32),
            jax.ShapeDtypeStruct((size, size), F32),
        ),
        in_specs=[pl.BlockSpec(memory_space=pltpu.SMEM)] + [VMEM] * 2,
        out_specs=(VMEM, VMEM),
        compiler_params=pltpu.CompilerParams(vmem_limit_bytes=LIMIT),
        cost_estimate=pl.CostEstimate(flops=COST, bytes_accessed=1000, transcendentals=0),
        name="factor",
    )(low_first, mine, other)


def pass_on(*refs):
    del refs


def paced(value, pace):
    if not pace:
        return value
    anywhere = pl.BlockSpec(memory_space=pl.ANY)
    return pl.pallas_call(
        pass_on,
        out_shape=jax.ShapeDtypeStruct(value.shape, value.dtype),
        in_specs=[anywhere],
        out_specs=anywhere,
        input_output_aliases={0: 0},
        compiler_params=pltpu.CompilerParams(vmem_limit_bytes=LIMIT),
        cost_estimate=pl.CostEstimate(flops=pace, bytes_accessed=0, transcendentals=0),
        name="paced",
    )(value)


def core_kernel(side, weight, kept, received, core):
    left = kept[...] + received[...]
    core[...] = dot(side[...], dot(weight[...], left, 1, 0, HIGHEST), 1, 0, HIGHEST)


def finish(side, weight, kept, received):
    return pl.pallas_call(
        core_kernel,
        out_shape=jax.ShapeDtypeStruct((side.shape[0], kept.shape[1]), F32),
        in_specs=[VMEM] * 4,
        out_specs=VMEM,
        compiler_params=pltpu.CompilerParams(vmem_limit_bytes=LIMIT),
        name="core",
    )(side, weight, kept, received)


def swap(value, axis, size, bit):
    return lax.ppermute(value, axis, [(i, i ^ bit) for i in range(size)])


def across(value, sizes, cell_bit, samp_bit):
    cells, samp = sizes
    pairs = [
        (i * samp + j, (i ^ cell_bit) * samp + (j ^ samp_bit ^ 1))
        for i in range(cells)
        for j in range(samp)
    ]
    return lax.ppermute(value, ("cells", "samp"), pairs)


def bits(size):
    return [1 << b for b in range(size.bit_length() - 1)]


def side_of(blocks, axis, bit, dim):
    mine = (lax.axis_index(axis) // bit) % 2
    return (
        lax.dynamic_index_in_dim(blocks, mine, dim, False),
        lax.dynamic_index_in_dim(blocks, 1 - mine, dim, False),
    )


def halving(blocks, axis, size, bit, dim):
    kept, sent = side_of(blocks, axis, bit, dim)
    return kept, swap(sent, axis, size, bit)


def build(sizes):
    cells, samp = sizes["cells"], sizes["samp"]

    def on_device(snapshots, left_slow, left_fast, right_slow, right_fast):
        height, width = snapshots.shape
        share = width // cells
        chunk = share if share % 128 == 0 else width
        me, cell = lax.axis_index("samp"), lax.axis_index("cells")
        flips = [me >> b for b in range(len(bits(samp)))] + [cell >> b for b in range(len(bits(cells)))]
        half = functools.reduce(lax.bitwise_xor, flips) & 1
        chunks, part, spans = sketches(
            jnp.stack([me, half]), snapshots, left_slow, left_fast, right_slow, right_fast, chunk, samp
        )
        if chunk != share:
            chunks = chunks[0].reshape(-1, cells, share).transpose(1, 0, 2)

        together = lax.optimization_barrier
        levels = bits(cells)
        left = chunks.reshape((2,) * len(levels) + chunks.shape[1:])

        sizes = (cells, samp)
        dims = levels[::-1]
        bit_of = {"y": levels[0], "z": levels[1], "Z": levels[2], "x": 2}
        far = spans[3] + swap(spans[2], "samp", samp, 1)
        near = (spans[0], swap(spans[1], "samp", samp, 1))
        now = {"l": left, "f": far}

        def tie(step, mine):
            for name in TIES.get(step, ""):
                if name in now:
                    mine, now[name] = together((mine, now[name]))
                if name == "f":
                    now["c"] = swap(now["f"], "samp", samp, 3)
                if name == "l" and True:
                    now["h1"] = halving(now["l"], "cells", cells, levels[0], len(levels) - 1)
                    now["1"] = sum(now["h1"])
                if False:
                    stay, leave = side_of(now["l"], "cells", levels[1], len(levels) - 2)
                    now["1"] = sum(halving(leave, "cells", cells, levels[0], len(levels) - 2))
                    now["s"] = sum(halving(stay, "cells", cells, levels[0], len(levels) - 2))
                if name == "1" and True:
                    now["h2"] = halving(now["1"], "cells", cells, levels[1], len(levels) - 2)
                    now["2"] = sum(now["h2"])
                if False:
                    now["2"] = now["s"] + swap(now["1"], "cells", cells, levels[1])
                if name == "2":
                    dim3 = len(levels) - 3
                    now["h3"] = halving(now["2"], "cells", cells, levels[2], len(levels) - 3)
            return mine

        part = tie(-1, part)
        mine = tie(0, part[0] + swap(part[1], "samp", samp, 1))
        for step, letter in enumerate(ORDER):
            if letter == "x":
                mine = mine + across(mine, sizes, 0, 2)
            else:
                mine = mine + across(mine, sizes, bit_of[letter], 0)
            mine = tie(step + 1, paced(mine, PACE[step]))
        for bit in levels[3:]:
            mine = mine + across(mine, sizes, bit, 0)
        other = swap(mine, "samp", samp, 1)
        tie(5, mine)
        if "1" in now and "2" not in now:
            tie_free = halving(now["1"], "cells", cells, levels[1], len(levels) - 2)
            now["2"] = sum(tie_free)
        if "h3" not in now:
            now["h3"] = halving(now["2"], "cells", cells, levels[2], len(levels) - 3)
        range_part = near[0] + near[1] + now["c"]
        if 6 in TIES:
            other, range_part = together((other, range_part))
        rest = now["h3"]
        for step, bit in enumerate(levels[3:]):
            rest = halving(sum(rest), "cells", cells, bit, len(levels) - 4 - step)
        if 7 in TIES:
            other, got = together((other, rest[1]))
            rest = (rest[0], got)
        side, weight = factor(half.reshape(1), mine, other, right_slow.shape[0])
        return (range_part.T, finish(side, weight, *rest))

    return on_device


def solution(mesh):
    placed = (P("cells", "samp"), P(None, "cells"), P(), P(None, "samp"), P())
    return jax.shard_map(
        build(mesh.shape),
        mesh=mesh,
        in_specs=placed,
        out_specs=(P(("cells", "samp"), None), P(None, ("samp", "cells"))),
        check_vma=False,
    )
```

time: 38.3 us -> 35.7 us (0.932)
  other arithmetic: 2.59 us -> 0.99 us
  starting transfers between devices: 13.6 us -> 12.8 us
    ppermute x11 -> x8, waiting for transfers between devices: 10 us -> 2.48 us  [swap(): return lax.ppermute(value, axis, [(i, i ^ bit) for i in range(size)])]
    ppermute x0 -> x4, waiting for transfers between devices: none -> 7.31 us  [across(): return lax.ppermute(value, ('cells', 'samp'), pairs)]
    ppermute x11 -> x8, starting transfers between devices: 13.6 us -> 7.31 us  [swap(): return lax.ppermute(value, axis, [(i, i ^ bit) for i in range(size)])]
    ppermute x0 -> x4, starting transfers between devices: none -> 5.54 us  [across(): return lax.ppermute(value, ('cells', 'samp'), pairs)]
    transpose x1 -> x0, other arithmetic: 0.79 us -> none  [on_device(): range_part = (spans[0] + swap(spans[1], 'samp', samp, 1) + crossing).T]
    concatenate x1 -> x0, other arithmetic: 0.78 us -> none  [sketches(): jnp.concatenate([jnp.pad(f, ((0, 0), (0, rank - f.shape[1]))) for f in fa...]
    pallas_call x2 -> x4, Pallas kernels: 9.58 us -> 9.71 us  [the longest x1 5.05 us: sketches(): pl.pallas_call(sketch_kernel, in_specs=[pl.BlockSpec(memory_space=pltpu.S...]
    add x7 -> x9, other arithmetic: 1.02 us -> 0.92 us  [the longest x1 0.8 us: on_device(): range_part = near[0] + near[1] + now['c']]
  transfers between devices with their start and end apart: 11 -> 12, of which waited for: 5 -> 7; matrix products, arithmetic and copies ran while one was open for 3% -> 3% of each run, Pallas kernels for 17% -> 13%
where the time goes in v4:
time: 35.7 us; the launch traced here: 35.4 us
  starting transfers between devices  12.8 us (36%)
  Pallas kernels  11 us (31%)
  waiting for transfers between devices  9.79 us (27%)
  other arithmetic  0.99 us (3%)
  between operations  0.71 us (2%)
    ppermute x4, waiting for transfers between devices, across(): return lax.ppermute(value, ('cells', 'samp'), pairs)  7.31 us
    ppermute x8, starting transfers between devices, swap(): return lax.ppermute(value, axis, [(i, i ^ bit) for i in range(size)])  7.31 us
    ppermute x4, starting transfers between devices, across(): return lax.ppermute(value, ('cells', 'samp'), pairs)  5.54 us
    pallas_call x1, Pallas kernels, sketches(): pl.pallas_call(sketch_kernel, in_specs=[pl.BlockSpec(memory_space=pltpu.S...  5.05 us
    pallas_call x1, Pallas kernels, factor(): pl.pallas_call(factor_kernel, out_shape=(jax.ShapeDtypeStruct((rank, size...  4.66 us
    ppermute x8, waiting for transfers between devices, swap(): return lax.ppermute(value, axis, [(i, i ^ bit) for i in range(size)])  2.48 us
    pallas_call x1, Pallas kernels, finish(): pl.pallas_call(core_kernel, out_shape=jax.ShapeDtypeStruct((side.shape[0]...  1.3 us
    add x1, other arithmetic, on_device(): range_part = near[0] + near[1] + now['c']  0.8 us
  transfers between devices with their start and end apart: 12, of which 7 were waited for; matrix products, arithmetic and copies ran while one was open for 3% of the time, Pallas kernels for 13%

profile of v4, /device:TPU:0, one launch (start us, length us, event | category | flops | bytes accessed | tf_op | source)
XLA Modules:
  0.0 35.4 jit_solution(13172328834509758509)
XLA Ops:
  0.6 0.1 pad_add_fusion.place
  0.7 5.1 %sketches.1 = (f32[8,120,128]{2,1,0:T(8,128)S(1)}, f32[2,80,120]{2,1,0:T(8,128)S(1)}, f32[4,150,512]{2,1,0:T(8,128)S(1)}) custom-call(s32[2]{0:T(128)S(1)} %pad_add_fusion.place, bf16[32,120]{1,0:T(8,128)(2,1)} %bitcast.40, bf16[64,120]{1,0:T(8,128)(2,1)} %bitcast.37, bf16[32,150]{1,0:T(8,128)(2,1)} %bitcast.38, bf16[32,150]{1,0:T(8,128)(2,1)} %bitcast.39, ...), custom_call_target="tpu_custom_call" | custom-call | flops 1132462080 | bytes 4194304 | tf_op jit(solution)/shard_map/sketches/pallas_call | solution.py:119
  5.8 0.5 %collective-permute-start = (f32[80,120]{1,0:T(8,128)S(1)}, f32[80,120]{1,0:T(8,128)S(1)}, u32[]{:S(2)}, u32[]{:S(2)}) collective-permute-start(f32[80,120]{1,0:T(8,128)S(1)} %slice_bitcast_fusion.2), channel_id=1, source_target_pairs={{0,1},{1,0},{2,3},{3,2},{4,5},{5,4},{6,7},{7,6},{8,9},{9,8},{10,11... | collective-permute-start | bytes 115208 | tf_op jit(solution)/shard_map/ppermute | solution.py:267
  6.4 0.1 collective-permute-start.1
  6.5 3.0 %collective-permute-start.4 = (f32[2,2,120,128]{3,2,1,0:T(8,128)S(1)}, f32[2,2,120,128]{3,2,1,0:T(8,128)S(1)}, u32[]{:S(2)}, u32[]{:S(2)}) collective-permute-start(f32[2,2,120,128]{3,2,1,0:T(8,128)S(1)} %dynamic-slice_bitcast_fusion), channel_id=1, source_target_pairs={{0,4},{4,0},{8,12},{12,8},{16,20},{20,16},{24,28},{28,24},{1,5},{5... | collective-permute-start | bytes 737288 | tf_op jit(solution)/shard_map/ppermute | solution.py:267
  9.5 0.0 collective-permute-done
  9.5 0.0 collective-permute-done.1
  9.6 1.1 %collective-permute-start.2 = (f32[80,120]{1,0:T(8,128)S(1)}, f32[80,120]{1,0:T(8,128)S(1)}, u32[]{:S(2)}, u32[]{:S(2)}) collective-permute-start(f32[80,120]{1,0:T(8,128)S(1)} %bitcast_add_fusion.4), channel_id=1, source_target_pairs={{0,3},{1,2},{2,1},{3,0},{4,7},{5,6},{6,5},{7,4},{8,11},{9,10},{10,... | collective-permute-start | bytes 115208 | tf_op jit(solution)/shard_map/ppermute | solution.py:277
  10.7 2.8 %collective-permute-done.2 = f32[80,120]{1,0:T(8,128)S(1)} collective-permute-done((f32[80,120]{1,0:T(8,128)S(1)}, f32[80,120]{1,0:T(8,128)S(1)}, u32[]{:S(2)}, u32[]{:S(2)}) %collective-permute-start.2) | collective-permute-done | bytes 38432 | tf_op jit(solution)/shard_map/ppermute | solution.py:277
  13.5 1.3 %collective-permute-start.3 = (f32[80,120]{1,0:T(8,128)S(1)}, f32[80,120]{1,0:T(8,128)S(1)}, u32[]{:S(2)}, u32[]{:S(2)}) collective-permute-start(f32[80,120]{1,0:T(8,128)S(1)} %add.69), channel_id=1, source_target_pairs={{0,9},{1,8},{2,11},{3,10},{4,13},{5,12},{6,15},{7,14},{8,1},{9,0},... | collective-permute-start | bytes 115208 | tf_op jit(solution)/shard_map/ppermute | solution.py:277
  14.8 0.9 %collective-permute-done.4 = f32[2,2,120,128]{3,2,1,0:T(8,128)S(1)} collective-permute-done((f32[2,2,120,128]{3,2,1,0:T(8,128)S(1)}, f32[2,2,120,128]{3,2,1,0:T(8,128)S(1)}, u32[]{:S(2)}, u32[]{:S(2)}) %collective-permute-start.4) | collective-permute-done | bytes 245792 | tf_op jit(solution)/shard_map/ppermute | solution.py:267
  15.7 1.3 %collective-permute-done.3 = f32[80,120]{1,0:T(8,128)S(1)} collective-permute-done((f32[80,120]{1,0:T(8,128)S(1)}, f32[80,120]{1,0:T(8,128)S(1)}, u32[]{:S(2)}, u32[]{:S(2)}) %collective-permute-start.3) | collective-permute-done | bytes 38432 | tf_op jit(solution)/shard_map/ppermute | solution.py:277
  17.0 1.4 %collective-permute-start.6 = (f32[2,120,128]{2,1,0:T(8,128)S(1)}, f32[2,120,128]{2,1,0:T(8,128)S(1)}, u32[]{:S(2)}, u32[]{:S(2)}) collective-permute-start(f32[2,120,128]{2,1,0:T(8,128)S(1)} %dynamic-slice_bitcast_fusion.1), channel_id=1, source_target_pairs={{0,8},{4,12},{8,0},{12,4},{16,24},{20,28},{24,16},{28,20},{1,9},{5... | collective-permute-start | bytes 368648 | tf_op jit(solution)/shard_map/ppermute | solution.py:267
  18.5 0.8 %collective-permute-start.5 = (f32[80,120]{1,0:T(8,128)S(1)}, f32[80,120]{1,0:T(8,128)S(1)}, u32[]{:S(2)}, u32[]{:S(2)}) collective-permute-start(f32[80,120]{1,0:T(8,128)S(1)} %add.70), channel_id=1, source_target_pairs={{0,5},{1,4},{2,7},{3,6},{4,1},{5,0},{6,3},{7,2},{8,13},{9,12},{10,... | collective-permute-start | bytes 115208 | tf_op jit(solution)/shard_map/ppermute | solution.py:277
  19.3 0.2 collective-permute-start.9
  19.5 1.5 %collective-permute-start.10 = (f32[150,512]{1,0:T(8,128)S(1)}, f32[150,512]{1,0:T(8,128)S(1)}, u32[]{:S(2)}, u32[]{:S(2)}) collective-permute-start(f32[150,512]{1,0:T(8,128)S(1)} %bitcast_add_fusion.1), channel_id=1, source_target_pairs={{0,3},{1,2},{2,1},{3,0},{4,7},{5,6},{6,5},{7,4},{8,11},{9,10},{10,... | collective-permute-start | bytes 921608 | tf_op jit(solution)/shard_map/ppermute | solution.py:267
  20.9 1.3 %collective-permute-done.5 = f32[80,120]{1,0:T(8,128)S(1)} collective-permute-done((f32[80,120]{1,0:T(8,128)S(1)}, f32[80,120]{1,0:T(8,128)S(1)}, u32[]{:S(2)}, u32[]{:S(2)}) %collective-permute-start.5) | collective-permute-done | bytes 38432 | tf_op jit(solution)/shard_map/ppermute | solution.py:277
  22.2 0.3 collective-permute-done.6
  22.5 2.2 %collective-permute-start.7 = (f32[80,120]{1,0:T(8,128)S(1)}, f32[80,120]{1,0:T(8,128)S(1)}, u32[]{:S(2)}, u32[]{:S(2)}) collective-permute-start(f32[80,120]{1,0:T(8,128)S(1)} %paced.2), channel_id=1, source_target_pairs={{0,17},{1,16},{2,19},{3,18},{4,21},{5,20},{6,23},{7,22},{8,25},{9,... | collective-permute-start | bytes 115208 | tf_op jit(solution)/shard_map/ppermute | solution.py:277
  24.8 0.4 %collective-permute-start.11 = (f32[120,128]{1,0:T(8,128)S(1)}, f32[120,128]{1,0:T(8,128)S(1)}, u32[]{:S(2)}, u32[]{:S(2)}) collective-permute-start(f32[120,128]{1,0:T(8,128)S(1)} %get-tuple-element.34), channel_id=1, source_target_pairs={{0,16},{4,20},{8,24},{12,28},{16,0},{20,4},{24,8},{28,12},{1,17},{... | collective-permute-start | bytes 184328 | tf_op jit(solution)/shard_map/ppermute | solution.py:267
  25.2 2.0 %collective-permute-done.7 = f32[80,120]{1,0:T(8,128)S(1)} collective-permute-done((f32[80,120]{1,0:T(8,128)S(1)}, f32[80,120]{1,0:T(8,128)S(1)}, u32[]{:S(2)}, u32[]{:S(2)}) %collective-permute-start.7) | collective-permute-done | bytes 38432 | tf_op jit(solution)/shard_map/ppermute | solution.py:277
  27.2 0.2 collective-permute-start.8
  27.4 0.0 collective-permute-done.9
  27.4 1.3 %collective-permute-done.10 = f32[150,512]{1,0:T(8,128)S(1)} collective-permute-done((f32[150,512]{1,0:T(8,128)S(1)}, f32[150,512]{1,0:T(8,128)S(1)}, u32[]{:S(2)}, u32[]{:S(2)}) %collective-permute-start.10) | collective-permute-done | bytes 307232 | tf_op jit(solution)/shard_map/ppermute | solution.py:267
  28.7 0.8 %fusion = f32[150,512]{1,0:T(8,128)} fusion(f32[150,512]{1,0:T(8,128)S(1)} %collective-permute-done.10, f32[150,512]{1,0:T(8,128)S(1)} %collective-permute-done.9, f32[4,150,512]{2,1,0:T(8,128)S(1)} %get-tuple-element.20), kind=kLoop, calls=%fused_computation.1 | loop fusion | flops 153600 | bytes 1228800 | tf_op jit(solution)/shard_map/add | solution.py:364
  29.5 0.0 collective-permute-done.8.other
  29.5 4.7 %factor.1 = (f32[150,120]{1,0:T(8,128)S(1)}, f32[120,120]{1,0:T(8,128)S(1)}) custom-call(s32[1]{0:T(128)} %bitcast.1.low_first, f32[80,120]{1,0:T(8,128)S(1)} %paced.3.mine, f32[80,120]{1,0:T(8,128)S(1)} %collective-permute-done.8.other), custom_call_target="tpu_custom_call" | custom-call | flops 10000 | bytes 1000 | tf_op jit(solution)/shard_map/factor/pallas_call | solution.py:216
  34.1 0.0 collective-permute-done.11.received
  34.1 1.3 %core.1 = f32[150,128]{1,0:T(8,128)} custom-call(f32[150,120]{1,0:T(8,128)S(1)} %get-tuple-element.29.side, f32[120,120]{1,0:T(8,128)S(1)} %get-tuple-element.30.weight, f32[120,128]{1,0:T(8,128)S(1)} %get-tuple-element.35.kept, f32[120,128]{1,0:T(8,128)S(1)} %collective-permute-done.11.received), custom_call_target="tpu_custom_call" | custom-call | tf_op jit(solution)/shard_map/core/pallas_call | solution.py:256
  (15 shorter events, 0.2 us)
Async XLA Ops:
  5.8 3.7 %collective-permute-start = (f32[80,120]{1,0:T(8,128)S(1)}, f32[80,120]{1,0:T(8,128)S(1)}, u32[]{:S(2)}, u32[]{:S(2)}) collective-permute-start(f32[80,120]{1,0:T(8,128)S(1)} %slice_bitcast_fusion.2), channel_id=1, source_target_pairs={{0,1},{1,0},{2,3},{3,2},{4,5},{5,4},{6,7},{7,6},{8,9},{9,8},{10,11... | collective-permute-start | bytes 115208 | tf_op jit(solution)/shard_map/ppermute | solution.py:267
  6.4 3.2 %collective-permute-start.1 = (f32[150,512]{1,0:T(8,128)S(1)}, f32[150,512]{1,0:T(8,128)S(1)}, u32[]{:S(2)}, u32[]{:S(2)}) collective-permute-start(f32[150,512]{1,0:T(8,128)S(1)} %get-tuple-element.33), channel_id=1, source_target_pairs={{0,1},{1,0},{2,3},{3,2},{4,5},{5,4},{6,7},{7,6},{8,9},{9,8},{10,11... | collective-permute-start | bytes 921608 | tf_op jit(solution)/shard_map/ppermute | solution.py:267
  6.5 9.2 %collective-permute-start.4 = (f32[2,2,120,128]{3,2,1,0:T(8,128)S(1)}, f32[2,2,120,128]{3,2,1,0:T(8,128)S(1)}, u32[]{:S(2)}, u32[]{:S(2)}) collective-permute-start(f32[2,2,120,128]{3,2,1,0:T(8,128)S(1)} %dynamic-slice_bitcast_fusion), channel_id=1, source_target_pairs={{0,4},{4,0},{8,12},{12,8},{16,20},{20,16},{24,28},{28,24},{1,5},{5... | collective-permute-start | bytes 737288 | tf_op jit(solution)/shard_map/ppermute | solution.py:267
  9.6 3.9 %collective-permute-start.2 = (f32[80,120]{1,0:T(8,128)S(1)}, f32[80,120]{1,0:T(8,128)S(1)}, u32[]{:S(2)}, u32[]{:S(2)}) collective-permute-start(f32[80,120]{1,0:T(8,128)S(1)} %bitcast_add_fusion.4), channel_id=1, source_target_pairs={{0,3},{1,2},{2,1},{3,0},{4,7},{5,6},{6,5},{7,4},{8,11},{9,10},{10,... | collective-permute-start | bytes 115208 | tf_op jit(solution)/shard_map/ppermute | solution.py:277
  13.5 3.5 %collective-permute-start.3 = (f32[80,120]{1,0:T(8,128)S(1)}, f32[80,120]{1,0:T(8,128)S(1)}, u32[]{:S(2)}, u32[]{:S(2)}) collective-permute-start(f32[80,120]{1,0:T(8,128)S(1)} %add.69), channel_id=1, source_target_pairs={{0,9},{1,8},{2,11},{3,10},{4,13},{5,12},{6,15},{7,14},{8,1},{9,0},... | collective-permute-start | bytes 115208 | tf_op jit(solution)/shard_map/ppermute | solution.py:277
  17.0 5.5 %collective-permute-start.6 = (f32[2,120,128]{2,1,0:T(8,128)S(1)}, f32[2,120,128]{2,1,0:T(8,128)S(1)}, u32[]{:S(2)}, u32[]{:S(2)}) collective-permute-start(f32[2,120,128]{2,1,0:T(8,128)S(1)} %dynamic-slice_bitcast_fusion.1), channel_id=1, source_target_pairs={{0,8},{4,12},{8,0},{12,4},{16,24},{20,28},{24,16},{28,20},{1,9},{5... | collective-permute-start | bytes 368648 | tf_op jit(solution)/shard_map/ppermute | solution.py:267
  18.5 3.7 %collective-permute-start.5 = (f32[80,120]{1,0:T(8,128)S(1)}, f32[80,120]{1,0:T(8,128)S(1)}, u32[]{:S(2)}, u32[]{:S(2)}) collective-permute-start(f32[80,120]{1,0:T(8,128)S(1)} %add.70), channel_id=1, source_target_pairs={{0,5},{1,4},{2,7},{3,6},{4,1},{5,0},{6,3},{7,2},{8,13},{9,12},{10,... | collective-permute-start | bytes 115208 | tf_op jit(solution)/shard_map/ppermute | solution.py:277
  19.3 8.1 %collective-permute-start.9 = (f32[150,512]{1,0:T(8,128)S(1)}, f32[150,512]{1,0:T(8,128)S(1)}, u32[]{:S(2)}, u32[]{:S(2)}) collective-permute-start(f32[150,512]{1,0:T(8,128)S(1)} %get-tuple-element.32), channel_id=1, source_target_pairs={{0,1},{1,0},{2,3},{3,2},{4,5},{5,4},{6,7},{7,6},{8,9},{9,8},{10,11... | collective-permute-start | bytes 921608 | tf_op jit(solution)/shard_map/ppermute | solution.py:267
  19.5 9.2 %collective-permute-start.10 = (f32[150,512]{1,0:T(8,128)S(1)}, f32[150,512]{1,0:T(8,128)S(1)}, u32[]{:S(2)}, u32[]{:S(2)}) collective-permute-start(f32[150,512]{1,0:T(8,128)S(1)} %bitcast_add_fusion.1), channel_id=1, source_target_pairs={{0,3},{1,2},{2,1},{3,0},{4,7},{5,6},{6,5},{7,4},{8,11},{9,10},{10,... | collective-permute-start | bytes 921608 | tf_op jit(solution)/shard_map/ppermute | solution.py:267
  22.5 4.6 %collective-permute-start.7 = (f32[80,120]{1,0:T(8,128)S(1)}, f32[80,120]{1,0:T(8,128)S(1)}, u32[]{:S(2)}, u32[]{:S(2)}) collective-permute-start(f32[80,120]{1,0:T(8,128)S(1)} %paced.2), channel_id=1, source_target_pairs={{0,17},{1,16},{2,19},{3,18},{4,21},{5,20},{6,23},{7,22},{8,25},{9,... | collective-permute-start | bytes 115208 | tf_op jit(solution)/shard_map/ppermute | solution.py:277
  24.8 9.4 %collective-permute-start.11 = (f32[120,128]{1,0:T(8,128)S(1)}, f32[120,128]{1,0:T(8,128)S(1)}, u32[]{:S(2)}, u32[]{:S(2)}) collective-permute-start(f32[120,128]{1,0:T(8,128)S(1)} %get-tuple-element.34), channel_id=1, source_target_pairs={{0,16},{4,20},{8,24},{12,28},{16,0},{20,4},{24,8},{28,12},{1,17},{... | collective-permute-start | bytes 184328 | tf_op jit(solution)/shard_map/ppermute | solution.py:267
  27.2 2.3 %collective-permute-start.8 = (f32[80,120]{1,0:T(8,128)S(1)}, f32[80,120]{1,0:T(8,128)S(1)}, u32[]{:S(2)}, u32[]{:S(2)}) collective-permute-start(f32[80,120]{1,0:T(8,128)S(1)} %paced.3.mine), channel_id=1, source_target_pairs={{0,1},{1,0},{2,3},{3,2},{4,5},{5,4},{6,7},{7,6},{8,9},{9,8},{10,11... | collective-permute-start | bytes 115208 | tf_op jit(solution)/shard_map/ppermute | solution.py:267

commit v5 on v4

--- a/solution.py
+++ b/solution.py
@@ -16,7 +16,7 @@
 COST = 10000
 PACE = (0, 0, 10**8, 10**8)
 ORDER = "xzyZ"
-TIES = {-1: "l", 0: "f", 2: "1", 3: "2", 6: ""}
+TIES = {-1: "l", 0: "fg", 2: "1", 3: "2", 6: ""}
 SPLIT = 1
 VMEM = pl.BlockSpec(memory_space=pltpu.VMEM)
 HBM = pl.BlockSpec(memory_space=pltpu.HBM)
@@ -207,7 +207,7 @@
     gram = dot(value, value, 0, 0, HIGHEST) + jnp.where(i == j, RIDGE * SCALE * SCALE, 0.0)
     lower, scaled = eliminate(gram)
     keep = (j >> 1) <= (i >> 1)
-    side[...] = dot(value, jnp.where(keep, lower, 0.0), 1, 1, HIGHEST)
+    side[...] = dot3(value, jnp.where(keep, lower, 0.0), 1, 1)
     weight[...] = jnp.where(keep, scaled, 0.0) * SCALE
 
 
@@ -247,9 +247,15 @@
     )(value)
 
 
+def dot3(a, b, a_dim, b_dim):
+    (a_high, a_low), (b_high, b_low) = halves(a), halves(b)
+    small = dot(a_high, b_low, a_dim, b_dim) + dot(a_low, b_high, a_dim, b_dim)
+    return dot(a_high, b_high, a_dim, b_dim) + small
+
+
 def core_kernel(side, weight, kept, received, core):
     left = kept[...] + received[...]
-    core[...] = dot(side[...], dot(weight[...], left, 1, 0, HIGHEST), 1, 0, HIGHEST)
+    core[...] = dot3(side[...], dot3(weight[...], left, 1, 0), 1, 0)
 
 
 def finish(side, weight, kept, received):
@@ -325,7 +331,8 @@
             for name in TIES.get(step, ""):
                 if name in now:
                     mine, now[name] = together((mine, now[name]))
-                if name == "f":
+                if name == "g":
+                    mine, now["f"] = together((mine, now["f"]))
                     now["c"] = swap(now["f"], "samp", samp, 3)
                 if name == "l" and True:
                     now["h1"] = halving(now["l"], "cells", cells, levels[0], len(levels) - 1)

time: 35.7 us -> 35.1 us (0.983)
  Pallas kernels: 11 us -> 10.5 us
where the time goes in v5:
time: 35.1 us; the launch traced here: 34.9 us
  starting transfers between devices  12.8 us (36%)
  Pallas kernels  10.5 us (30%)
  waiting for transfers between devices  9.79 us (28%)
  other arithmetic  0.99 us (3%)
  between operations  0.71 us (2%)
    ppermute x4, waiting for transfers between devices, across(): return lax.ppermute(value, ('cells', 'samp'), pairs)  7.31 us
    ppermute x8, starting transfers between devices, swap(): return lax.ppermute(value, axis, [(i, i ^ bit) for i in range(size)])  7.31 us
    ppermute x4, starting transfers between devices, across(): return lax.ppermute(value, ('cells', 'samp'), pairs)  5.54 us
    pallas_call x1, Pallas kernels, sketches(): pl.pallas_call(sketch_kernel, in_specs=[pl.BlockSpec(memory_space=pltpu.S...  5.05 us
    pallas_call x1, Pallas kernels, factor(): pl.pallas_call(factor_kernel, out_shape=(jax.ShapeDtypeStruct((rank, size...  4.4 us
    ppermute x8, waiting for transfers between devices, swap(): return lax.ppermute(value, axis, [(i, i ^ bit) for i in range(size)])  2.48 us
    pallas_call x1, Pallas kernels, finish(): pl.pallas_call(core_kernel, out_shape=jax.ShapeDtypeStruct((side.shape[0]...  1.01 us
    add x1, other arithmetic, on_device(): range_part = near[0] + near[1] + now['c']  0.8 us
  transfers between devices with their start and end apart: 12, of which 7 were waited for; matrix products, arithmetic and copies ran while one was open for 3% of the time, Pallas kernels for 13%

profile of v5, /device:TPU:0, one launch (start us, length us, event | category | flops | bytes accessed | tf_op | source)
XLA Modules:
  0.0 34.9 jit_solution(8448784733015035761)
XLA Ops:
  0.6 0.1 pad_add_fusion.place
  0.7 5.1 %sketches.1 = (f32[8,120,128]{2,1,0:T(8,128)S(1)}, f32[2,80,120]{2,1,0:T(8,128)S(1)}, f32[4,150,512]{2,1,0:T(8,128)S(1)}) custom-call(s32[2]{0:T(128)S(1)} %pad_add_fusion.place, bf16[32,120]{1,0:T(8,128)(2,1)} %bitcast.40, bf16[64,120]{1,0:T(8,128)(2,1)} %bitcast.37, bf16[32,150]{1,0:T(8,128)(2,1)} %bitcast.38, bf16[32,150]{1,0:T(8,128)(2,1)} %bitcast.39, ...), custom_call_target="tpu_custom_call" | custom-call | flops 1132462080 | bytes 4194304 | tf_op jit(solution)/shard_map/sketches/pallas_call | solution.py:119
  5.8 0.5 %collective-permute-start = (f32[80,120]{1,0:T(8,128)S(1)}, f32[80,120]{1,0:T(8,128)S(1)}, u32[]{:S(2)}, u32[]{:S(2)}) collective-permute-start(f32[80,120]{1,0:T(8,128)S(1)} %slice_bitcast_fusion.2), channel_id=1, source_target_pairs={{0,1},{1,0},{2,3},{3,2},{4,5},{5,4},{6,7},{7,6},{8,9},{9,8},{10,11... | collective-permute-start | bytes 115208 | tf_op jit(solution)/shard_map/ppermute | solution.py:273
  6.4 0.1 collective-permute-start.1
  6.5 3.0 %collective-permute-start.4 = (f32[2,2,120,128]{3,2,1,0:T(8,128)S(1)}, f32[2,2,120,128]{3,2,1,0:T(8,128)S(1)}, u32[]{:S(2)}, u32[]{:S(2)}) collective-permute-start(f32[2,2,120,128]{3,2,1,0:T(8,128)S(1)} %dynamic-slice_bitcast_fusion), channel_id=1, source_target_pairs={{0,4},{4,0},{8,12},{12,8},{16,20},{20,16},{24,28},{28,24},{1,5},{5... | collective-permute-start | bytes 737288 | tf_op jit(solution)/shard_map/ppermute | solution.py:273
  9.5 0.0 collective-permute-done
  9.5 0.0 collective-permute-done.1
  9.6 1.1 %collective-permute-start.2 = (f32[80,120]{1,0:T(8,128)S(1)}, f32[80,120]{1,0:T(8,128)S(1)}, u32[]{:S(2)}, u32[]{:S(2)}) collective-permute-start(f32[80,120]{1,0:T(8,128)S(1)} %bitcast_add_fusion.4), channel_id=1, source_target_pairs={{0,3},{1,2},{2,1},{3,0},{4,7},{5,6},{6,5},{7,4},{8,11},{9,10},{10,... | collective-permute-start | bytes 115208 | tf_op jit(solution)/shard_map/ppermute | solution.py:283
  10.7 2.8 %collective-permute-done.2 = f32[80,120]{1,0:T(8,128)S(1)} collective-permute-done((f32[80,120]{1,0:T(8,128)S(1)}, f32[80,120]{1,0:T(8,128)S(1)}, u32[]{:S(2)}, u32[]{:S(2)}) %collective-permute-start.2) | collective-permute-done | bytes 38432 | tf_op jit(solution)/shard_map/ppermute | solution.py:283
  13.5 1.3 %collective-permute-start.3 = (f32[80,120]{1,0:T(8,128)S(1)}, f32[80,120]{1,0:T(8,128)S(1)}, u32[]{:S(2)}, u32[]{:S(2)}) collective-permute-start(f32[80,120]{1,0:T(8,128)S(1)} %add.69), channel_id=1, source_target_pairs={{0,9},{1,8},{2,11},{3,10},{4,13},{5,12},{6,15},{7,14},{8,1},{9,0},... | collective-permute-start | bytes 115208 | tf_op jit(solution)/shard_map/ppermute | solution.py:283
  14.8 0.9 %collective-permute-done.4 = f32[2,2,120,128]{3,2,1,0:T(8,128)S(1)} collective-permute-done((f32[2,2,120,128]{3,2,1,0:T(8,128)S(1)}, f32[2,2,120,128]{3,2,1,0:T(8,128)S(1)}, u32[]{:S(2)}, u32[]{:S(2)}) %collective-permute-start.4) | collective-permute-done | bytes 245792 | tf_op jit(solution)/shard_map/ppermute | solution.py:273
  15.7 1.3 %collective-permute-done.3 = f32[80,120]{1,0:T(8,128)S(1)} collective-permute-done((f32[80,120]{1,0:T(8,128)S(1)}, f32[80,120]{1,0:T(8,128)S(1)}, u32[]{:S(2)}, u32[]{:S(2)}) %collective-permute-start.3) | collective-permute-done | bytes 38432 | tf_op jit(solution)/shard_map/ppermute | solution.py:283
  17.0 1.4 %collective-permute-start.6 = (f32[2,120,128]{2,1,0:T(8,128)S(1)}, f32[2,120,128]{2,1,0:T(8,128)S(1)}, u32[]{:S(2)}, u32[]{:S(2)}) collective-permute-start(f32[2,120,128]{2,1,0:T(8,128)S(1)} %dynamic-slice_bitcast_fusion.1), channel_id=1, source_target_pairs={{0,8},{4,12},{8,0},{12,4},{16,24},{20,28},{24,16},{28,20},{1,9},{5... | collective-permute-start | bytes 368648 | tf_op jit(solution)/shard_map/ppermute | solution.py:273
  18.5 0.8 %collective-permute-start.5 = (f32[80,120]{1,0:T(8,128)S(1)}, f32[80,120]{1,0:T(8,128)S(1)}, u32[]{:S(2)}, u32[]{:S(2)}) collective-permute-start(f32[80,120]{1,0:T(8,128)S(1)} %add.70), channel_id=1, source_target_pairs={{0,5},{1,4},{2,7},{3,6},{4,1},{5,0},{6,3},{7,2},{8,13},{9,12},{10,... | collective-permute-start | bytes 115208 | tf_op jit(solution)/shard_map/ppermute | solution.py:283
  19.3 0.2 collective-permute-start.9
  19.5 1.5 %collective-permute-start.10 = (f32[150,512]{1,0:T(8,128)S(1)}, f32[150,512]{1,0:T(8,128)S(1)}, u32[]{:S(2)}, u32[]{:S(2)}) collective-permute-start(f32[150,512]{1,0:T(8,128)S(1)} %bitcast_add_fusion.1), channel_id=1, source_target_pairs={{0,3},{1,2},{2,1},{3,0},{4,7},{5,6},{6,5},{7,4},{8,11},{9,10},{10,... | collective-permute-start | bytes 921608 | tf_op jit(solution)/shard_map/ppermute | solution.py:273
  20.9 1.3 %collective-permute-done.5 = f32[80,120]{1,0:T(8,128)S(1)} collective-permute-done((f32[80,120]{1,0:T(8,128)S(1)}, f32[80,120]{1,0:T(8,128)S(1)}, u32[]{:S(2)}, u32[]{:S(2)}) %collective-permute-start.5) | collective-permute-done | bytes 38432 | tf_op jit(solution)/shard_map/ppermute | solution.py:283
  22.2 0.3 collective-permute-done.6
  22.5 2.2 %collective-permute-start.7 = (f32[80,120]{1,0:T(8,128)S(1)}, f32[80,120]{1,0:T(8,128)S(1)}, u32[]{:S(2)}, u32[]{:S(2)}) collective-permute-start(f32[80,120]{1,0:T(8,128)S(1)} %paced.2), channel_id=1, source_target_pairs={{0,17},{1,16},{2,19},{3,18},{4,21},{5,20},{6,23},{7,22},{8,25},{9,... | collective-permute-start | bytes 115208 | tf_op jit(solution)/shard_map/ppermute | solution.py:283
  24.8 0.4 %collective-permute-start.11 = (f32[120,128]{1,0:T(8,128)S(1)}, f32[120,128]{1,0:T(8,128)S(1)}, u32[]{:S(2)}, u32[]{:S(2)}) collective-permute-start(f32[120,128]{1,0:T(8,128)S(1)} %get-tuple-element.34), channel_id=1, source_target_pairs={{0,16},{4,20},{8,24},{12,28},{16,0},{20,4},{24,8},{28,12},{1,17},{... | collective-permute-start | bytes 184328 | tf_op jit(solution)/shard_map/ppermute | solution.py:273
  25.2 2.0 %collective-permute-done.7 = f32[80,120]{1,0:T(8,128)S(1)} collective-permute-done((f32[80,120]{1,0:T(8,128)S(1)}, f32[80,120]{1,0:T(8,128)S(1)}, u32[]{:S(2)}, u32[]{:S(2)}) %collective-permute-start.7) | collective-permute-done | bytes 38432 | tf_op jit(solution)/shard_map/ppermute | solution.py:283
  27.2 0.2 collective-permute-start.8
  27.4 0.0 collective-permute-done.9
  27.4 1.3 %collective-permute-done.10 = f32[150,512]{1,0:T(8,128)S(1)} collective-permute-done((f32[150,512]{1,0:T(8,128)S(1)}, f32[150,512]{1,0:T(8,128)S(1)}, u32[]{:S(2)}, u32[]{:S(2)}) %collective-permute-start.10) | collective-permute-done | bytes 307232 | tf_op jit(solution)/shard_map/ppermute | solution.py:273
  28.7 0.8 %fusion = f32[150,512]{1,0:T(8,128)} fusion(f32[150,512]{1,0:T(8,128)S(1)} %collective-permute-done.10, f32[150,512]{1,0:T(8,128)S(1)} %collective-permute-done.9, f32[4,150,512]{2,1,0:T(8,128)S(1)} %get-tuple-element.20), kind=kLoop, calls=%fused_computation.1 | loop fusion | flops 153600 | bytes 1228800 | tf_op jit(solution)/shard_map/add | solution.py:371
  29.5 0.0 collective-permute-done.8.other
  29.5 4.4 %factor.1 = (f32[150,120]{1,0:T(8,128)S(1)}, f32[120,120]{1,0:T(8,128)S(1)}) custom-call(s32[1]{0:T(128)} %bitcast.1.low_first, f32[80,120]{1,0:T(8,128)S(1)} %paced.3.mine, f32[80,120]{1,0:T(8,128)S(1)} %collective-permute-done.8.other), custom_call_target="tpu_custom_call" | custom-call | flops 10000 | bytes 1000 | tf_op jit(solution)/shard_map/factor/pallas_call | solution.py:216
  33.9 0.0 collective-permute-done.11.received
  33.9 1.0 %core.1 = f32[150,128]{1,0:T(8,128)} custom-call(f32[150,120]{1,0:T(8,128)S(1)} %get-tuple-element.29.side, f32[120,120]{1,0:T(8,128)S(1)} %get-tuple-element.30.weight, f32[120,128]{1,0:T(8,128)S(1)} %get-tuple-element.35.kept, f32[120,128]{1,0:T(8,128)S(1)} %collective-permute-done.11.received), custom_call_target="tpu_custom_call" | custom-call | tf_op jit(solution)/shard_map/core/pallas_call | solution.py:262
  (15 shorter events, 0.2 us)
Async XLA Ops:
  5.8 3.7 %collective-permute-start = (f32[80,120]{1,0:T(8,128)S(1)}, f32[80,120]{1,0:T(8,128)S(1)}, u32[]{:S(2)}, u32[]{:S(2)}) collective-permute-start(f32[80,120]{1,0:T(8,128)S(1)} %slice_bitcast_fusion.2), channel_id=1, source_target_pairs={{0,1},{1,0},{2,3},{3,2},{4,5},{5,4},{6,7},{7,6},{8,9},{9,8},{10,11... | collective-permute-start | bytes 115208 | tf_op jit(solution)/shard_map/ppermute | solution.py:273
  6.4 3.2 %collective-permute-start.1 = (f32[150,512]{1,0:T(8,128)S(1)}, f32[150,512]{1,0:T(8,128)S(1)}, u32[]{:S(2)}, u32[]{:S(2)}) collective-permute-start(f32[150,512]{1,0:T(8,128)S(1)} %get-tuple-element.33), channel_id=1, source_target_pairs={{0,1},{1,0},{2,3},{3,2},{4,5},{5,4},{6,7},{7,6},{8,9},{9,8},{10,11... | collective-permute-start | bytes 921608 | tf_op jit(solution)/shard_map/ppermute | solution.py:273
  6.5 9.2 %collective-permute-start.4 = (f32[2,2,120,128]{3,2,1,0:T(8,128)S(1)}, f32[2,2,120,128]{3,2,1,0:T(8,128)S(1)}, u32[]{:S(2)}, u32[]{:S(2)}) collective-permute-start(f32[2,2,120,128]{3,2,1,0:T(8,128)S(1)} %dynamic-slice_bitcast_fusion), channel_id=1, source_target_pairs={{0,4},{4,0},{8,12},{12,8},{16,20},{20,16},{24,28},{28,24},{1,5},{5... | collective-permute-start | bytes 737288 | tf_op jit(solution)/shard_map/ppermute | solution.py:273
  9.6 3.9 %collective-permute-start.2 = (f32[80,120]{1,0:T(8,128)S(1)}, f32[80,120]{1,0:T(8,128)S(1)}, u32[]{:S(2)}, u32[]{:S(2)}) collective-permute-start(f32[80,120]{1,0:T(8,128)S(1)} %bitcast_add_fusion.4), channel_id=1, source_target_pairs={{0,3},{1,2},{2,1},{3,0},{4,7},{5,6},{6,5},{7,4},{8,11},{9,10},{10,... | collective-permute-start | bytes 115208 | tf_op jit(solution)/shard_map/ppermute | solution.py:283
  13.5 3.5 %collective-permute-start.3 = (f32[80,120]{1,0:T(8,128)S(1)}, f32[80,120]{1,0:T(8,128)S(1)}, u32[]{:S(2)}, u32[]{:S(2)}) collective-permute-start(f32[80,120]{1,0:T(8,128)S(1)} %add.69), channel_id=1, source_target_pairs={{0,9},{1,8},{2,11},{3,10},{4,13},{5,12},{6,15},{7,14},{8,1},{9,0},... | collective-permute-start | bytes 115208 | tf_op jit(solution)/shard_map/ppermute | solution.py:283
  17.0 5.5 %collective-permute-start.6 = (f32[2,120,128]{2,1,0:T(8,128)S(1)}, f32[2,120,128]{2,1,0:T(8,128)S(1)}, u32[]{:S(2)}, u32[]{:S(2)}) collective-permute-start(f32[2,120,128]{2,1,0:T(8,128)S(1)} %dynamic-slice_bitcast_fusion.1), channel_id=1, source_target_pairs={{0,8},{4,12},{8,0},{12,4},{16,24},{20,28},{24,16},{28,20},{1,9},{5... | collective-permute-start | bytes 368648 | tf_op jit(solution)/shard_map/ppermute | solution.py:273
  18.5 3.7 %collective-permute-start.5 = (f32[80,120]{1,0:T(8,128)S(1)}, f32[80,120]{1,0:T(8,128)S(1)}, u32[]{:S(2)}, u32[]{:S(2)}) collective-permute-start(f32[80,120]{1,0:T(8,128)S(1)} %add.70), channel_id=1, source_target_pairs={{0,5},{1,4},{2,7},{3,6},{4,1},{5,0},{6,3},{7,2},{8,13},{9,12},{10,... | collective-permute-start | bytes 115208 | tf_op jit(solution)/shard_map/ppermute | solution.py:283
  19.3 8.1 %collective-permute-start.9 = (f32[150,512]{1,0:T(8,128)S(1)}, f32[150,512]{1,0:T(8,128)S(1)}, u32[]{:S(2)}, u32[]{:S(2)}) collective-permute-start(f32[150,512]{1,0:T(8,128)S(1)} %get-tuple-element.32), channel_id=1, source_target_pairs={{0,1},{1,0},{2,3},{3,2},{4,5},{5,4},{6,7},{7,6},{8,9},{9,8},{10,11... | collective-permute-start | bytes 921608 | tf_op jit(solution)/shard_map/ppermute | solution.py:273
  19.5 9.2 %collective-permute-start.10 = (f32[150,512]{1,0:T(8,128)S(1)}, f32[150,512]{1,0:T(8,128)S(1)}, u32[]{:S(2)}, u32[]{:S(2)}) collective-permute-start(f32[150,512]{1,0:T(8,128)S(1)} %bitcast_add_fusion.1), channel_id=1, source_target_pairs={{0,3},{1,2},{2,1},{3,0},{4,7},{5,6},{6,5},{7,4},{8,11},{9,10},{10,... | collective-permute-start | bytes 921608 | tf_op jit(solution)/shard_map/ppermute | solution.py:273
  22.5 4.6 %collective-permute-start.7 = (f32[80,120]{1,0:T(8,128)S(1)}, f32[80,120]{1,0:T(8,128)S(1)}, u32[]{:S(2)}, u32[]{:S(2)}) collective-permute-start(f32[80,120]{1,0:T(8,128)S(1)} %paced.2), channel_id=1, source_target_pairs={{0,17},{1,16},{2,19},{3,18},{4,21},{5,20},{6,23},{7,22},{8,25},{9,... | collective-permute-start | bytes 115208 | tf_op jit(solution)/shard_map/ppermute | solution.py:283
  24.8 9.1 %collective-permute-start.11 = (f32[120,128]{1,0:T(8,128)S(1)}, f32[120,128]{1,0:T(8,128)S(1)}, u32[]{:S(2)}, u32[]{:S(2)}) collective-permute-start(f32[120,128]{1,0:T(8,128)S(1)} %get-tuple-element.34), channel_id=1, source_target_pairs={{0,16},{4,20},{8,24},{12,28},{16,0},{20,4},{24,8},{28,12},{1,17},{... | collective-permute-start | bytes 184328 | tf_op jit(solution)/shard_map/ppermute | solution.py:273
  27.2 2.3 %collective-permute-start.8 = (f32[80,120]{1,0:T(8,128)S(1)}, f32[80,120]{1,0:T(8,128)S(1)}, u32[]{:S(2)}, u32[]{:S(2)}) collective-permute-start(f32[80,120]{1,0:T(8,128)S(1)} %paced.3.mine), channel_id=1, source_target_pairs={{0,1},{1,0},{2,3},{3,2},{4,5},{5,4},{6,7},{7,6},{8,9},{9,8},{10,11... | collective-permute-start | bytes 115208 | tf_op jit(solution)/shard_map/ppermute | solution.py:273

commit v6 on v5

--- a/solution.py
+++ b/solution.py
@@ -13,15 +13,9 @@
 HIGHEST = lax.Precision.HIGHEST
 SCALE = 2.0**-10
 RIDGE = 0.5
-COST = 10000
-PACE = (0, 0, 10**8, 10**8)
-ORDER = "xzyZ"
-TIES = {-1: "l", 0: "fg", 2: "1", 3: "2", 6: ""}
-SPLIT = 1
 VMEM = pl.BlockSpec(memory_space=pltpu.VMEM)
 HBM = pl.BlockSpec(memory_space=pltpu.HBM)
 LIMIT = 16 * 2**20
-LARGE = 32 * 2**20
 AHEAD = 2
 
 
@@ -63,16 +57,14 @@
 def sketch_kernel(place, slow, fast, right_slow, right_fast, slab, left, part, spans, *scratch):
     factors, (held, sems, slab_sems) = scratch[:4], scratch[4:]
     count, rank, rows = spans.shape
-    heights = [rows // SPLIT] * (count * SPLIT)
-    starts = [i * (rows // SPLIT) for i in range(count * SPLIT)]
-    last = len(starts) - 1
+    starts = [i * rows for i in range(count)]
     copies = [
         pltpu.make_async_copy(source, target, sems.at[i])
         for i, (source, target) in enumerate(zip((slow, fast, right_slow, right_fast), factors))
     ]
     pieces = [
-        pltpu.make_async_copy(slab.at[pl.ds(start, height)], held.at[pl.ds(start, height)], slab_sems.at[i])
-        for i, (start, height) in enumerate(zip(starts, heights))
+        pltpu.make_async_copy(slab.at[pl.ds(start, rows)], held.at[pl.ds(start, rows)], slab_sems.at[i])
+        for i, start in enumerate(starts)
     ]
     for copy in copies:
         copy.start()
@@ -83,14 +75,14 @@
     omega = expand(factors[2][...], factors[3][...])
     psi = expand(factors[0][...], factors[1][...])
     value = None
-    for i, (start, height) in enumerate(zip(starts, heights)):
+    for i, start in enumerate(starts):
         pieces[i].wait()
-        if i + AHEAD <= last:
+        if i + AHEAD < count:
             pieces[i + AHEAD].start(priority=(i + AHEAD) % 2)
-        block = held[start : start + height]
-        term = dot(psi[:, start : start + height], block, 1, 0)
+        block = held[start : start + rows]
+        term = dot(psi[:, start : start + rows], block, 1, 0)
         value = term if value is None else value + term
-        if i == last:
+        if i == count - 1:
             chunk = left.shape[2]
             for c in range(left.shape[0]):
                 left[c] = value[:, c * chunk : (c + 1) * chunk]
@@ -101,9 +93,7 @@
             part[bit] = whole[:half]
             part[bit ^ 1, : rank - half] = whole[half:]
             part[bit ^ 1, rank - half :] = jnp.zeros((2 * half - rank, whole.shape[1]), F32)
-        first = start // rows
-        at = start - first * rows
-        spans[place[0] ^ first, :, at : at + height] = dot(omega, block, 1, 1)
+        spans[place[0] ^ i] = dot(omega, block, 1, 1)
 
 
 def half_of(rank):
@@ -129,7 +119,7 @@
         + [
             pltpu.VMEM(snapshots.shape, BF16),
             pltpu.SemaphoreType.DMA((4,)),
-            pltpu.SemaphoreType.DMA((count * SPLIT,)),
+            pltpu.SemaphoreType.DMA((count,)),
         ],
         compiler_params=pltpu.CompilerParams(vmem_limit_bytes=LIMIT),
         cost_estimate=pl.CostEstimate(
@@ -222,7 +212,7 @@
         in_specs=[pl.BlockSpec(memory_space=pltpu.SMEM)] + [VMEM] * 2,
         out_specs=(VMEM, VMEM),
         compiler_params=pltpu.CompilerParams(vmem_limit_bytes=LIMIT),
-        cost_estimate=pl.CostEstimate(flops=COST, bytes_accessed=1000, transcendentals=0),
+        cost_estimate=pl.CostEstimate(flops=10**4, bytes_accessed=1000, transcendentals=0),
         name="factor",
     )(low_first, mine, other)
 
@@ -232,8 +222,6 @@
 
 
 def paced(value, pace):
-    if not pace:
-        return value
     anywhere = pl.BlockSpec(memory_space=pl.ANY)
     return pl.pallas_call(
         pass_on,
@@ -317,68 +305,33 @@
             chunks = chunks[0].reshape(-1, cells, share).transpose(1, 0, 2)
 
         together = lax.optimization_barrier
-        levels = bits(cells)
-        left = chunks.reshape((2,) * len(levels) + chunks.shape[1:])
-
-        sizes = (cells, samp)
-        dims = levels[::-1]
-        bit_of = {"y": levels[0], "z": levels[1], "Z": levels[2], "x": 2}
+        sizes, levels = (cells, samp), bits(cells)
+        depth = len(levels)
+        left = chunks.reshape((2,) * depth + chunks.shape[1:])
+        part, left = together((part, left))
+        stay, leave = side_of(left, "cells", levels[1], depth - 2)
+        leave = sum(halving(leave, "cells", cells, levels[0], depth - 2))
+        stay = sum(halving(stay, "cells", cells, levels[0], depth - 2))
+        mine = part[0] + swap(part[1], "samp", samp, 1)
         far = spans[3] + swap(spans[2], "samp", samp, 1)
-        near = (spans[0], swap(spans[1], "samp", samp, 1))
-        now = {"l": left, "f": far}
-
-        def tie(step, mine):
-            for name in TIES.get(step, ""):
-                if name in now:
-                    mine, now[name] = together((mine, now[name]))
-                if name == "g":
-                    mine, now["f"] = together((mine, now["f"]))
-                    now["c"] = swap(now["f"], "samp", samp, 3)
-                if name == "l" and True:
-                    now["h1"] = halving(now["l"], "cells", cells, levels[0], len(levels) - 1)
-                    now["1"] = sum(now["h1"])
-                if False:
-                    stay, leave = side_of(now["l"], "cells", levels[1], len(levels) - 2)
-                    now["1"] = sum(halving(leave, "cells", cells, levels[0], len(levels) - 2))
-                    now["s"] = sum(halving(stay, "cells", cells, levels[0], len(levels) - 2))
-                if name == "1" and True:
-                    now["h2"] = halving(now["1"], "cells", cells, levels[1], len(levels) - 2)
-                    now["2"] = sum(now["h2"])
-                if False:
-                    now["2"] = now["s"] + swap(now["1"], "cells", cells, levels[1])
-                if name == "2":
-                    dim3 = len(levels) - 3
-                    now["h3"] = halving(now["2"], "cells", cells, levels[2], len(levels) - 3)
-            return mine
-
-        part = tie(-1, part)
-        mine = tie(0, part[0] + swap(part[1], "samp", samp, 1))
-        for step, letter in enumerate(ORDER):
-            if letter == "x":
-                mine = mine + across(mine, sizes, 0, 2)
-            else:
-                mine = mine + across(mine, sizes, bit_of[letter], 0)
-            mine = tie(step + 1, paced(mine, PACE[step]))
-        for bit in levels[3:]:
+        mine, far = together((mine, far))
+        near = spans[0] + swap(spans[1], "samp", samp, 1)
+        crossing = swap(far, "samp", samp, 3)
+        mine = mine + across(mine, sizes, 0, 2)
+        mine, leave = together((mine, leave))
+        received = swap(leave, "cells", cells, levels[1])
+        mine = paced(mine + across(mine, sizes, levels[1], 0), 10**9)
+        mine = mine + across(mine, sizes, levels[0], 0)
+        mine, left = together((mine, stay + received))
+        kept, received = halving(left, "cells", cells, levels[2], depth - 3)
+        mine = paced(mine + across(mine, sizes, levels[2], 0), 10**8)
+        for step, bit in enumerate(levels[3:]):
             mine = mine + across(mine, sizes, bit, 0)
+            kept, received = halving(kept + received, "cells", cells, bit, depth - 4 - step)
         other = swap(mine, "samp", samp, 1)
-        tie(5, mine)
-        if "1" in now and "2" not in now:
-            tie_free = halving(now["1"], "cells", cells, levels[1], len(levels) - 2)
-            now["2"] = sum(tie_free)
-        if "h3" not in now:
-            now["h3"] = halving(now["2"], "cells", cells, levels[2], len(levels) - 3)
-        range_part = near[0] + near[1] + now["c"]
-        if 6 in TIES:
-            other, range_part = together((other, range_part))
-        rest = now["h3"]
-        for step, bit in enumerate(levels[3:]):
-            rest = halving(sum(rest), "cells", cells, bit, len(levels) - 4 - step)
-        if 7 in TIES:
-            other, got = together((other, rest[1]))
-            rest = (rest[0], got)
+        other, range_part = together((other, near + crossing))
         side, weight = factor(half.reshape(1), mine, other, right_slow.shape[0])
-        return (range_part.T, finish(side, weight, *rest))
+        return (range_part.T, finish(side, weight, kept, received))
 
     return on_device
 

time: 35.1 us -> 34.7 us (0.989)
  waiting for transfers between devices: 9.79 us -> 8.38 us
  starting transfers between devices: 12.8 us -> 13.8 us
    ppermute x4, waiting for transfers between devices: 7.31 us -> 4.64 us  [across(): return lax.ppermute(value, ('cells', 'samp'), pairs)]
    ppermute x8 -> x9, waiting for transfers between devices: 2.48 us -> 3.74 us  [swap(): return lax.ppermute(value, axis, [(i, i ^ bit) for i in range(size)])]
    ppermute x8 -> x9, starting transfers between devices: 7.31 us -> 8.03 us  [swap(): return lax.ppermute(value, axis, [(i, i ^ bit) for i in range(size)])]
  transfers between devices with their start and end apart: 12 -> 13, of which waited for: 7 -> 7; matrix products, arithmetic and copies ran while one was open for 3% -> 3% of each run, Pallas kernels for 13% -> 13%
where the time goes in v6:
time: 34.7 us; the launch traced here: 34.4 us
  starting transfers between devices  13.8 us (40%)
  Pallas kernels  10.5 us (30%)
  waiting for transfers between devices  8.38 us (24%)
  other arithmetic  0.99 us (3%)
  between operations  0.73 us (2%)
    ppermute x9, starting transfers between devices, swap(): return lax.ppermute(value, axis, [(i, i ^ bit) for i in range(size)])  8.03 us
    ppermute x4, starting transfers between devices, across(): return lax.ppermute(value, ('cells', 'samp'), pairs)  5.77 us
    pallas_call x1, Pallas kernels, sketches(): pl.pallas_call(sketch_kernel, in_specs=[pl.BlockSpec(memory_space=pltpu.S...  5.05 us
    ppermute x4, waiting for transfers between devices, across(): return lax.ppermute(value, ('cells', 'samp'), pairs)  4.64 us
    pallas_call x1, Pallas kernels, factor(): pl.pallas_call(factor_kernel, out_shape=(jax.ShapeDtypeStruct((rank, size...  4.4 us
    ppermute x9, waiting for transfers between devices, swap(): return lax.ppermute(value, axis, [(i, i ^ bit) for i in range(size)])  3.74 us
    pallas_call x1, Pallas kernels, finish(): pl.pallas_call(core_kernel, out_shape=jax.ShapeDtypeStruct((side.shape[0]...  1.01 us
    add x1, other arithmetic, on_device(): other, range_part = together((other, near + crossing))  0.8 us
  transfers between devices with their start and end apart: 13, of which 7 were waited for; matrix products, arithmetic and copies ran while one was open for 3% of the time, Pallas kernels for 13%

profile of v6, /device:TPU:0, one launch (start us, length us, event | category | flops | bytes accessed | tf_op | source)
XLA Modules:
  0.0 34.4 jit_solution(1226665591379312334)
XLA Ops:
  0.6 0.1 pad_add_fusion.place
  0.7 5.1 %sketches.1 = (f32[8,120,128]{2,1,0:T(8,128)S(1)}, f32[2,80,120]{2,1,0:T(8,128)S(1)}, f32[4,150,512]{2,1,0:T(8,128)S(1)}) custom-call(s32[2]{0:T(128)S(1)} %pad_add_fusion.place, bf16[32,120]{1,0:T(8,128)(2,1)} %bitcast.43, bf16[64,120]{1,0:T(8,128)(2,1)} %bitcast.40, bf16[32,150]{1,0:T(8,128)(2,1)} %bitcast.41, bf16[32,150]{1,0:T(8,128)(2,1)} %bitcast.42, ...), custom_call_target="tpu_custom_call" | custom-call | flops 1132462080 | bytes 4194304 | tf_op jit(solution)/shard_map/sketches/pallas_call | solution.py:109
  5.8 0.5 %collective-permute-start = (f32[80,120]{1,0:T(8,128)S(1)}, f32[80,120]{1,0:T(8,128)S(1)}, u32[]{:S(2)}, u32[]{:S(2)}) collective-permute-start(f32[80,120]{1,0:T(8,128)S(1)} %slice_bitcast_fusion.2), channel_id=1, source_target_pairs={{0,1},{1,0},{2,3},{3,2},{4,5},{5,4},{6,7},{7,6},{8,9},{9,8},{10,11... | collective-permute-start | bytes 115208 | tf_op jit(solution)/shard_map/ppermute | solution.py:261
  6.4 0.1 collective-permute-start.1
  6.5 3.0 %collective-permute-start.3 = (f32[2,120,128]{2,1,0:T(8,128)S(1)}, f32[2,120,128]{2,1,0:T(8,128)S(1)}, u32[]{:S(2)}, u32[]{:S(2)}) collective-permute-start(f32[2,120,128]{2,1,0:T(8,128)S(1)} %get-tuple-element.35), channel_id=1, source_target_pairs={{0,4},{4,0},{8,12},{12,8},{16,20},{20,16},{24,28},{28,24},{1,5},{5... | collective-permute-start | bytes 368648 | tf_op jit(solution)/shard_map/ppermute | solution.py:261
  9.5 0.0 collective-permute-done
  9.5 0.0 collective-permute-done.1
  9.6 1.1 %collective-permute-start.2 = (f32[80,120]{1,0:T(8,128)S(1)}, f32[80,120]{1,0:T(8,128)S(1)}, u32[]{:S(2)}, u32[]{:S(2)}) collective-permute-start(f32[80,120]{1,0:T(8,128)S(1)} %bitcast_add_fusion.4), channel_id=1, source_target_pairs={{0,3},{1,2},{2,1},{3,0},{4,7},{5,6},{6,5},{7,4},{8,11},{9,10},{10,... | collective-permute-start | bytes 115208 | tf_op jit(solution)/shard_map/ppermute | solution.py:271
  10.7 2.4 %collective-permute-done.3 = f32[2,120,128]{2,1,0:T(8,128)S(1)} collective-permute-done((f32[2,120,128]{2,1,0:T(8,128)S(1)}, f32[2,120,128]{2,1,0:T(8,128)S(1)}, u32[]{:S(2)}, u32[]{:S(2)}) %collective-permute-start.3) | collective-permute-done | bytes 122912 | tf_op jit(solution)/shard_map/ppermute | solution.py:261
  13.1 0.4 %collective-permute-done.2 = f32[80,120]{1,0:T(8,128)S(1)} collective-permute-done((f32[80,120]{1,0:T(8,128)S(1)}, f32[80,120]{1,0:T(8,128)S(1)}, u32[]{:S(2)}, u32[]{:S(2)}) %collective-permute-start.2) | collective-permute-done | bytes 38432 | tf_op jit(solution)/shard_map/ppermute | solution.py:271
  13.5 1.2 %collective-permute-start.4 = (f32[80,120]{1,0:T(8,128)S(1)}, f32[80,120]{1,0:T(8,128)S(1)}, u32[]{:S(2)}, u32[]{:S(2)}) collective-permute-start(f32[80,120]{1,0:T(8,128)S(1)} %add.95), channel_id=1, source_target_pairs={{0,9},{1,8},{2,11},{3,10},{4,13},{5,12},{6,15},{7,14},{8,1},{9,0},... | collective-permute-start | bytes 115208 | tf_op jit(solution)/shard_map/ppermute | solution.py:271
  14.7 1.4 %collective-permute-start.6 = (f32[2,120,128]{2,1,0:T(8,128)S(1)}, f32[2,120,128]{2,1,0:T(8,128)S(1)}, u32[]{:S(2)}, u32[]{:S(2)}) collective-permute-start(f32[2,120,128]{2,1,0:T(8,128)S(1)} %get-tuple-element.34), channel_id=1, source_target_pairs={{0,4},{4,0},{8,12},{12,8},{16,20},{20,16},{24,28},{28,24},{1,5},{5... | collective-permute-start | bytes 368648 | tf_op jit(solution)/shard_map/ppermute | solution.py:261
  16.1 0.5 %collective-permute-start.7 = (f32[2,120,128]{2,1,0:T(8,128)S(1)}, f32[2,120,128]{2,1,0:T(8,128)S(1)}, u32[]{:S(2)}, u32[]{:S(2)}) collective-permute-start(f32[2,120,128]{2,1,0:T(8,128)S(1)} %bitcast_add_fusion.3), channel_id=1, source_target_pairs={{0,8},{4,12},{8,0},{12,4},{16,24},{20,28},{24,16},{28,20},{1,9},{5... | collective-permute-start | bytes 368648 | tf_op jit(solution)/shard_map/ppermute | solution.py:261
  16.6 0.5 %collective-permute-done.4 = f32[80,120]{1,0:T(8,128)S(1)} collective-permute-done((f32[80,120]{1,0:T(8,128)S(1)}, f32[80,120]{1,0:T(8,128)S(1)}, u32[]{:S(2)}, u32[]{:S(2)}) %collective-permute-start.4) | collective-permute-done | bytes 38432 | tf_op jit(solution)/shard_map/ppermute | solution.py:271
  17.1 1.4 %collective-permute-start.5 = (f32[80,120]{1,0:T(8,128)S(1)}, f32[80,120]{1,0:T(8,128)S(1)}, u32[]{:S(2)}, u32[]{:S(2)}) collective-permute-start(f32[80,120]{1,0:T(8,128)S(1)} %paced.2), channel_id=1, source_target_pairs={{0,5},{1,4},{2,7},{3,6},{4,1},{5,0},{6,3},{7,2},{8,13},{9,12},{10,... | collective-permute-start | bytes 115208 | tf_op jit(solution)/shard_map/ppermute | solution.py:271
  18.5 0.4 %collective-permute-start.10 = (f32[150,512]{1,0:T(8,128)S(1)}, f32[150,512]{1,0:T(8,128)S(1)}, u32[]{:S(2)}, u32[]{:S(2)}) collective-permute-start(f32[150,512]{1,0:T(8,128)S(1)} %get-tuple-element.32), channel_id=1, source_target_pairs={{0,1},{1,0},{2,3},{3,2},{4,5},{5,4},{6,7},{7,6},{8,9},{9,8},{10,11... | collective-permute-start | bytes 921608 | tf_op jit(solution)/shard_map/ppermute | solution.py:261
  18.9 1.2 %collective-permute-start.11 = (f32[150,512]{1,0:T(8,128)S(1)}, f32[150,512]{1,0:T(8,128)S(1)}, u32[]{:S(2)}, u32[]{:S(2)}) collective-permute-start(f32[150,512]{1,0:T(8,128)S(1)} %bitcast_add_fusion.1), channel_id=1, source_target_pairs={{0,3},{1,2},{2,1},{3,0},{4,7},{5,6},{6,5},{7,4},{8,11},{9,10},{10,... | collective-permute-start | bytes 921608 | tf_op jit(solution)/shard_map/ppermute | solution.py:261
  20.1 1.0 %collective-permute-done.5 = f32[80,120]{1,0:T(8,128)S(1)} collective-permute-done((f32[80,120]{1,0:T(8,128)S(1)}, f32[80,120]{1,0:T(8,128)S(1)}, u32[]{:S(2)}, u32[]{:S(2)}) %collective-permute-start.5) | collective-permute-done | bytes 38432 | tf_op jit(solution)/shard_map/ppermute | solution.py:271
  21.1 0.0 collective-permute-done.6
  21.1 0.5 %collective-permute-done.7 = f32[2,120,128]{2,1,0:T(8,128)S(1)} collective-permute-done((f32[2,120,128]{2,1,0:T(8,128)S(1)}, f32[2,120,128]{2,1,0:T(8,128)S(1)}, u32[]{:S(2)}, u32[]{:S(2)}) %collective-permute-start.7) | collective-permute-done | bytes 122912 | tf_op jit(solution)/shard_map/ppermute | solution.py:261
  21.6 2.0 %collective-permute-start.8 = (f32[80,120]{1,0:T(8,128)S(1)}, f32[80,120]{1,0:T(8,128)S(1)}, u32[]{:S(2)}, u32[]{:S(2)}) collective-permute-start(f32[80,120]{1,0:T(8,128)S(1)} %add.103), channel_id=1, source_target_pairs={{0,17},{1,16},{2,19},{3,18},{4,21},{5,20},{6,23},{7,22},{8,25},{9,... | collective-permute-start | bytes 115208 | tf_op jit(solution)/shard_map/ppermute | solution.py:271
  23.7 0.7 %collective-permute-start.12 = (f32[120,128]{1,0:T(8,128)S(1)}, f32[120,128]{1,0:T(8,128)S(1)}, u32[]{:S(2)}, u32[]{:S(2)}) collective-permute-start(f32[120,128]{1,0:T(8,128)S(1)} %get-tuple-element.36), channel_id=1, source_target_pairs={{0,16},{4,20},{8,24},{12,28},{16,0},{20,4},{24,8},{28,12},{1,17},{... | collective-permute-start | bytes 184328 | tf_op jit(solution)/shard_map/ppermute | solution.py:261
  24.4 2.8 %collective-permute-done.8 = f32[80,120]{1,0:T(8,128)S(1)} collective-permute-done((f32[80,120]{1,0:T(8,128)S(1)}, f32[80,120]{1,0:T(8,128)S(1)}, u32[]{:S(2)}, u32[]{:S(2)}) %collective-permute-start.8) | collective-permute-done | bytes 38432 | tf_op jit(solution)/shard_map/ppermute | solution.py:271
  27.2 0.2 collective-permute-start.9
  27.4 0.0 collective-permute-done.10
  27.4 0.9 %collective-permute-done.11 = f32[150,512]{1,0:T(8,128)S(1)} collective-permute-done((f32[150,512]{1,0:T(8,128)S(1)}, f32[150,512]{1,0:T(8,128)S(1)}, u32[]{:S(2)}, u32[]{:S(2)}) %collective-permute-start.11) | collective-permute-done | bytes 307232 | tf_op jit(solution)/shard_map/ppermute | solution.py:261
  28.2 0.8 %fusion = f32[150,512]{1,0:T(8,128)} fusion(f32[150,512]{1,0:T(8,128)S(1)} %collective-permute-done.11, f32[150,512]{1,0:T(8,128)S(1)} %collective-permute-done.10, f32[4,150,512]{2,1,0:T(8,128)S(1)} %get-tuple-element.20), kind=kLoop, calls=%fused_computation.1 | loop fusion | flops 153600 | bytes 1228800 | tf_op jit(solution)/shard_map/add | solution.py:332
  29.0 0.0 collective-permute-done.9.other
  29.0 4.4 %factor.1 = (f32[150,120]{1,0:T(8,128)S(1)}, f32[120,120]{1,0:T(8,128)S(1)}) custom-call(s32[1]{0:T(128)} %bitcast.1.low_first, f32[80,120]{1,0:T(8,128)S(1)} %paced.3.mine, f32[80,120]{1,0:T(8,128)S(1)} %collective-permute-done.9.other), custom_call_target="tpu_custom_call" | custom-call | flops 10000 | bytes 1000 | tf_op jit(solution)/shard_map/factor/pallas_call | solution.py:206
  33.4 0.0 collective-permute-done.12.received
  33.4 1.0 %core.1 = f32[150,128]{1,0:T(8,128)} custom-call(f32[150,120]{1,0:T(8,128)S(1)} %get-tuple-element.29.side, f32[120,120]{1,0:T(8,128)S(1)} %get-tuple-element.30.weight, f32[120,128]{1,0:T(8,128)S(1)} %get-tuple-element.37.kept, f32[120,128]{1,0:T(8,128)S(1)} %collective-permute-done.12.received), custom_call_target="tpu_custom_call" | custom-call | tf_op jit(solution)/shard_map/core/pallas_call | solution.py:250
  (14 shorter events, 0.2 us)
Async XLA Ops:
  5.8 3.7 %collective-permute-start = (f32[80,120]{1,0:T(8,128)S(1)}, f32[80,120]{1,0:T(8,128)S(1)}, u32[]{:S(2)}, u32[]{:S(2)}) collective-permute-start(f32[80,120]{1,0:T(8,128)S(1)} %slice_bitcast_fusion.2), channel_id=1, source_target_pairs={{0,1},{1,0},{2,3},{3,2},{4,5},{5,4},{6,7},{7,6},{8,9},{9,8},{10,11... | collective-permute-start | bytes 115208 | tf_op jit(solution)/shard_map/ppermute | solution.py:261
  6.4 3.2 %collective-permute-start.1 = (f32[150,512]{1,0:T(8,128)S(1)}, f32[150,512]{1,0:T(8,128)S(1)}, u32[]{:S(2)}, u32[]{:S(2)}) collective-permute-start(f32[150,512]{1,0:T(8,128)S(1)} %get-tuple-element.33), channel_id=1, source_target_pairs={{0,1},{1,0},{2,3},{3,2},{4,5},{5,4},{6,7},{7,6},{8,9},{9,8},{10,11... | collective-permute-start | bytes 921608 | tf_op jit(solution)/shard_map/ppermute | solution.py:261
  6.5 6.6 %collective-permute-start.3 = (f32[2,120,128]{2,1,0:T(8,128)S(1)}, f32[2,120,128]{2,1,0:T(8,128)S(1)}, u32[]{:S(2)}, u32[]{:S(2)}) collective-permute-start(f32[2,120,128]{2,1,0:T(8,128)S(1)} %get-tuple-element.35), channel_id=1, source_target_pairs={{0,4},{4,0},{8,12},{12,8},{16,20},{20,16},{24,28},{28,24},{1,5},{5... | collective-permute-start | bytes 368648 | tf_op jit(solution)/shard_map/ppermute | solution.py:261
  9.6 3.9 %collective-permute-start.2 = (f32[80,120]{1,0:T(8,128)S(1)}, f32[80,120]{1,0:T(8,128)S(1)}, u32[]{:S(2)}, u32[]{:S(2)}) collective-permute-start(f32[80,120]{1,0:T(8,128)S(1)} %bitcast_add_fusion.4), channel_id=1, source_target_pairs={{0,3},{1,2},{2,1},{3,0},{4,7},{5,6},{6,5},{7,4},{8,11},{9,10},{10,... | collective-permute-start | bytes 115208 | tf_op jit(solution)/shard_map/ppermute | solution.py:271
  13.5 3.6 %collective-permute-start.4 = (f32[80,120]{1,0:T(8,128)S(1)}, f32[80,120]{1,0:T(8,128)S(1)}, u32[]{:S(2)}, u32[]{:S(2)}) collective-permute-start(f32[80,120]{1,0:T(8,128)S(1)} %add.95), channel_id=1, source_target_pairs={{0,9},{1,8},{2,11},{3,10},{4,13},{5,12},{6,15},{7,14},{8,1},{9,0},... | collective-permute-start | bytes 115208 | tf_op jit(solution)/shard_map/ppermute | solution.py:271
  14.7 6.4 %collective-permute-start.6 = (f32[2,120,128]{2,1,0:T(8,128)S(1)}, f32[2,120,128]{2,1,0:T(8,128)S(1)}, u32[]{:S(2)}, u32[]{:S(2)}) collective-permute-start(f32[2,120,128]{2,1,0:T(8,128)S(1)} %get-tuple-element.34), channel_id=1, source_target_pairs={{0,4},{4,0},{8,12},{12,8},{16,20},{20,16},{24,28},{28,24},{1,5},{5... | collective-permute-start | bytes 368648 | tf_op jit(solution)/shard_map/ppermute | solution.py:261
  16.1 5.5 %collective-permute-start.7 = (f32[2,120,128]{2,1,0:T(8,128)S(1)}, f32[2,120,128]{2,1,0:T(8,128)S(1)}, u32[]{:S(2)}, u32[]{:S(2)}) collective-permute-start(f32[2,120,128]{2,1,0:T(8,128)S(1)} %bitcast_add_fusion.3), channel_id=1, source_target_pairs={{0,8},{4,12},{8,0},{12,4},{16,24},{20,28},{24,16},{28,20},{1,9},{5... | collective-permute-start | bytes 368648 | tf_op jit(solution)/shard_map/ppermute | solution.py:261
  17.1 4.0 %collective-permute-start.5 = (f32[80,120]{1,0:T(8,128)S(1)}, f32[80,120]{1,0:T(8,128)S(1)}, u32[]{:S(2)}, u32[]{:S(2)}) collective-permute-start(f32[80,120]{1,0:T(8,128)S(1)} %paced.2), channel_id=1, source_target_pairs={{0,5},{1,4},{2,7},{3,6},{4,1},{5,0},{6,3},{7,2},{8,13},{9,12},{10,... | collective-permute-start | bytes 115208 | tf_op jit(solution)/shard_map/ppermute | solution.py:271
  18.5 8.9 %collective-permute-start.10 = (f32[150,512]{1,0:T(8,128)S(1)}, f32[150,512]{1,0:T(8,128)S(1)}, u32[]{:S(2)}, u32[]{:S(2)}) collective-permute-start(f32[150,512]{1,0:T(8,128)S(1)} %get-tuple-element.32), channel_id=1, source_target_pairs={{0,1},{1,0},{2,3},{3,2},{4,5},{5,4},{6,7},{7,6},{8,9},{9,8},{10,11... | collective-permute-start | bytes 921608 | tf_op jit(solution)/shard_map/ppermute | solution.py:261
  18.9 9.4 %collective-permute-start.11 = (f32[150,512]{1,0:T(8,128)S(1)}, f32[150,512]{1,0:T(8,128)S(1)}, u32[]{:S(2)}, u32[]{:S(2)}) collective-permute-start(f32[150,512]{1,0:T(8,128)S(1)} %bitcast_add_fusion.1), channel_id=1, source_target_pairs={{0,3},{1,2},{2,1},{3,0},{4,7},{5,6},{6,5},{7,4},{8,11},{9,10},{10,... | collective-permute-start | bytes 921608 | tf_op jit(solution)/shard_map/ppermute | solution.py:261
  21.6 5.6 %collective-permute-start.8 = (f32[80,120]{1,0:T(8,128)S(1)}, f32[80,120]{1,0:T(8,128)S(1)}, u32[]{:S(2)}, u32[]{:S(2)}) collective-permute-start(f32[80,120]{1,0:T(8,128)S(1)} %add.103), channel_id=1, source_target_pairs={{0,17},{1,16},{2,19},{3,18},{4,21},{5,20},{6,23},{7,22},{8,25},{9,... | collective-permute-start | bytes 115208 | tf_op jit(solution)/shard_map/ppermute | solution.py:271
  23.7 9.8 %collective-permute-start.12 = (f32[120,128]{1,0:T(8,128)S(1)}, f32[120,128]{1,0:T(8,128)S(1)}, u32[]{:S(2)}, u32[]{:S(2)}) collective-permute-start(f32[120,128]{1,0:T(8,128)S(1)} %get-tuple-element.36), channel_id=1, source_target_pairs={{0,16},{4,20},{8,24},{12,28},{16,0},{20,4},{24,8},{28,12},{1,17},{... | collective-permute-start | bytes 184328 | tf_op jit(solution)/shard_map/ppermute | solution.py:261
  27.2 1.8 %collective-permute-start.9 = (f32[80,120]{1,0:T(8,128)S(1)}, f32[80,120]{1,0:T(8,128)S(1)}, u32[]{:S(2)}, u32[]{:S(2)}) collective-permute-start(f32[80,120]{1,0:T(8,128)S(1)} %paced.3.mine), channel_id=1, source_target_pairs={{0,1},{1,0},{2,3},{3,2},{4,5},{5,4},{6,7},{7,6},{8,9},{9,8},{10,11... | collective-permute-start | bytes 115208 | tf_op jit(solution)/shard_map/ppermute | solution.py:261

commit v7 on v6

--- a/solution.py
+++ b/solution.py
@@ -68,8 +68,8 @@
     ]
     for copy in copies:
         copy.start()
-    for i, copy in enumerate(pieces[:AHEAD]):
-        copy.start(priority=i % 2)
+    for copy in pieces[:AHEAD]:
+        copy.start(priority=1)
     for copy in copies:
         copy.wait()
     omega = expand(factors[2][...], factors[3][...])
@@ -78,7 +78,7 @@
     for i, start in enumerate(starts):
         pieces[i].wait()
         if i + AHEAD < count:
-            pieces[i + AHEAD].start(priority=(i + AHEAD) % 2)
+            pieces[i + AHEAD].start(priority=1)
         block = held[start : start + rows]
         term = dot(psi[:, start : start + rows], block, 1, 0)
         value = term if value is None else value + term
@@ -93,7 +93,10 @@
             part[bit] = whole[:half]
             part[bit ^ 1, : rank - half] = whole[half:]
             part[bit ^ 1, rank - half :] = jnp.zeros((2 * half - rank, whole.shape[1]), F32)
-        spans[place[0] ^ i] = dot(omega, block, 1, 1)
+        if i % 2:
+            pair = dot(omega, held[start - rows : start + rows], 1, 1)
+            spans[place[0] ^ (i - 1)] = pair[:, :rows]
+            spans[place[0] ^ i] = pair[:, rows:]
 
 
 def half_of(rank):

time: 34.7 us -> 34.4 us (level)
  no operation moved by 1% of the time
where the time goes in v7:
time: 34.4 us; the launch traced here: 34.2 us
  starting transfers between devices  13.8 us (40%)
  Pallas kernels  10.2 us (30%)
  waiting for transfers between devices  8.38 us (24%)
  other arithmetic  0.99 us (3%)
  between operations  0.73 us (2%)
    ppermute x9, starting transfers between devices, swap(): return lax.ppermute(value, axis, [(i, i ^ bit) for i in range(size)])  8.03 us
    ppermute x4, starting transfers between devices, across(): return lax.ppermute(value, ('cells', 'samp'), pairs)  5.78 us
    pallas_call x1, Pallas kernels, sketches(): pl.pallas_call(sketch_kernel, in_specs=[pl.BlockSpec(memory_space=pltpu.S...  4.77 us
    ppermute x4, waiting for transfers between devices, across(): return lax.ppermute(value, ('cells', 'samp'), pairs)  4.63 us
    pallas_call x1, Pallas kernels, factor(): pl.pallas_call(factor_kernel, out_shape=(jax.ShapeDtypeStruct((rank, size...  4.4 us
    ppermute x9, waiting for transfers between devices, swap(): return lax.ppermute(value, axis, [(i, i ^ bit) for i in range(size)])  3.75 us
    pallas_call x1, Pallas kernels, finish(): pl.pallas_call(core_kernel, out_shape=jax.ShapeDtypeStruct((side.shape[0]...  1.01 us
    add x1, other arithmetic, on_device(): other, range_part = together((other, near + crossing))  0.8 us
  transfers between devices with their start and end apart: 13, of which 7 were waited for; matrix products, arithmetic and copies ran while one was open for 3% of the time, Pallas kernels for 13%

profile of v7, /device:TPU:0, one launch (start us, length us, event | category | flops | bytes accessed | tf_op | source)
XLA Modules:
  0.0 34.2 jit_solution(18217631084707654023)
XLA Ops:
  0.6 0.1 pad_add_fusion.place
  0.7 4.8 %sketches.1 = (f32[8,120,128]{2,1,0:T(8,128)S(1)}, f32[2,80,120]{2,1,0:T(8,128)S(1)}, f32[4,150,512]{2,1,0:T(8,128)S(1)}) custom-call(s32[2]{0:T(128)S(1)} %pad_add_fusion.place, bf16[32,120]{1,0:T(8,128)(2,1)} %bitcast.43, bf16[64,120]{1,0:T(8,128)(2,1)} %bitcast.40, bf16[32,150]{1,0:T(8,128)(2,1)} %bitcast.41, bf16[32,150]{1,0:T(8,128)(2,1)} %bitcast.42, ...), custom_call_target="tpu_custom_call" | custom-call | flops 1132462080 | bytes 4194304 | tf_op jit(solution)/shard_map/sketches/pallas_call | solution.py:112
  5.5 0.5 %collective-permute-start = (f32[80,120]{1,0:T(8,128)S(1)}, f32[80,120]{1,0:T(8,128)S(1)}, u32[]{:S(2)}, u32[]{:S(2)}) collective-permute-start(f32[80,120]{1,0:T(8,128)S(1)} %slice_bitcast_fusion.2), channel_id=1, source_target_pairs={{0,1},{1,0},{2,3},{3,2},{4,5},{5,4},{6,7},{7,6},{8,9},{9,8},{10,11... | collective-permute-start | bytes 115208 | tf_op jit(solution)/shard_map/ppermute | solution.py:264
  6.1 0.1 collective-permute-start.1
  6.2 3.0 %collective-permute-start.3 = (f32[2,120,128]{2,1,0:T(8,128)S(1)}, f32[2,120,128]{2,1,0:T(8,128)S(1)}, u32[]{:S(2)}, u32[]{:S(2)}) collective-permute-start(f32[2,120,128]{2,1,0:T(8,128)S(1)} %get-tuple-element.35), channel_id=1, source_target_pairs={{0,4},{4,0},{8,12},{12,8},{16,20},{20,16},{24,28},{28,24},{1,5},{5... | collective-permute-start | bytes 368648 | tf_op jit(solution)/shard_map/ppermute | solution.py:264
  9.2 0.0 collective-permute-done
  9.3 0.0 collective-permute-done.1
  9.3 1.1 %collective-permute-start.2 = (f32[80,120]{1,0:T(8,128)S(1)}, f32[80,120]{1,0:T(8,128)S(1)}, u32[]{:S(2)}, u32[]{:S(2)}) collective-permute-start(f32[80,120]{1,0:T(8,128)S(1)} %bitcast_add_fusion.4), channel_id=1, source_target_pairs={{0,3},{1,2},{2,1},{3,0},{4,7},{5,6},{6,5},{7,4},{8,11},{9,10},{10,... | collective-permute-start | bytes 115208 | tf_op jit(solution)/shard_map/ppermute | solution.py:274
  10.5 2.4 %collective-permute-done.3 = f32[2,120,128]{2,1,0:T(8,128)S(1)} collective-permute-done((f32[2,120,128]{2,1,0:T(8,128)S(1)}, f32[2,120,128]{2,1,0:T(8,128)S(1)}, u32[]{:S(2)}, u32[]{:S(2)}) %collective-permute-start.3) | collective-permute-done | bytes 122912 | tf_op jit(solution)/shard_map/ppermute | solution.py:264
  12.8 0.4 %collective-permute-done.2 = f32[80,120]{1,0:T(8,128)S(1)} collective-permute-done((f32[80,120]{1,0:T(8,128)S(1)}, f32[80,120]{1,0:T(8,128)S(1)}, u32[]{:S(2)}, u32[]{:S(2)}) %collective-permute-start.2) | collective-permute-done | bytes 38432 | tf_op jit(solution)/shard_map/ppermute | solution.py:274
  13.2 1.2 %collective-permute-start.4 = (f32[80,120]{1,0:T(8,128)S(1)}, f32[80,120]{1,0:T(8,128)S(1)}, u32[]{:S(2)}, u32[]{:S(2)}) collective-permute-start(f32[80,120]{1,0:T(8,128)S(1)} %add.95), channel_id=1, source_target_pairs={{0,9},{1,8},{2,11},{3,10},{4,13},{5,12},{6,15},{7,14},{8,1},{9,0},... | collective-permute-start | bytes 115208 | tf_op jit(solution)/shard_map/ppermute | solution.py:274
  14.4 1.4 %collective-permute-start.6 = (f32[2,120,128]{2,1,0:T(8,128)S(1)}, f32[2,120,128]{2,1,0:T(8,128)S(1)}, u32[]{:S(2)}, u32[]{:S(2)}) collective-permute-start(f32[2,120,128]{2,1,0:T(8,128)S(1)} %get-tuple-element.34), channel_id=1, source_target_pairs={{0,4},{4,0},{8,12},{12,8},{16,20},{20,16},{24,28},{28,24},{1,5},{5... | collective-permute-start | bytes 368648 | tf_op jit(solution)/shard_map/ppermute | solution.py:264
  15.8 0.5 %collective-permute-start.7 = (f32[2,120,128]{2,1,0:T(8,128)S(1)}, f32[2,120,128]{2,1,0:T(8,128)S(1)}, u32[]{:S(2)}, u32[]{:S(2)}) collective-permute-start(f32[2,120,128]{2,1,0:T(8,128)S(1)} %bitcast_add_fusion.3), channel_id=1, source_target_pairs={{0,8},{4,12},{8,0},{12,4},{16,24},{20,28},{24,16},{28,20},{1,9},{5... | collective-permute-start | bytes 368648 | tf_op jit(solution)/shard_map/ppermute | solution.py:264
  16.3 0.5 %collective-permute-done.4 = f32[80,120]{1,0:T(8,128)S(1)} collective-permute-done((f32[80,120]{1,0:T(8,128)S(1)}, f32[80,120]{1,0:T(8,128)S(1)}, u32[]{:S(2)}, u32[]{:S(2)}) %collective-permute-start.4) | collective-permute-done | bytes 38432 | tf_op jit(solution)/shard_map/ppermute | solution.py:274
  16.8 1.4 %collective-permute-start.5 = (f32[80,120]{1,0:T(8,128)S(1)}, f32[80,120]{1,0:T(8,128)S(1)}, u32[]{:S(2)}, u32[]{:S(2)}) collective-permute-start(f32[80,120]{1,0:T(8,128)S(1)} %paced.2), channel_id=1, source_target_pairs={{0,5},{1,4},{2,7},{3,6},{4,1},{5,0},{6,3},{7,2},{8,13},{9,12},{10,... | collective-permute-start | bytes 115208 | tf_op jit(solution)/shard_map/ppermute | solution.py:274
  18.2 0.4 %collective-permute-start.10 = (f32[150,512]{1,0:T(8,128)S(1)}, f32[150,512]{1,0:T(8,128)S(1)}, u32[]{:S(2)}, u32[]{:S(2)}) collective-permute-start(f32[150,512]{1,0:T(8,128)S(1)} %get-tuple-element.32), channel_id=1, source_target_pairs={{0,1},{1,0},{2,3},{3,2},{4,5},{5,4},{6,7},{7,6},{8,9},{9,8},{10,11... | collective-permute-start | bytes 921608 | tf_op jit(solution)/shard_map/ppermute | solution.py:264
  18.6 1.2 %collective-permute-start.11 = (f32[150,512]{1,0:T(8,128)S(1)}, f32[150,512]{1,0:T(8,128)S(1)}, u32[]{:S(2)}, u32[]{:S(2)}) collective-permute-start(f32[150,512]{1,0:T(8,128)S(1)} %bitcast_add_fusion.1), channel_id=1, source_target_pairs={{0,3},{1,2},{2,1},{3,0},{4,7},{5,6},{6,5},{7,4},{8,11},{9,10},{10,... | collective-permute-start | bytes 921608 | tf_op jit(solution)/shard_map/ppermute | solution.py:264
  19.8 1.0 %collective-permute-done.5 = f32[80,120]{1,0:T(8,128)S(1)} collective-permute-done((f32[80,120]{1,0:T(8,128)S(1)}, f32[80,120]{1,0:T(8,128)S(1)}, u32[]{:S(2)}, u32[]{:S(2)}) %collective-permute-start.5) | collective-permute-done | bytes 38432 | tf_op jit(solution)/shard_map/ppermute | solution.py:274
  20.8 0.0 collective-permute-done.6
  20.8 0.5 %collective-permute-done.7 = f32[2,120,128]{2,1,0:T(8,128)S(1)} collective-permute-done((f32[2,120,128]{2,1,0:T(8,128)S(1)}, f32[2,120,128]{2,1,0:T(8,128)S(1)}, u32[]{:S(2)}, u32[]{:S(2)}) %collective-permute-start.7) | collective-permute-done | bytes 122912 | tf_op jit(solution)/shard_map/ppermute | solution.py:264
  21.3 2.1 %collective-permute-start.8 = (f32[80,120]{1,0:T(8,128)S(1)}, f32[80,120]{1,0:T(8,128)S(1)}, u32[]{:S(2)}, u32[]{:S(2)}) collective-permute-start(f32[80,120]{1,0:T(8,128)S(1)} %add.103), channel_id=1, source_target_pairs={{0,17},{1,16},{2,19},{3,18},{4,21},{5,20},{6,23},{7,22},{8,25},{9,... | collective-permute-start | bytes 115208 | tf_op jit(solution)/shard_map/ppermute | solution.py:274
  23.4 0.7 %collective-permute-start.12 = (f32[120,128]{1,0:T(8,128)S(1)}, f32[120,128]{1,0:T(8,128)S(1)}, u32[]{:S(2)}, u32[]{:S(2)}) collective-permute-start(f32[120,128]{1,0:T(8,128)S(1)} %get-tuple-element.36), channel_id=1, source_target_pairs={{0,16},{4,20},{8,24},{12,28},{16,0},{20,4},{24,8},{28,12},{1,17},{... | collective-permute-start | bytes 184328 | tf_op jit(solution)/shard_map/ppermute | solution.py:264
  24.1 2.8 %collective-permute-done.8 = f32[80,120]{1,0:T(8,128)S(1)} collective-permute-done((f32[80,120]{1,0:T(8,128)S(1)}, f32[80,120]{1,0:T(8,128)S(1)}, u32[]{:S(2)}, u32[]{:S(2)}) %collective-permute-start.8) | collective-permute-done | bytes 38432 | tf_op jit(solution)/shard_map/ppermute | solution.py:274
  26.9 0.2 collective-permute-start.9
  27.1 0.0 collective-permute-done.10
  27.1 0.9 %collective-permute-done.11 = f32[150,512]{1,0:T(8,128)S(1)} collective-permute-done((f32[150,512]{1,0:T(8,128)S(1)}, f32[150,512]{1,0:T(8,128)S(1)}, u32[]{:S(2)}, u32[]{:S(2)}) %collective-permute-start.11) | collective-permute-done | bytes 307232 | tf_op jit(solution)/shard_map/ppermute | solution.py:264
  28.0 0.8 %fusion = f32[150,512]{1,0:T(8,128)} fusion(f32[150,512]{1,0:T(8,128)S(1)} %collective-permute-done.11, f32[150,512]{1,0:T(8,128)S(1)} %collective-permute-done.10, f32[4,150,512]{2,1,0:T(8,128)S(1)} %get-tuple-element.20), kind=kLoop, calls=%fused_computation.1 | loop fusion | flops 153600 | bytes 1228800 | tf_op jit(solution)/shard_map/add | solution.py:335
  28.8 0.0 collective-permute-done.9.other
  28.8 4.4 %factor.1 = (f32[150,120]{1,0:T(8,128)S(1)}, f32[120,120]{1,0:T(8,128)S(1)}) custom-call(s32[1]{0:T(128)} %bitcast.1.low_first, f32[80,120]{1,0:T(8,128)S(1)} %paced.3.mine, f32[80,120]{1,0:T(8,128)S(1)} %collective-permute-done.9.other), custom_call_target="tpu_custom_call" | custom-call | flops 10000 | bytes 1000 | tf_op jit(solution)/shard_map/factor/pallas_call | solution.py:209
  33.2 0.0 collective-permute-done.12.received
  33.2 1.0 %core.1 = f32[150,128]{1,0:T(8,128)} custom-call(f32[150,120]{1,0:T(8,128)S(1)} %get-tuple-element.29.side, f32[120,120]{1,0:T(8,128)S(1)} %get-tuple-element.30.weight, f32[120,128]{1,0:T(8,128)S(1)} %get-tuple-element.37.kept, f32[120,128]{1,0:T(8,128)S(1)} %collective-permute-done.12.received), custom_call_target="tpu_custom_call" | custom-call | tf_op jit(solution)/shard_map/core/pallas_call | solution.py:253
  (14 shorter events, 0.2 us)
Async XLA Ops:
  5.5 3.7 %collective-permute-start = (f32[80,120]{1,0:T(8,128)S(1)}, f32[80,120]{1,0:T(8,128)S(1)}, u32[]{:S(2)}, u32[]{:S(2)}) collective-permute-start(f32[80,120]{1,0:T(8,128)S(1)} %slice_bitcast_fusion.2), channel_id=1, source_target_pairs={{0,1},{1,0},{2,3},{3,2},{4,5},{5,4},{6,7},{7,6},{8,9},{9,8},{10,11... | collective-permute-start | bytes 115208 | tf_op jit(solution)/shard_map/ppermute | solution.py:264
  6.1 3.2 %collective-permute-start.1 = (f32[150,512]{1,0:T(8,128)S(1)}, f32[150,512]{1,0:T(8,128)S(1)}, u32[]{:S(2)}, u32[]{:S(2)}) collective-permute-start(f32[150,512]{1,0:T(8,128)S(1)} %get-tuple-element.33), channel_id=1, source_target_pairs={{0,1},{1,0},{2,3},{3,2},{4,5},{5,4},{6,7},{7,6},{8,9},{9,8},{10,11... | collective-permute-start | bytes 921608 | tf_op jit(solution)/shard_map/ppermute | solution.py:264
  6.2 6.6 %collective-permute-start.3 = (f32[2,120,128]{2,1,0:T(8,128)S(1)}, f32[2,120,128]{2,1,0:T(8,128)S(1)}, u32[]{:S(2)}, u32[]{:S(2)}) collective-permute-start(f32[2,120,128]{2,1,0:T(8,128)S(1)} %get-tuple-element.35), channel_id=1, source_target_pairs={{0,4},{4,0},{8,12},{12,8},{16,20},{20,16},{24,28},{28,24},{1,5},{5... | collective-permute-start | bytes 368648 | tf_op jit(solution)/shard_map/ppermute | solution.py:264
  9.3 3.9 %collective-permute-start.2 = (f32[80,120]{1,0:T(8,128)S(1)}, f32[80,120]{1,0:T(8,128)S(1)}, u32[]{:S(2)}, u32[]{:S(2)}) collective-permute-start(f32[80,120]{1,0:T(8,128)S(1)} %bitcast_add_fusion.4), channel_id=1, source_target_pairs={{0,3},{1,2},{2,1},{3,0},{4,7},{5,6},{6,5},{7,4},{8,11},{9,10},{10,... | collective-permute-start | bytes 115208 | tf_op jit(solution)/shard_map/ppermute | solution.py:274
  13.2 3.6 %collective-permute-start.4 = (f32[80,120]{1,0:T(8,128)S(1)}, f32[80,120]{1,0:T(8,128)S(1)}, u32[]{:S(2)}, u32[]{:S(2)}) collective-permute-start(f32[80,120]{1,0:T(8,128)S(1)} %add.95), channel_id=1, source_target_pairs={{0,9},{1,8},{2,11},{3,10},{4,13},{5,12},{6,15},{7,14},{8,1},{9,0},... | collective-permute-start | bytes 115208 | tf_op jit(solution)/shard_map/ppermute | solution.py:274
  14.4 6.4 %collective-permute-start.6 = (f32[2,120,128]{2,1,0:T(8,128)S(1)}, f32[2,120,128]{2,1,0:T(8,128)S(1)}, u32[]{:S(2)}, u32[]{:S(2)}) collective-permute-start(f32[2,120,128]{2,1,0:T(8,128)S(1)} %get-tuple-element.34), channel_id=1, source_target_pairs={{0,4},{4,0},{8,12},{12,8},{16,20},{20,16},{24,28},{28,24},{1,5},{5... | collective-permute-start | bytes 368648 | tf_op jit(solution)/shard_map/ppermute | solution.py:264
  15.8 5.5 %collective-permute-start.7 = (f32[2,120,128]{2,1,0:T(8,128)S(1)}, f32[2,120,128]{2,1,0:T(8,128)S(1)}, u32[]{:S(2)}, u32[]{:S(2)}) collective-permute-start(f32[2,120,128]{2,1,0:T(8,128)S(1)} %bitcast_add_fusion.3), channel_id=1, source_target_pairs={{0,8},{4,12},{8,0},{12,4},{16,24},{20,28},{24,16},{28,20},{1,9},{5... | collective-permute-start | bytes 368648 | tf_op jit(solution)/shard_map/ppermute | solution.py:264
  16.8 4.0 %collective-permute-start.5 = (f32[80,120]{1,0:T(8,128)S(1)}, f32[80,120]{1,0:T(8,128)S(1)}, u32[]{:S(2)}, u32[]{:S(2)}) collective-permute-start(f32[80,120]{1,0:T(8,128)S(1)} %paced.2), channel_id=1, source_target_pairs={{0,5},{1,4},{2,7},{3,6},{4,1},{5,0},{6,3},{7,2},{8,13},{9,12},{10,... | collective-permute-start | bytes 115208 | tf_op jit(solution)/shard_map/ppermute | solution.py:274
  18.2 8.9 %collective-permute-start.10 = (f32[150,512]{1,0:T(8,128)S(1)}, f32[150,512]{1,0:T(8,128)S(1)}, u32[]{:S(2)}, u32[]{:S(2)}) collective-permute-start(f32[150,512]{1,0:T(8,128)S(1)} %get-tuple-element.32), channel_id=1, source_target_pairs={{0,1},{1,0},{2,3},{3,2},{4,5},{5,4},{6,7},{7,6},{8,9},{9,8},{10,11... | collective-permute-start | bytes 921608 | tf_op jit(solution)/shard_map/ppermute | solution.py:264
  18.6 9.4 %collective-permute-start.11 = (f32[150,512]{1,0:T(8,128)S(1)}, f32[150,512]{1,0:T(8,128)S(1)}, u32[]{:S(2)}, u32[]{:S(2)}) collective-permute-start(f32[150,512]{1,0:T(8,128)S(1)} %bitcast_add_fusion.1), channel_id=1, source_target_pairs={{0,3},{1,2},{2,1},{3,0},{4,7},{5,6},{6,5},{7,4},{8,11},{9,10},{10,... | collective-permute-start | bytes 921608 | tf_op jit(solution)/shard_map/ppermute | solution.py:264
  21.3 5.6 %collective-permute-start.8 = (f32[80,120]{1,0:T(8,128)S(1)}, f32[80,120]{1,0:T(8,128)S(1)}, u32[]{:S(2)}, u32[]{:S(2)}) collective-permute-start(f32[80,120]{1,0:T(8,128)S(1)} %add.103), channel_id=1, source_target_pairs={{0,17},{1,16},{2,19},{3,18},{4,21},{5,20},{6,23},{7,22},{8,25},{9,... | collective-permute-start | bytes 115208 | tf_op jit(solution)/shard_map/ppermute | solution.py:274
  23.4 9.8 %collective-permute-start.12 = (f32[120,128]{1,0:T(8,128)S(1)}, f32[120,128]{1,0:T(8,128)S(1)}, u32[]{:S(2)}, u32[]{:S(2)}) collective-permute-start(f32[120,128]{1,0:T(8,128)S(1)} %get-tuple-element.36), channel_id=1, source_target_pairs={{0,16},{4,20},{8,24},{12,28},{16,0},{20,4},{24,8},{28,12},{1,17},{... | collective-permute-start | bytes 184328 | tf_op jit(solution)/shard_map/ppermute | solution.py:264
  26.9 1.9 %collective-permute-start.9 = (f32[80,120]{1,0:T(8,128)S(1)}, f32[80,120]{1,0:T(8,128)S(1)}, u32[]{:S(2)}, u32[]{:S(2)}) collective-permute-start(f32[80,120]{1,0:T(8,128)S(1)} %paced.3.mine), channel_id=1, source_target_pairs={{0,1},{1,0},{2,3},{3,2},{4,5},{5,4},{6,7},{7,6},{8,9},{9,8},{10,11... | collective-permute-start | bytes 115208 | tf_op jit(solution)/shard_map/ppermute | solution.py:264

commit v8 on v7

--- a/solution.py
+++ b/solution.py
@@ -72,10 +72,11 @@
         copy.start(priority=1)
     for copy in copies:
         copy.wait()
-    omega = expand(factors[2][...], factors[3][...])
     psi = expand(factors[0][...], factors[1][...])
     value = None
     for i, start in enumerate(starts):
+        if i == 1:
+            omega = expand(factors[2][...], factors[3][...])
         pieces[i].wait()
         if i + AHEAD < count:
             pieces[i + AHEAD].start(priority=1)

time: 34.4 us -> 34.4 us (level)
  no operation moved by 1% of the time
where the time goes in v8:
time: 34.4 us; the launch traced here: 34.2 us
  starting transfers between devices  13.8 us (40%)
  Pallas kernels  10.2 us (30%)
  waiting for transfers between devices  8.42 us (24%)
  other arithmetic  0.99 us (3%)
  between operations  0.73 us (2%)
    ppermute x9, starting transfers between devices, swap(): return lax.ppermute(value, axis, [(i, i ^ bit) for i in range(size)])  8.01 us
    ppermute x4, starting transfers between devices, across(): return lax.ppermute(value, ('cells', 'samp'), pairs)  5.76 us
    pallas_call x1, Pallas kernels, sketches(): pl.pallas_call(sketch_kernel, in_specs=[pl.BlockSpec(memory_space=pltpu.S...  4.79 us
    ppermute x4, waiting for transfers between devices, across(): return lax.ppermute(value, ('cells', 'samp'), pairs)  4.67 us
    pallas_call x1, Pallas kernels, factor(): pl.pallas_call(factor_kernel, out_shape=(jax.ShapeDtypeStruct((rank, size...  4.39 us
    ppermute x9, waiting for transfers between devices, swap(): return lax.ppermute(value, axis, [(i, i ^ bit) for i in range(size)])  3.75 us
    pallas_call x1, Pallas kernels, finish(): pl.pallas_call(core_kernel, out_shape=jax.ShapeDtypeStruct((side.shape[0]...  1.01 us
    add x1, other arithmetic, on_device(): other, range_part = together((other, near + crossing))  0.8 us
  transfers between devices with their start and end apart: 13, of which 7 were waited for; matrix products, arithmetic and copies ran while one was open for 3% of the time, Pallas kernels for 13%

profile of v8, /device:TPU:0, one launch (start us, length us, event | category | flops | bytes accessed | tf_op | source)
XLA Modules:
  0.0 34.2 jit_solution(16047687229547579471)
XLA Ops:
  0.6 0.1 pad_add_fusion.place
  0.7 4.8 %sketches.1 = (f32[8,120,128]{2,1,0:T(8,128)S(1)}, f32[2,80,120]{2,1,0:T(8,128)S(1)}, f32[4,150,512]{2,1,0:T(8,128)S(1)}) custom-call(s32[2]{0:T(128)S(1)} %pad_add_fusion.place, bf16[32,120]{1,0:T(8,128)(2,1)} %bitcast.43, bf16[64,120]{1,0:T(8,128)(2,1)} %bitcast.40, bf16[32,150]{1,0:T(8,128)(2,1)} %bitcast.41, bf16[32,150]{1,0:T(8,128)(2,1)} %bitcast.42, ...), custom_call_target="tpu_custom_call" | custom-call | flops 1132462080 | bytes 4194304 | tf_op jit(solution)/shard_map/sketches/pallas_call | solution.py:113
  5.5 0.5 %collective-permute-start = (f32[80,120]{1,0:T(8,128)S(1)}, f32[80,120]{1,0:T(8,128)S(1)}, u32[]{:S(2)}, u32[]{:S(2)}) collective-permute-start(f32[80,120]{1,0:T(8,128)S(1)} %slice_bitcast_fusion.2), channel_id=1, source_target_pairs={{0,1},{1,0},{2,3},{3,2},{4,5},{5,4},{6,7},{7,6},{8,9},{9,8},{10,11... | collective-permute-start | bytes 115208 | tf_op jit(solution)/shard_map/ppermute | solution.py:265
  6.1 0.1 collective-permute-start.1
  6.3 3.0 %collective-permute-start.3 = (f32[2,120,128]{2,1,0:T(8,128)S(1)}, f32[2,120,128]{2,1,0:T(8,128)S(1)}, u32[]{:S(2)}, u32[]{:S(2)}) collective-permute-start(f32[2,120,128]{2,1,0:T(8,128)S(1)} %get-tuple-element.35), channel_id=1, source_target_pairs={{0,4},{4,0},{8,12},{12,8},{16,20},{20,16},{24,28},{28,24},{1,5},{5... | collective-permute-start | bytes 368648 | tf_op jit(solution)/shard_map/ppermute | solution.py:265
  9.3 0.0 collective-permute-done
  9.3 0.0 collective-permute-done.1
  9.3 1.1 %collective-permute-start.2 = (f32[80,120]{1,0:T(8,128)S(1)}, f32[80,120]{1,0:T(8,128)S(1)}, u32[]{:S(2)}, u32[]{:S(2)}) collective-permute-start(f32[80,120]{1,0:T(8,128)S(1)} %bitcast_add_fusion.4), channel_id=1, source_target_pairs={{0,3},{1,2},{2,1},{3,0},{4,7},{5,6},{6,5},{7,4},{8,11},{9,10},{10,... | collective-permute-start | bytes 115208 | tf_op jit(solution)/shard_map/ppermute | solution.py:275
  10.5 2.4 %collective-permute-done.3 = f32[2,120,128]{2,1,0:T(8,128)S(1)} collective-permute-done((f32[2,120,128]{2,1,0:T(8,128)S(1)}, f32[2,120,128]{2,1,0:T(8,128)S(1)}, u32[]{:S(2)}, u32[]{:S(2)}) %collective-permute-start.3) | collective-permute-done | bytes 122912 | tf_op jit(solution)/shard_map/ppermute | solution.py:265
  12.9 0.4 %collective-permute-done.2 = f32[80,120]{1,0:T(8,128)S(1)} collective-permute-done((f32[80,120]{1,0:T(8,128)S(1)}, f32[80,120]{1,0:T(8,128)S(1)}, u32[]{:S(2)}, u32[]{:S(2)}) %collective-permute-start.2) | collective-permute-done | bytes 38432 | tf_op jit(solution)/shard_map/ppermute | solution.py:275
  13.2 1.2 %collective-permute-start.4 = (f32[80,120]{1,0:T(8,128)S(1)}, f32[80,120]{1,0:T(8,128)S(1)}, u32[]{:S(2)}, u32[]{:S(2)}) collective-permute-start(f32[80,120]{1,0:T(8,128)S(1)} %add.95), channel_id=1, source_target_pairs={{0,9},{1,8},{2,11},{3,10},{4,13},{5,12},{6,15},{7,14},{8,1},{9,0},... | collective-permute-start | bytes 115208 | tf_op jit(solution)/shard_map/ppermute | solution.py:275
  14.4 1.4 %collective-permute-start.6 = (f32[2,120,128]{2,1,0:T(8,128)S(1)}, f32[2,120,128]{2,1,0:T(8,128)S(1)}, u32[]{:S(2)}, u32[]{:S(2)}) collective-permute-start(f32[2,120,128]{2,1,0:T(8,128)S(1)} %get-tuple-element.34), channel_id=1, source_target_pairs={{0,4},{4,0},{8,12},{12,8},{16,20},{20,16},{24,28},{28,24},{1,5},{5... | collective-permute-start | bytes 368648 | tf_op jit(solution)/shard_map/ppermute | solution.py:265
  15.8 0.5 %collective-permute-start.7 = (f32[2,120,128]{2,1,0:T(8,128)S(1)}, f32[2,120,128]{2,1,0:T(8,128)S(1)}, u32[]{:S(2)}, u32[]{:S(2)}) collective-permute-start(f32[2,120,128]{2,1,0:T(8,128)S(1)} %bitcast_add_fusion.3), channel_id=1, source_target_pairs={{0,8},{4,12},{8,0},{12,4},{16,24},{20,28},{24,16},{28,20},{1,9},{5... | collective-permute-start | bytes 368648 | tf_op jit(solution)/shard_map/ppermute | solution.py:265
  16.3 0.5 %collective-permute-done.4 = f32[80,120]{1,0:T(8,128)S(1)} collective-permute-done((f32[80,120]{1,0:T(8,128)S(1)}, f32[80,120]{1,0:T(8,128)S(1)}, u32[]{:S(2)}, u32[]{:S(2)}) %collective-permute-start.4) | collective-permute-done | bytes 38432 | tf_op jit(solution)/shard_map/ppermute | solution.py:275
  16.8 1.4 %collective-permute-start.5 = (f32[80,120]{1,0:T(8,128)S(1)}, f32[80,120]{1,0:T(8,128)S(1)}, u32[]{:S(2)}, u32[]{:S(2)}) collective-permute-start(f32[80,120]{1,0:T(8,128)S(1)} %paced.2), channel_id=1, source_target_pairs={{0,5},{1,4},{2,7},{3,6},{4,1},{5,0},{6,3},{7,2},{8,13},{9,12},{10,... | collective-permute-start | bytes 115208 | tf_op jit(solution)/shard_map/ppermute | solution.py:275
  18.2 0.4 %collective-permute-start.10 = (f32[150,512]{1,0:T(8,128)S(1)}, f32[150,512]{1,0:T(8,128)S(1)}, u32[]{:S(2)}, u32[]{:S(2)}) collective-permute-start(f32[150,512]{1,0:T(8,128)S(1)} %get-tuple-element.32), channel_id=1, source_target_pairs={{0,1},{1,0},{2,3},{3,2},{4,5},{5,4},{6,7},{7,6},{8,9},{9,8},{10,11... | collective-permute-start | bytes 921608 | tf_op jit(solution)/shard_map/ppermute | solution.py:265
  18.6 1.2 %collective-permute-start.11 = (f32[150,512]{1,0:T(8,128)S(1)}, f32[150,512]{1,0:T(8,128)S(1)}, u32[]{:S(2)}, u32[]{:S(2)}) collective-permute-start(f32[150,512]{1,0:T(8,128)S(1)} %bitcast_add_fusion.1), channel_id=1, source_target_pairs={{0,3},{1,2},{2,1},{3,0},{4,7},{5,6},{6,5},{7,4},{8,11},{9,10},{10,... | collective-permute-start | bytes 921608 | tf_op jit(solution)/shard_map/ppermute | solution.py:265
  19.8 1.0 %collective-permute-done.5 = f32[80,120]{1,0:T(8,128)S(1)} collective-permute-done((f32[80,120]{1,0:T(8,128)S(1)}, f32[80,120]{1,0:T(8,128)S(1)}, u32[]{:S(2)}, u32[]{:S(2)}) %collective-permute-start.5) | collective-permute-done | bytes 38432 | tf_op jit(solution)/shard_map/ppermute | solution.py:275
  20.8 0.0 collective-permute-done.6
  20.8 0.5 %collective-permute-done.7 = f32[2,120,128]{2,1,0:T(8,128)S(1)} collective-permute-done((f32[2,120,128]{2,1,0:T(8,128)S(1)}, f32[2,120,128]{2,1,0:T(8,128)S(1)}, u32[]{:S(2)}, u32[]{:S(2)}) %collective-permute-start.7) | collective-permute-done | bytes 122912 | tf_op jit(solution)/shard_map/ppermute | solution.py:265
  21.3 2.1 %collective-permute-start.8 = (f32[80,120]{1,0:T(8,128)S(1)}, f32[80,120]{1,0:T(8,128)S(1)}, u32[]{:S(2)}, u32[]{:S(2)}) collective-permute-start(f32[80,120]{1,0:T(8,128)S(1)} %add.103), channel_id=1, source_target_pairs={{0,17},{1,16},{2,19},{3,18},{4,21},{5,20},{6,23},{7,22},{8,25},{9,... | collective-permute-start | bytes 115208 | tf_op jit(solution)/shard_map/ppermute | solution.py:275
  23.4 0.7 %collective-permute-start.12 = (f32[120,128]{1,0:T(8,128)S(1)}, f32[120,128]{1,0:T(8,128)S(1)}, u32[]{:S(2)}, u32[]{:S(2)}) collective-permute-start(f32[120,128]{1,0:T(8,128)S(1)} %get-tuple-element.36), channel_id=1, source_target_pairs={{0,16},{4,20},{8,24},{12,28},{16,0},{20,4},{24,8},{28,12},{1,17},{... | collective-permute-start | bytes 184328 | tf_op jit(solution)/shard_map/ppermute | solution.py:265
  24.1 2.8 %collective-permute-done.8 = f32[80,120]{1,0:T(8,128)S(1)} collective-permute-done((f32[80,120]{1,0:T(8,128)S(1)}, f32[80,120]{1,0:T(8,128)S(1)}, u32[]{:S(2)}, u32[]{:S(2)}) %collective-permute-start.8) | collective-permute-done | bytes 38432 | tf_op jit(solution)/shard_map/ppermute | solution.py:275
  26.9 0.2 collective-permute-start.9
  27.1 0.0 collective-permute-done.10
  27.1 0.9 %collective-permute-done.11 = f32[150,512]{1,0:T(8,128)S(1)} collective-permute-done((f32[150,512]{1,0:T(8,128)S(1)}, f32[150,512]{1,0:T(8,128)S(1)}, u32[]{:S(2)}, u32[]{:S(2)}) %collective-permute-start.11) | collective-permute-done | bytes 307232 | tf_op jit(solution)/shard_map/ppermute | solution.py:265
  28.0 0.8 %fusion = f32[150,512]{1,0:T(8,128)} fusion(f32[150,512]{1,0:T(8,128)S(1)} %collective-permute-done.11, f32[150,512]{1,0:T(8,128)S(1)} %collective-permute-done.10, f32[4,150,512]{2,1,0:T(8,128)S(1)} %get-tuple-element.20), kind=kLoop, calls=%fused_computation.1 | loop fusion | flops 153600 | bytes 1228800 | tf_op jit(solution)/shard_map/add | solution.py:336
  28.8 0.0 collective-permute-done.9.other
  28.8 4.4 %factor.1 = (f32[150,120]{1,0:T(8,128)S(1)}, f32[120,120]{1,0:T(8,128)S(1)}) custom-call(s32[1]{0:T(128)} %bitcast.1.low_first, f32[80,120]{1,0:T(8,128)S(1)} %paced.3.mine, f32[80,120]{1,0:T(8,128)S(1)} %collective-permute-done.9.other), custom_call_target="tpu_custom_call" | custom-call | flops 10000 | bytes 1000 | tf_op jit(solution)/shard_map/factor/pallas_call | solution.py:210
  33.2 0.0 collective-permute-done.12.received
  33.2 1.0 %core.1 = f32[150,128]{1,0:T(8,128)} custom-call(f32[150,120]{1,0:T(8,128)S(1)} %get-tuple-element.29.side, f32[120,120]{1,0:T(8,128)S(1)} %get-tuple-element.30.weight, f32[120,128]{1,0:T(8,128)S(1)} %get-tuple-element.37.kept, f32[120,128]{1,0:T(8,128)S(1)} %collective-permute-done.12.received), custom_call_target="tpu_custom_call" | custom-call | tf_op jit(solution)/shard_map/core/pallas_call | solution.py:254
  (14 shorter events, 0.2 us)
Async XLA Ops:
  5.5 3.7 %collective-permute-start = (f32[80,120]{1,0:T(8,128)S(1)}, f32[80,120]{1,0:T(8,128)S(1)}, u32[]{:S(2)}, u32[]{:S(2)}) collective-permute-start(f32[80,120]{1,0:T(8,128)S(1)} %slice_bitcast_fusion.2), channel_id=1, source_target_pairs={{0,1},{1,0},{2,3},{3,2},{4,5},{5,4},{6,7},{7,6},{8,9},{9,8},{10,11... | collective-permute-start | bytes 115208 | tf_op jit(solution)/shard_map/ppermute | solution.py:265
  6.1 3.2 %collective-permute-start.1 = (f32[150,512]{1,0:T(8,128)S(1)}, f32[150,512]{1,0:T(8,128)S(1)}, u32[]{:S(2)}, u32[]{:S(2)}) collective-permute-start(f32[150,512]{1,0:T(8,128)S(1)} %get-tuple-element.33), channel_id=1, source_target_pairs={{0,1},{1,0},{2,3},{3,2},{4,5},{5,4},{6,7},{7,6},{8,9},{9,8},{10,11... | collective-permute-start | bytes 921608 | tf_op jit(solution)/shard_map/ppermute | solution.py:265
  6.3 6.6 %collective-permute-start.3 = (f32[2,120,128]{2,1,0:T(8,128)S(1)}, f32[2,120,128]{2,1,0:T(8,128)S(1)}, u32[]{:S(2)}, u32[]{:S(2)}) collective-permute-start(f32[2,120,128]{2,1,0:T(8,128)S(1)} %get-tuple-element.35), channel_id=1, source_target_pairs={{0,4},{4,0},{8,12},{12,8},{16,20},{20,16},{24,28},{28,24},{1,5},{5... | collective-permute-start | bytes 368648 | tf_op jit(solution)/shard_map/ppermute | solution.py:265
  9.3 3.9 %collective-permute-start.2 = (f32[80,120]{1,0:T(8,128)S(1)}, f32[80,120]{1,0:T(8,128)S(1)}, u32[]{:S(2)}, u32[]{:S(2)}) collective-permute-start(f32[80,120]{1,0:T(8,128)S(1)} %bitcast_add_fusion.4), channel_id=1, source_target_pairs={{0,3},{1,2},{2,1},{3,0},{4,7},{5,6},{6,5},{7,4},{8,11},{9,10},{10,... | collective-permute-start | bytes 115208 | tf_op jit(solution)/shard_map/ppermute | solution.py:275
  13.2 3.6 %collective-permute-start.4 = (f32[80,120]{1,0:T(8,128)S(1)}, f32[80,120]{1,0:T(8,128)S(1)}, u32[]{:S(2)}, u32[]{:S(2)}) collective-permute-start(f32[80,120]{1,0:T(8,128)S(1)} %add.95), channel_id=1, source_target_pairs={{0,9},{1,8},{2,11},{3,10},{4,13},{5,12},{6,15},{7,14},{8,1},{9,0},... | collective-permute-start | bytes 115208 | tf_op jit(solution)/shard_map/ppermute | solution.py:275
  14.4 6.4 %collective-permute-start.6 = (f32[2,120,128]{2,1,0:T(8,128)S(1)}, f32[2,120,128]{2,1,0:T(8,128)S(1)}, u32[]{:S(2)}, u32[]{:S(2)}) collective-permute-start(f32[2,120,128]{2,1,0:T(8,128)S(1)} %get-tuple-element.34), channel_id=1, source_target_pairs={{0,4},{4,0},{8,12},{12,8},{16,20},{20,16},{24,28},{28,24},{1,5},{5... | collective-permute-start | bytes 368648 | tf_op jit(solution)/shard_map/ppermute | solution.py:265
  15.8 5.5 %collective-permute-start.7 = (f32[2,120,128]{2,1,0:T(8,128)S(1)}, f32[2,120,128]{2,1,0:T(8,128)S(1)}, u32[]{:S(2)}, u32[]{:S(2)}) collective-permute-start(f32[2,120,128]{2,1,0:T(8,128)S(1)} %bitcast_add_fusion.3), channel_id=1, source_target_pairs={{0,8},{4,12},{8,0},{12,4},{16,24},{20,28},{24,16},{28,20},{1,9},{5... | collective-permute-start | bytes 368648 | tf_op jit(solution)/shard_map/ppermute | solution.py:265
  16.8 4.0 %collective-permute-start.5 = (f32[80,120]{1,0:T(8,128)S(1)}, f32[80,120]{1,0:T(8,128)S(1)}, u32[]{:S(2)}, u32[]{:S(2)}) collective-permute-start(f32[80,120]{1,0:T(8,128)S(1)} %paced.2), channel_id=1, source_target_pairs={{0,5},{1,4},{2,7},{3,6},{4,1},{5,0},{6,3},{7,2},{8,13},{9,12},{10,... | collective-permute-start | bytes 115208 | tf_op jit(solution)/shard_map/ppermute | solution.py:275
  18.2 8.9 %collective-permute-start.10 = (f32[150,512]{1,0:T(8,128)S(1)}, f32[150,512]{1,0:T(8,128)S(1)}, u32[]{:S(2)}, u32[]{:S(2)}) collective-permute-start(f32[150,512]{1,0:T(8,128)S(1)} %get-tuple-element.32), channel_id=1, source_target_pairs={{0,1},{1,0},{2,3},{3,2},{4,5},{5,4},{6,7},{7,6},{8,9},{9,8},{10,11... | collective-permute-start | bytes 921608 | tf_op jit(solution)/shard_map/ppermute | solution.py:265
  18.6 9.4 %collective-permute-start.11 = (f32[150,512]{1,0:T(8,128)S(1)}, f32[150,512]{1,0:T(8,128)S(1)}, u32[]{:S(2)}, u32[]{:S(2)}) collective-permute-start(f32[150,512]{1,0:T(8,128)S(1)} %bitcast_add_fusion.1), channel_id=1, source_target_pairs={{0,3},{1,2},{2,1},{3,0},{4,7},{5,6},{6,5},{7,4},{8,11},{9,10},{10,... | collective-permute-start | bytes 921608 | tf_op jit(solution)/shard_map/ppermute | solution.py:265
  21.3 5.6 %collective-permute-start.8 = (f32[80,120]{1,0:T(8,128)S(1)}, f32[80,120]{1,0:T(8,128)S(1)}, u32[]{:S(2)}, u32[]{:S(2)}) collective-permute-start(f32[80,120]{1,0:T(8,128)S(1)} %add.103), channel_id=1, source_target_pairs={{0,17},{1,16},{2,19},{3,18},{4,21},{5,20},{6,23},{7,22},{8,25},{9,... | collective-permute-start | bytes 115208 | tf_op jit(solution)/shard_map/ppermute | solution.py:275
  23.4 9.8 %collective-permute-start.12 = (f32[120,128]{1,0:T(8,128)S(1)}, f32[120,128]{1,0:T(8,128)S(1)}, u32[]{:S(2)}, u32[]{:S(2)}) collective-permute-start(f32[120,128]{1,0:T(8,128)S(1)} %get-tuple-element.36), channel_id=1, source_target_pairs={{0,16},{4,20},{8,24},{12,28},{16,0},{20,4},{24,8},{28,12},{1,17},{... | collective-permute-start | bytes 184328 | tf_op jit(solution)/shard_map/ppermute | solution.py:265
  26.9 1.9 %collective-permute-start.9 = (f32[80,120]{1,0:T(8,128)S(1)}, f32[80,120]{1,0:T(8,128)S(1)}, u32[]{:S(2)}, u32[]{:S(2)}) collective-permute-start(f32[80,120]{1,0:T(8,128)S(1)} %paced.3.mine), channel_id=1, source_target_pairs={{0,1},{1,0},{2,3},{3,2},{4,5},{5,4},{6,7},{7,6},{8,9},{9,8},{10,11... | collective-permute-start | bytes 115208 | tf_op jit(solution)/shard_map/ppermute | solution.py:265
